TPU v7x, 128 devices: a whole 4x4x4 slice. The times are simulated.
128 devices in a mesh: section: 4 (over z), dp: 8 (over x, y_lo), tensor: 4 (over y_hi, core).
Axes of the slice: x: 4, y: 4 (y_hi: 2, y_lo: 2; y = y_hi * 2 + y_lo), z: 4, core: 2. Of those that a mesh axis runs over, the one named last changes fastest.
Arguments:
- base: bfloat16 [4, 256, 8192], P(None, None, 'dp'), may hold values from -6 to 6
- w_in: bfloat16 [4, 8192, 14336], P('section', 'dp', 'tensor'), may hold values from -0.0625 to 0.0625
- w_out: bfloat16 [4, 14336, 8192], P('section', 'tensor', 'dp'), may hold values from -0.046875 to 0.046875
- basis: float32 [8192, 128], P('dp'), may hold values from -0.0625 to 0.0625
- cotangent: float32 [4, 256, 128], P(None, 'dp'), may hold values from -6 to 6
Outputs:
- coefs: float32 [4, 4, 256, 128], P('section', None, 'dp')
- grads: float32 [4, 4, 256, 128], P('section', None, 'dp')
- grad_up: bfloat16 [4, 8192, 14336], P('section', 'dp', 'tensor')
- down_coefs: float32 [4, 14336, 128], P('section', 'tensor')
All inputs are finite; a program needn't handle non-finite values.
Results may differ from a plain program's by a relative error of at most 0.007.
Values may be sent and summed in bfloat16 or wider, within the bound.
No kernel may reach another device: no remote copies, remote signals or barrier semaphores. Data moves between devices by JAX's collectives and lax.ppermute only.
A program may use at most 128 MiB of HBM per device.

v0:
```python
import jax
import jax.numpy as jnp
from jax import lax
from jax.sharding import PartitionSpec as P


def shifted(x, axis, by):
    devices = lax.axis_size(axis)
    pairs = [(i, i + by) for i in range(devices) if 0 <= i + by < devices]
    return lax.ppermute(x, axis, pairs)


def silu_slope(pre_act):
    sigmoid_val = jax.nn.sigmoid(pre_act)
    return sigmoid_val * (1.0 + pre_act * (1.0 - sigmoid_val))


def pass_on(payload, shift_by):
    return shifted(payload, "section", shift_by)


def put_block(store, payload, slot_idx, is_live):
    old_block = lax.dynamic_index_in_dim(store, slot_idx, 0, keepdims=False)
    renewed = jnp.where(is_live, payload, old_block)
    return lax.dynamic_update_index_in_dim(store, renewed, slot_idx, 0)


def on_device(base, w_in, w_out, basis, cotangent):
    highest = lax.Precision.HIGHEST
    contract_first = (((0,), (0,)), ((), ()))
    contract_last = (((1,), (1,)), ((), ()))
    section_idx = lax.axis_index("section")
    section_count = lax.axis_size("section")
    dp_count = lax.axis_size("dp")
    micro_count, all_rows, width_share = base.shape
    tok_rows = all_rows // dp_count
    rank_width = basis.shape[1]
    w_in_loc = w_in[0]
    w_out_loc = w_out[0]
    hid_local = w_in_loc.shape[1]
    gram_matrix, proj_up, down_sum = lax.psum(
        (
            lax.dot_general(basis, basis, contract_first, precision=highest),
            lax.dot_general(w_in_loc.astype(jnp.float32), basis, contract_first, precision=highest),
            jnp.dot(w_out_loc.astype(jnp.float32), basis, precision=highest),
        ),
        "dp",
    )
    proj_down = down_sum.astype(jnp.bfloat16)
    down_wide = lax.optimization_barrier(proj_down).astype(jnp.float32)
    turn_count = micro_count + section_count - 1
    is_first = section_idx == 0
    is_last = section_idx == section_count - 1

    def build_input(c_in, slot_idx):
        c_all = lax.all_gather(c_in, "dp", axis=0, tiled=True)
        rebuilt = lax.dot_general(c_all, basis, contract_last, precision=highest)
        base_rows = lax.dynamic_index_in_dim(base, slot_idx, 0, keepdims=False)
        return (base_rows.astype(jnp.float32) + rebuilt).astype(jnp.bfloat16)

    def forward_slot(turn_idx):
        micro_idx = turn_idx - section_idx
        is_live = (micro_idx >= 0) & (micro_idx < micro_count)
        return (jnp.clip(micro_idx, 0, micro_count - 1), is_live)

    def backward_slot(turn_idx):
        micro_idx = turn_idx - (section_count - 1 - section_idx)
        is_live = (micro_idx >= 0) & (micro_idx < micro_count)
        return (jnp.clip(micro_idx, 0, micro_count - 1), is_live)

    def outgoing(received, slot_idx, is_live):
        supplied = lax.dynamic_index_in_dim(cotangent, slot_idx, 0, keepdims=False)
        g_out = jnp.where(is_last, supplied, received)
        return jnp.where(is_live, g_out, jnp.zeros_like(g_out))

    def forward_step(turn_idx, loop_state):
        received, inputs_store, pre_store, coef_store = loop_state
        slot_idx, is_live = forward_slot(turn_idx)
        c_in = jnp.where(is_first, jnp.zeros_like(received), received)
        section_input = build_input(c_in, slot_idx)
        pre_act = lax.psum_scatter(
            jnp.dot(section_input, w_in_loc, preferred_element_type=jnp.float32),
            "dp",
            scatter_dimension=0,
            tiled=True,
        )
        hidden = jax.nn.silu(pre_act).astype(jnp.bfloat16)
        coef_mix = lax.psum(
            jnp.dot(hidden, proj_down, preferred_element_type=jnp.float32), "tensor"
        )
        c_out = jnp.dot(c_in, gram_matrix, precision=highest) + coef_mix
        inputs_store = put_block(inputs_store, section_input, slot_idx, is_live)
        pre_store = put_block(pre_store, pre_act, slot_idx, is_live)
        coef_store = put_block(coef_store, c_out, slot_idx, is_live)
        return (pass_on(c_out, 1), inputs_store, pre_store, coef_store)

    initial = (
        jnp.zeros((tok_rows, rank_width), jnp.float32),
        jnp.zeros((micro_count, all_rows, width_share), jnp.bfloat16),
        jnp.zeros((micro_count, tok_rows, hid_local), jnp.float32),
        jnp.zeros((micro_count, tok_rows, rank_width), jnp.float32),
    )
    unused, inputs_store, pre_store, coef_store = lax.fori_loop(
        0, turn_count, forward_step, initial
    )

    def backward_step(turn_idx, loop_state):
        received, grad_store, acc_up, acc_coef = loop_state
        slot_idx, is_live = backward_slot(turn_idx)
        g_out = outgoing(received, slot_idx, is_live)
        section_input = lax.dynamic_index_in_dim(inputs_store, slot_idx, 0, keepdims=False)
        pre_act = lax.dynamic_index_in_dim(pre_store, slot_idx, 0, keepdims=False)
        g_hidden = lax.dot_general(g_out, down_wide, contract_last, precision=highest)
        g_pre = g_hidden * silu_slope(pre_act)
        back_sum = lax.psum(jnp.dot(g_pre, proj_up, precision=highest), "tensor")
        g_in = jnp.dot(g_out, gram_matrix, precision=highest) + back_sum
        grad_store = put_block(grad_store, g_in, slot_idx, is_live)
        slope_all = lax.all_gather(g_pre.astype(jnp.bfloat16), "dp", axis=0, tiled=True)
        acc_up = acc_up + lax.dot_general(
            section_input, slope_all, contract_first, preferred_element_type=jnp.float32
        )
        hidden_wide = lax.optimization_barrier(jax.nn.silu(pre_act).astype(jnp.bfloat16)).astype(
            jnp.float32
        )
        acc_coef = acc_coef + lax.dot_general(hidden_wide, g_out, contract_first, precision=highest)
        return (pass_on(g_in, -1), grad_store, acc_up, acc_coef)

    initial_back = (
        jnp.zeros((tok_rows, rank_width), jnp.float32),
        jnp.zeros((micro_count, tok_rows, rank_width), jnp.float32),
        jnp.zeros((width_share, hid_local), jnp.float32),
        jnp.zeros((hid_local, rank_width), jnp.float32),
    )
    unused, grad_store, acc_up, acc_coef = lax.fori_loop(0, turn_count, backward_step, initial_back)
    totals = lax.psum(acc_coef, "dp")
    return (coef_store[None], grad_store[None], acc_up.astype(jnp.bfloat16)[None], totals[None])


def solution(mesh):
    return jax.shard_map(
        on_device,
        mesh=mesh,
        in_specs=(
            P(None, None, "dp"),
            P("section", "dp", "tensor"),
            P("section", "tensor", "dp"),
            P("dp", None),
            P(None, "dp", None),
        ),
        out_specs=(
            P("section", None, "dp", None),
            P("section", None, "dp", None),
            P("section", "dp", "tensor"),
            P("section", "tensor", None),
        ),
        check_vma=False,
    )
```

profile of v0, /device:TPU:1, one launch (start us, length us, event | category | flops | bytes accessed | tf_op | source)
XLA Modules:
  0.0 1726.6 jit_solution(12208410979756206619)
XLA Ops:
  30.3 137.6 %all-reduce.8 = bf16[3584,128]{1,0:T(8,128)(2,1)} all-reduce(f32[3584,128]{1,0:T(8,128)S(1)} %fusion.13), channel_id=1, replica_groups=mesh['section'=4,'dp'=8,'tensor'=4] {'dp'}, use_global_device_ids=true, to_apply=%region_0.0 | all-reduce | flops 458752 | bytes 2752512 | tf_op jit(solution)/shard_map/psum | solution.py:41
  182.1 983.9 %while.41 = (s32[]{:T(128)}, f32[32,128]{1,0:T(8,128)S(1)}, bf16[4,256,1024]{2,1,0:T(8,128)(2,1)}, f32[4,32,3584]{2,1,0:T(8,128)}, f32[4,32,128]{2,1,0:T(8,128)S...) while((s32[]{:T(128)}, f32[32,128]{1,0:T(8,128)S(1)}, ...), condition=%wide.region_5.6_spmd, body=%wide.region_2.5_spmd.sunk | while | flops 2319106048 | bytes 33702228 | solution.py:103
  182.1 21.9 %all_gather.19 = f32[256,128]{1,0:T(8,128)S(1)} all-gather(f32[32,128]{1,0:T(8,128)S(1)} %broadcast_select_fusion.2), channel_id=1, replica_groups=mesh['section'=4,'dp'=8,'tensor'=4] {'dp'}, dimensions={0}, use_global_device_ids=true | all-gather | bytes 147456 | tf_op jit(solution)/shard_map/while/body/eval_jaxpr/all_gather | solution.py:56
  216.1 84.6 %reduce-scatter.2.cloned.1.call-done = f32[32,3584]{1,0:T(8,128)} async-done(((f32[256,3584]{1,0:T(8,128)}), f32[32,3584]{1,0:T(8,128)}) %reduce-scatter.2.cloned.1.call-update) | async-done | bytes 458768 | tf_op jit(solution)/shard_map/while/body/eval_jaxpr/reduce_scatter | solution.py:81
  319.8 22.0 %all_gather.19 = f32[256,128]{1,0:T(8,128)S(1)} all-gather(f32[32,128]{1,0:T(8,128)S(1)} %broadcast_select_fusion.2), channel_id=1, replica_groups=mesh['section'=4,'dp'=8,'tensor'=4] {'dp'}, dimensions={0}, use_global_device_ids=true | all-gather | bytes 147456 | tf_op jit(solution)/shard_map/while/body/eval_jaxpr/all_gather | solution.py:56
  353.9 87.8 %reduce-scatter.2.cloned.1.call-done = f32[32,3584]{1,0:T(8,128)} async-done(((f32[256,3584]{1,0:T(8,128)}), f32[32,3584]{1,0:T(8,128)}) %reduce-scatter.2.cloned.1.call-update) | async-done | bytes 458768 | tf_op jit(solution)/shard_map/while/body/eval_jaxpr/reduce_scatter | solution.py:81
  460.8 22.0 %all_gather.19 = f32[256,128]{1,0:T(8,128)S(1)} all-gather(f32[32,128]{1,0:T(8,128)S(1)} %broadcast_select_fusion.2), channel_id=1, replica_groups=mesh['section'=4,'dp'=8,'tensor'=4] {'dp'}, dimensions={0}, use_global_device_ids=true | all-gather | bytes 147456 | tf_op jit(solution)/shard_map/while/body/eval_jaxpr/all_gather | solution.py:56
  495.0 87.8 %reduce-scatter.2.cloned.1.call-done = f32[32,3584]{1,0:T(8,128)} async-done(((f32[256,3584]{1,0:T(8,128)}), f32[32,3584]{1,0:T(8,128)}) %reduce-scatter.2.cloned.1.call-update) | async-done | bytes 458768 | tf_op jit(solution)/shard_map/while/body/eval_jaxpr/reduce_scatter | solution.py:81
  601.8 22.1 %all_gather.19 = f32[256,128]{1,0:T(8,128)S(1)} all-gather(f32[32,128]{1,0:T(8,128)S(1)} %broadcast_select_fusion.2), channel_id=1, replica_groups=mesh['section'=4,'dp'=8,'tensor'=4] {'dp'}, dimensions={0}, use_global_device_ids=true | all-gather | bytes 147456 | tf_op jit(solution)/shard_map/while/body/eval_jaxpr/all_gather | solution.py:56
  636.0 87.8 %reduce-scatter.2.cloned.1.call-done = f32[32,3584]{1,0:T(8,128)} async-done(((f32[256,3584]{1,0:T(8,128)}), f32[32,3584]{1,0:T(8,128)}) %reduce-scatter.2.cloned.1.call-update) | async-done | bytes 458768 | tf_op jit(solution)/shard_map/while/body/eval_jaxpr/reduce_scatter | solution.py:81
  742.9 22.0 %all_gather.19 = f32[256,128]{1,0:T(8,128)S(1)} all-gather(f32[32,128]{1,0:T(8,128)S(1)} %broadcast_select_fusion.2), channel_id=1, replica_groups=mesh['section'=4,'dp'=8,'tensor'=4] {'dp'}, dimensions={0}, use_global_device_ids=true | all-gather | bytes 147456 | tf_op jit(solution)/shard_map/while/body/eval_jaxpr/all_gather | solution.py:56
  777.0 87.8 %reduce-scatter.2.cloned.1.call-done = f32[32,3584]{1,0:T(8,128)} async-done(((f32[256,3584]{1,0:T(8,128)}), f32[32,3584]{1,0:T(8,128)}) %reduce-scatter.2.cloned.1.call-update) | async-done | bytes 458768 | tf_op jit(solution)/shard_map/while/body/eval_jaxpr/reduce_scatter | solution.py:81
  883.9 22.1 %all_gather.19 = f32[256,128]{1,0:T(8,128)S(1)} all-gather(f32[32,128]{1,0:T(8,128)S(1)} %broadcast_select_fusion.2), channel_id=1, replica_groups=mesh['section'=4,'dp'=8,'tensor'=4] {'dp'}, dimensions={0}, use_global_device_ids=true | all-gather | bytes 147456 | tf_op jit(solution)/shard_map/while/body/eval_jaxpr/all_gather | solution.py:56
  918.0 87.8 %reduce-scatter.2.cloned.1.call-done = f32[32,3584]{1,0:T(8,128)} async-done(((f32[256,3584]{1,0:T(8,128)}), f32[32,3584]{1,0:T(8,128)}) %reduce-scatter.2.cloned.1.call-update) | async-done | bytes 458768 | tf_op jit(solution)/shard_map/while/body/eval_jaxpr/reduce_scatter | solution.py:81
  1025.0 22.0 %all_gather.19 = f32[256,128]{1,0:T(8,128)S(1)} all-gather(f32[32,128]{1,0:T(8,128)S(1)} %broadcast_select_fusion.2), channel_id=1, replica_groups=mesh['section'=4,'dp'=8,'tensor'=4] {'dp'}, dimensions={0}, use_global_device_ids=true | all-gather | bytes 147456 | tf_op jit(solution)/shard_map/while/body/eval_jaxpr/all_gather | solution.py:56
  1059.1 87.8 %reduce-scatter.2.cloned.1.call-done = f32[32,3584]{1,0:T(8,128)} async-done(((f32[256,3584]{1,0:T(8,128)}), f32[32,3584]{1,0:T(8,128)}) %reduce-scatter.2.cloned.1.call-update) | async-done | bytes 458768 | tf_op jit(solution)/shard_map/while/body/eval_jaxpr/reduce_scatter | solution.py:81
  1166.6 451.7 %while.42 = (s32[]{:T(128)}, f32[32,128]{1,0:T(8,128)S(1)}, f32[4,32,128]{2,1,0:T(8,128)S(1)}, f32[1024,3584]{1,0:T(8,128)}, f32[3584,128]{1,0:T(8,128)}, /*inde...) while((s32[]{:T(128)}, f32[32,128]{1,0:T(8,128)S(1)}, ...), condition=%wide.region_9.10_spmd.clone, body=%wide.region_7.9_spmd.clone.sunk | while | flops 2423705600 | bytes 48152904 | solution.py:134
  1193.0 26.6 %all-gather.2.cloned.1.call-done = bf16[256,3584]{1,0:T(8,128)(2,1)} async-done(((bf16[32,3584]{1,0:T(8,128)(2,1)}), bf16[256,3584]{1,0:T(8,128)(2,1)}) %all-gather.2.cloned.1.call-update) | async-done | bytes 1835024 | tf_op jit(solution)/shard_map/while/body/eval_jaxpr/all_gather | solution.py:118
  1258.1 21.5 %all-gather.2.cloned.1.call-done = bf16[256,3584]{1,0:T(8,128)(2,1)} async-done(((bf16[32,3584]{1,0:T(8,128)(2,1)}), bf16[256,3584]{1,0:T(8,128)(2,1)}) %all-gather.2.cloned.1.call-update) | async-done | bytes 1835024 | tf_op jit(solution)/shard_map/while/body/eval_jaxpr/all_gather | solution.py:118
  1322.9 22.0 %all-gather.2.cloned.1.call-done = bf16[256,3584]{1,0:T(8,128)(2,1)} async-done(((bf16[32,3584]{1,0:T(8,128)(2,1)}), bf16[256,3584]{1,0:T(8,128)(2,1)}) %all-gather.2.cloned.1.call-update) | async-done | bytes 1835024 | tf_op jit(solution)/shard_map/while/body/eval_jaxpr/all_gather | solution.py:118
  1388.5 21.7 %all-gather.2.cloned.1.call-done = bf16[256,3584]{1,0:T(8,128)(2,1)} async-done(((bf16[32,3584]{1,0:T(8,128)(2,1)}), bf16[256,3584]{1,0:T(8,128)(2,1)}) %all-gather.2.cloned.1.call-update) | async-done | bytes 1835024 | tf_op jit(solution)/shard_map/while/body/eval_jaxpr/all_gather | solution.py:118
  1453.0 22.2 %all-gather.2.cloned.1.call-done = bf16[256,3584]{1,0:T(8,128)(2,1)} async-done(((bf16[32,3584]{1,0:T(8,128)(2,1)}), bf16[256,3584]{1,0:T(8,128)(2,1)}) %all-gather.2.cloned.1.call-update) | async-done | bytes 1835024 | tf_op jit(solution)/shard_map/while/body/eval_jaxpr/all_gather | solution.py:118
  1518.1 22.3 %all-gather.2.cloned.1.call-done = bf16[256,3584]{1,0:T(8,128)(2,1)} async-done(((bf16[32,3584]{1,0:T(8,128)(2,1)}), bf16[256,3584]{1,0:T(8,128)(2,1)}) %all-gather.2.cloned.1.call-update) | async-done | bytes 1835024 | tf_op jit(solution)/shard_map/while/body/eval_jaxpr/all_gather | solution.py:118
  1628.0 89.2 %all-reduce.5.cloned.1.call-done = f32[1,3584,128]{2,1,0:T(8,128)} async-done(((f32[1,3584,128]{2,1,0:T(8,128)}), f32[1,3584,128]{2,1,0:T(8,128)}) %all-reduce.5.cloned.1.call-update) | async-done | bytes 1835024 | tf_op jit(solution)/shard_map/psum | solution.py:135
  (231 shorter events, 583.3 us)
Async XLA Ops:
  7.2 171.9 %all-reduce.7.cloned.1.call-start = ((), (), s32[]{:S(2)}) async-start(), calls=%async_computation.2 | async-start | bytes 3801088 | tf_op jit(solution)/shard_map/psum | solution.py:41
  182.1 118.6 %reduce-scatter.2.cloned.1.call-start = ((), (), s32[]{:S(2)}) async-start(), calls=%async_computation.3 | async-start | bytes 4128768 | tf_op jit(solution)/shard_map/while/body/eval_jaxpr/reduce_scatter | solution.py:81
  319.8 121.9 %reduce-scatter.2.cloned.1.call-start = ((), (), s32[]{:S(2)}) async-start(), calls=%async_computation.3 | async-start | bytes 4128768 | tf_op jit(solution)/shard_map/while/body/eval_jaxpr/reduce_scatter | solution.py:81
  460.8 122.0 %reduce-scatter.2.cloned.1.call-start = ((), (), s32[]{:S(2)}) async-start(), calls=%async_computation.3 | async-start | bytes 4128768 | tf_op jit(solution)/shard_map/while/body/eval_jaxpr/reduce_scatter | solution.py:81
  601.8 122.0 %reduce-scatter.2.cloned.1.call-start = ((), (), s32[]{:S(2)}) async-start(), calls=%async_computation.3 | async-start | bytes 4128768 | tf_op jit(solution)/shard_map/while/body/eval_jaxpr/reduce_scatter | solution.py:81
  738.7 4.1 collective-permute-start
  742.9 121.9 %reduce-scatter.2.cloned.1.call-start = ((), (), s32[]{:S(2)}) async-start(), calls=%async_computation.3 | async-start | bytes 4128768 | tf_op jit(solution)/shard_map/while/body/eval_jaxpr/reduce_scatter | solution.py:81
  883.9 122.0 %reduce-scatter.2.cloned.1.call-start = ((), (), s32[]{:S(2)}) async-start(), calls=%async_computation.3 | async-start | bytes 4128768 | tf_op jit(solution)/shard_map/while/body/eval_jaxpr/reduce_scatter | solution.py:81
  1024.9 121.9 %reduce-scatter.2.cloned.1.call-start = ((), (), s32[]{:S(2)}) async-start(), calls=%async_computation.3 | async-start | bytes 4128768 | tf_op jit(solution)/shard_map/while/body/eval_jaxpr/reduce_scatter | solution.py:81
  1166.6 53.0 %all-gather.2.cloned.1.call-start = ((), (), s32[]{:S(2)}) async-start(), calls=%async_computation.4 | async-start | bytes 2064384 | tf_op jit(solution)/shard_map/while/body/eval_jaxpr/all_gather | solution.py:118
  1188.2 40.4 %collective-permute-start.1 = (f32[32,128]{1,0:T(8,128)S(1)}, f32[32,128]{1,0:T(8,128)S(1)}, u32[]{:S(2)}, u32[]{:S(2)}) collective-permute-start(f32[32,128]{1,0:T(8,128)S(1)} %get-tuple-element.776), channel_id=1, source_target_pairs={{32,0},{64,32},{96,64},{33,1},{65,33},{97,65},{34,2},{66,34},{98,6... | collective-permute-start | bytes 49160 | tf_op jit(solution)/shard_map/while/body/eval_jaxpr/ppermute | solution.py:10
  1228.6 51.0 %all-gather.2.cloned.1.call-start = ((), (), s32[]{:S(2)}) async-start(), calls=%async_computation.4 | async-start | bytes 2064384 | tf_op jit(solution)/shard_map/while/body/eval_jaxpr/all_gather | solution.py:118
  1251.8 41.1 %collective-permute-start.1 = (f32[32,128]{1,0:T(8,128)S(1)}, f32[32,128]{1,0:T(8,128)S(1)}, u32[]{:S(2)}, u32[]{:S(2)}) collective-permute-start(f32[32,128]{1,0:T(8,128)S(1)} %get-tuple-element.776), channel_id=1, source_target_pairs={{32,0},{64,32},{96,64},{33,1},{65,33},{97,65},{34,2},{66,34},{98,6... | collective-permute-start | bytes 49160 | tf_op jit(solution)/shard_map/while/body/eval_jaxpr/ppermute | solution.py:10
  1292.9 52.0 %all-gather.2.cloned.1.call-start = ((), (), s32[]{:S(2)}) async-start(), calls=%async_computation.4 | async-start | bytes 2064384 | tf_op jit(solution)/shard_map/while/body/eval_jaxpr/all_gather | solution.py:118
  1316.5 41.5 %collective-permute-start.1 = (f32[32,128]{1,0:T(8,128)S(1)}, f32[32,128]{1,0:T(8,128)S(1)}, u32[]{:S(2)}, u32[]{:S(2)}) collective-permute-start(f32[32,128]{1,0:T(8,128)S(1)} %get-tuple-element.776), channel_id=1, source_target_pairs={{32,0},{64,32},{96,64},{33,1},{65,33},{97,65},{34,2},{66,34},{98,6... | collective-permute-start | bytes 49160 | tf_op jit(solution)/shard_map/while/body/eval_jaxpr/ppermute | solution.py:10
  1358.0 52.2 %all-gather.2.cloned.1.call-start = ((), (), s32[]{:S(2)}) async-start(), calls=%async_computation.4 | async-start | bytes 2064384 | tf_op jit(solution)/shard_map/while/body/eval_jaxpr/all_gather | solution.py:118
  1382.2 41.3 %collective-permute-start.1 = (f32[32,128]{1,0:T(8,128)S(1)}, f32[32,128]{1,0:T(8,128)S(1)}, u32[]{:S(2)}, u32[]{:S(2)}) collective-permute-start(f32[32,128]{1,0:T(8,128)S(1)} %get-tuple-element.776), channel_id=1, source_target_pairs={{32,0},{64,32},{96,64},{33,1},{65,33},{97,65},{34,2},{66,34},{98,6... | collective-permute-start | bytes 49160 | tf_op jit(solution)/shard_map/while/body/eval_jaxpr/ppermute | solution.py:10
  1423.5 51.7 %all-gather.2.cloned.1.call-start = ((), (), s32[]{:S(2)}) async-start(), calls=%async_computation.4 | async-start | bytes 2064384 | tf_op jit(solution)/shard_map/while/body/eval_jaxpr/all_gather | solution.py:118
  1446.6 41.7 %collective-permute-start.1 = (f32[32,128]{1,0:T(8,128)S(1)}, f32[32,128]{1,0:T(8,128)S(1)}, u32[]{:S(2)}, u32[]{:S(2)}) collective-permute-start(f32[32,128]{1,0:T(8,128)S(1)} %get-tuple-element.776), channel_id=1, source_target_pairs={{32,0},{64,32},{96,64},{33,1},{65,33},{97,65},{34,2},{66,34},{98,6... | collective-permute-start | bytes 49160 | tf_op jit(solution)/shard_map/while/body/eval_jaxpr/ppermute | solution.py:10
  1488.4 52.0 %all-gather.2.cloned.1.call-start = ((), (), s32[]{:S(2)}) async-start(), calls=%async_computation.4 | async-start | bytes 2064384 | tf_op jit(solution)/shard_map/while/body/eval_jaxpr/all_gather | solution.py:118
  1511.8 41.8 %collective-permute-start.1 = (f32[32,128]{1,0:T(8,128)S(1)}, f32[32,128]{1,0:T(8,128)S(1)}, u32[]{:S(2)}, u32[]{:S(2)}) collective-permute-start(f32[32,128]{1,0:T(8,128)S(1)} %get-tuple-element.776), channel_id=1, source_target_pairs={{32,0},{64,32},{96,64},{33,1},{65,33},{97,65},{34,2},{66,34},{98,6... | collective-permute-start | bytes 49160 | tf_op jit(solution)/shard_map/while/body/eval_jaxpr/ppermute | solution.py:10
  1553.6 51.5 %all-gather.2.cloned.1.call-start = ((), (), s32[]{:S(2)}) async-start(), calls=%async_computation.4 | async-start | bytes 2064384 | tf_op jit(solution)/shard_map/while/body/eval_jaxpr/all_gather | solution.py:118
  1577.3 41.0 %collective-permute-start.1 = (f32[32,128]{1,0:T(8,128)S(1)}, f32[32,128]{1,0:T(8,128)S(1)}, u32[]{:S(2)}, u32[]{:S(2)}) collective-permute-start(f32[32,128]{1,0:T(8,128)S(1)} %get-tuple-element.776), channel_id=1, source_target_pairs={{32,0},{64,32},{96,64},{33,1},{65,33},{97,65},{34,2},{66,34},{98,6... | collective-permute-start | bytes 49160 | tf_op jit(solution)/shard_map/while/body/eval_jaxpr/ppermute | solution.py:10
  1618.3 98.9 %all-reduce.5.cloned.1.call-start = ((), (), s32[]{:S(2)}) async-start(), calls=%async_computation.1 | async-start | bytes 3670016 | tf_op jit(solution)/shard_map/psum | solution.py:135
  (17 other events, 166.7 us)
Sparse Core Ops, SparseCore 0:
  21.2 157.8 all-reduce.6
  215.1 85.4 reduce-scatter.1
  352.9 88.6 reduce-scatter.1
  494.0 88.7 reduce-scatter.1
  635.0 88.7 reduce-scatter.1
  776.1 88.6 reduce-scatter.1
  917.1 88.7 reduce-scatter.1
  1058.1 88.6 reduce-scatter.1
  1171.1 48.4 all-gather.1
  1233.1 46.4 all-gather.1
  1297.4 47.3 all-gather.1
  1362.6 47.6 all-gather.1
  1428.0 47.1 all-gather.1
  1492.9 47.4 all-gather.1
  1558.1 46.9 all-gather.1
  1621.5 95.6 all-reduce.4
where the time goes:
time: 1730 us
  waiting for transfers between devices  869 us (50%)
  blocking collectives  497 us (29%)
  matrix products  262 us (15%)
  starting transfers between devices  31.9 us (2%)
  other arithmetic  29.3 us (2%)
  local copies, waits for them, and re-layouts  22.5 us (1%)
    reduce_scatter x7, waiting for transfers between devices, forward_step(): lax.psum_scatter(jnp.dot(section_input, w_in_loc, preferred_element_type=...  611 us
    all_gather x7, waiting for transfers between devices, backward_step(): lax.all_gather(g_pre.astype(jnp.bfloat16), 'dp', axis=0, tiled=True)  158 us
    all_gather x7, blocking collectives, build_input(): c_all = lax.all_gather(c_in, 'dp', axis=0, tiled=True)  154 us
    psum x1, blocking collectives, on_device(): lax.psum((lax.dot_general(basis, basis, contract_first, precision=highest...  138 us
    psum x7, blocking collectives, backward_step(): back_sum = lax.psum(jnp.dot(g_pre, proj_up, precision=highest), 'tensor')  113 us
    psum x7, blocking collectives, forward_step(): lax.psum(jnp.dot(hidden, proj_down, preferred_element_type=jnp.float32),...  92.1 us
    psum x1, waiting for transfers between devices, on_device(): totals = lax.psum(acc_coef, 'dp')  89.2 us
    dot_general x7, matrix products, backward_step(): lax.dot_general(section_input, slope_all, contract_first, preferred_eleme...  88.3 us
  transfers between devices with their start and end apart: 30, of which 16 were waited for; matrix products, arithmetic and copies ran while one was open for 10% of the time, Pallas kernels for 0%

commit v1 on v0

v1 whole, which is shorter than its diff:
```python
import jax
import jax.numpy as jnp
from jax import lax
from jax.experimental import pallas as pl
from jax.experimental.pallas import tpu as pltpu
from jax.sharding import PartitionSpec as P

BF = jnp.bfloat16
F32 = jnp.float32
HIGHEST = lax.Precision.HIGHEST
NT = (((1,), (1,)), ((), ()))
CHUNK = 512


def split2(x):
    hi = x.astype(BF)
    return hi, (x - hi.astype(F32)).astype(BF)


def mm(a, b):
    return jnp.dot(a, b, preferred_element_type=F32)


def mm_nt(a, b):
    return lax.dot_general(a, b, NT, preferred_element_type=F32)


def sigma(v):
    return 0.5 * jnp.tanh(0.5 * v) + 0.5


def wide(x):
    hi, lo = split2(x)
    return jnp.concatenate([hi, lo], axis=1)


def twice(x):
    return jnp.concatenate([x, x], axis=0)


def chunks_of(width):
    return [slice(i, i + CHUNK) for i in range(0, width, CHUNK)]


def gram_share(x, gram):
    return 0.25 * jnp.dot(x, gram, precision=HIGHEST, preferred_element_type=F32)


def forward_kernel(base_ref, up_ref, down_ref, gram_ref, r0, r1, r2, r3, part_ref):
    c = (r0[...] + r1[...]) + (r2[...] + r3[...])
    cw = wide(c)
    acc = gram_share(c, gram_ref[...])
    for cols in chunks_of(base_ref.shape[1]):
        pre = base_ref[:, cols] + mm(cw, twice(up_ref[:, cols]))
        hidden = (pre * sigma(pre)).astype(BF)
        acc += mm_nt(hidden, down_ref[:, cols])
    part_ref[...] = acc


def first_kernel(base_ref, down_ref, part_ref):
    acc = jnp.zeros(part_ref.shape, F32)
    for cols in chunks_of(base_ref.shape[1]):
        pre = base_ref[:, cols]
        hidden = (pre * sigma(pre)).astype(BF)
        acc += mm_nt(hidden, down_ref[:, cols])
    part_ref[...] = acc


def middle_kernel(
    base_ref, up_ref, down_ref, gram_ref, r0, r1, r2, r3, c_ref, part_ref, hidden_ref, slope_ref
):
    c = (r0[...] + r1[...]) + (r2[...] + r3[...])
    c_ref[...] = c
    cw = wide(c)
    acc = gram_share(c, gram_ref[...])
    for cols in chunks_of(base_ref.shape[1]):
        pre = base_ref[:, cols] + mm(cw, twice(up_ref[:, cols]))
        sig = sigma(pre)
        hidden = (pre * sig).astype(BF)
        hidden_ref[:, cols] = hidden
        slope_ref[:, cols] = sig * (1.0 + pre * (1.0 - sig))
        acc += mm_nt(hidden, down_ref[:, cols])
    part_ref[...] = acc


def backward_kernel(slope_ref, up_ref, down_ref, gram_ref, g_ref, part_ref):
    g = g_ref[...]
    gw = wide(g)
    acc = gram_share(g, gram_ref[...])
    for cols in chunks_of(slope_ref.shape[1]):
        g_pre = mm(gw, twice(down_ref[:, cols])) * slope_ref[:, cols]
        hi, lo = split2(g_pre)
        acc += mm_nt(hi, up_ref[:, cols]) + mm_nt(lo, up_ref[:, cols])
    part_ref[...] = acc


def last_kernel(slope_ref, hidden_ref, up_ref, down_ref, gram_ref, g_ref, part_ref, g_pre_ref, dc_ref):
    g = g_ref[...]
    gw = wide(g)
    gt = wide(g.T)
    acc = gram_share(g, gram_ref[...])
    for cols in chunks_of(slope_ref.shape[1]):
        g_pre = mm(gw, twice(down_ref[:, cols])) * slope_ref[:, cols]
        hi, lo = split2(g_pre)
        g_pre_ref[:, cols] = hi
        dc_ref[:, cols] = mm(gt, twice(hidden_ref[:, cols])).astype(BF)
        acc += mm_nt(hi, up_ref[:, cols]) + mm_nt(lo, up_ref[:, cols])
    part_ref[...] = acc


def call(kernel, outs, *args):
    return pl.pallas_call(
        kernel,
        out_shape=outs,
        compiler_params=pltpu.CompilerParams(vmem_limit_bytes=40 * 1024 * 1024),
    )(*args)


def relay(x, by, k, sections, tensors):
    pairs = [
        (s * tensors + t, (s + by) * tensors + (t ^ k))
        for s in range(sections)
        for t in range(tensors)
        if 0 <= s + by < sections
    ]
    return lax.ppermute(x, ("section", "tensor"), pairs)


def tensor_sum(x, tensors):
    parts = [x] + [
        lax.ppermute(x, "tensor", [(t, t ^ k) for t in range(tensors)]) for k in range(1, tensors)
    ]
    return (parts[0] + parts[1]) + (parts[2] + parts[3])


def swap(x):
    return lax.all_to_all(x, "dp", 0, 0, tiled=True)


def spread(x, count):
    return swap(jnp.broadcast_to(x[None], (count,) + x.shape))


def on_device(base, w_in, w_out, basis, cotangent):
    sections = lax.axis_size("section")
    tensors = lax.axis_size("tensor")
    dp = lax.axis_size("dp")
    is_last = lax.axis_index("section") == sections - 1
    micro, tokens, width = base.shape
    rows = tokens // dp
    own = micro * rows
    rank = basis.shape[1]
    w_in = w_in[0]
    w_out = w_out[0]
    hid = w_in.shape[1]
    tok = jax.ShapeDtypeStruct((own, rank), F32)
    wide_bf = jax.ShapeDtypeStruct((own, hid), BF)
    wide_f = jax.ShapeDtypeStruct((own, hid), F32)

    base_rows = base.reshape(micro, dp, rows, width).transpose(1, 0, 2, 3).reshape(dp * own, width)
    basis_t = wide(basis).T
    gram = lax.psum(
        lax.dot_general(basis, basis, (((0,), (0,)), ((), ())), precision=HIGHEST), "dp"
    )
    up2 = mm(basis_t, w_in)
    down2 = mm_nt(basis_t, w_out)
    proj = jnp.concatenate(
        [
            (up2[:rank] + up2[rank:]).astype(BF).reshape(dp, rank // dp, hid),
            (down2[:rank] + down2[rank:]).astype(BF).reshape(dp, rank // dp, hid),
        ],
        axis=1,
    )
    proj = jnp.sum(swap(proj).reshape(dp, 2 * rank // dp, hid).astype(F32), axis=0).astype(BF)
    proj = spread(proj, dp).reshape(dp, 2, rank // dp, hid)
    up = proj[:, 0].reshape(rank, hid)
    down = proj[:, 1].reshape(rank, hid)
    base_part = mm(base_rows, w_in).astype(BF).reshape(dp, own, hid)
    base_pre = jnp.sum(swap(base_part).astype(F32), axis=0)

    part = call(first_kernel, tok, base_pre, down)
    for turn in range(1, sections - 1):
        got = [relay(part, 1, k, sections, tensors) for k in range(tensors)]
        part = call(forward_kernel, tok, base_pre, up, down, gram, *got)
    got = [relay(part, 1, k, sections, tensors) for k in range(tensors)]
    c_in, part, hidden, slope = call(
        middle_kernel, (tok, tok, wide_bf, wide_f), base_pre, up, down, gram, *got
    )
    coefs = tensor_sum(part, tensors)
    c_all = spread(c_in.astype(BF), dp).reshape(dp * own, rank)

    cot = cotangent.reshape(own, rank)
    g_out = cot
    for turn in range(sections - 1):
        part = call(backward_kernel, tok, slope, up, down, gram, g_out)
        got = [relay(part, -1, k, sections, tensors) for k in range(tensors)]
        g_out = jnp.where(is_last, cot, (got[0] + got[1]) + (got[2] + got[3]))
    part, g_pre, dc = call(
        last_kernel, (tok, wide_bf, jax.ShapeDtypeStruct((rank, hid), BF)),
        slope, hidden, up, down, gram, g_out,
    )
    grads = tensor_sum(part, tensors)

    dc = jnp.sum(swap(dc.reshape(dp, rank // dp, hid)).astype(F32), axis=0).astype(BF)
    dc = spread(dc, dp).reshape(rank, hid)
    g_all = spread(g_pre, dp).reshape(dp * own, hid)
    inputs = (base_rows.astype(F32) + mm_nt(c_all, basis.astype(BF))).astype(BF)
    grad_up = lax.dot_general(
        inputs, g_all, (((0,), (0,)), ((), ())), preferred_element_type=F32
    ).astype(BF)
    return (
        coefs.reshape(1, micro, rows, rank),
        grads.reshape(1, micro, rows, rank),
        grad_up[None],
        dc.T.astype(F32)[None],
    )


def solution(mesh):
    return jax.shard_map(
        on_device,
        mesh=mesh,
        in_specs=(
            P(None, None, "dp"),
            P("section", "dp", "tensor"),
            P("section", "tensor", "dp"),
            P("dp", None),
            P(None, "dp", None),
        ),
        out_specs=(
            P("section", None, "dp", None),
            P("section", None, "dp", None),
            P("section", "dp", "tensor"),
            P("section", "tensor", None),
        ),
        check_vma=False,
    )
```

time: 1730 us -> 493 us (0.28)
  waiting for transfers between devices: 869 us -> 237 us
  blocking collectives: 497 us -> 42.4 us
  matrix products: 262 us -> 37.2 us
  starting transfers between devices: 31.9 us -> 117 us
  other arithmetic: 29.3 us -> 8.26 us
    reduce_scatter x7 -> x0, waiting for transfers between devices: 611 us -> none  [forward_step(): lax.psum_scatter(jnp.dot(section_input, w_in_loc, preferred_element_type=...]
    psum x15 -> x0, blocking collectives: 343 us -> none  [the longest x1 138 us: on_device(): lax.psum((lax.dot_general(basis, basis, contract_first, precision=highest...]
    dot_general x66 -> x5, matrix products: 262 us -> 37.2 us  [the longest x1 15.3 us: on_device(): lax.dot_general(inputs, g_all, (((0,), (0,)), ((), ())), preferred_elemen...]
    all_gather x7 -> x0, waiting for transfers between devices: 158 us -> none  [backward_step(): lax.all_gather(g_pre.astype(jnp.bfloat16), 'dp', axis=0, tiled=True)]
    all_gather x7 -> x0, blocking collectives: 154 us -> none  [build_input(): c_all = lax.all_gather(c_in, 'dp', axis=0, tiled=True)]
    all_to_all x0 -> x5, waiting for transfers between devices: none -> 137 us  [swap(): return lax.all_to_all(x, 'dp', 0, 0, tiled=True)]
    ppermute x14 -> x30, waiting for transfers between devices: 0.15 us -> 83.9 us  [the longest x6 56.1 us: tensor_sum(): lax.ppermute(x, 'tensor', [(t, t ^ k) for t in range(tensors)])]
    psum x2 -> x1, waiting for transfers between devices: 99.1 us -> 16.2 us  [on_device(): lax.psum(lax.dot_general(basis, basis, (((0,), (0,)), ((), ())), precisio...]
  transfers between devices with their start and end apart: 30 -> 36, of which waited for: 16 -> 23; matrix products, arithmetic and copies ran while one was open for 10% -> 5% of each run, Pallas kernels for 0% -> 0%
where the time goes in v1:
time: 493 us; the launch traced here: 487 us
  waiting for transfers between devices  237 us (48%)
  starting transfers between devices  117 us (24%)
  blocking collectives  42.4 us (9%)
  matrix products  37.2 us (8%)
  local copies, waits for them, and re-layouts  21.7 us (4%)
  between operations  14.6 us (3%)
  Pallas kernels  8.86 us (2%)
  other arithmetic  8.26 us (2%)
    all_to_all x5, waiting for transfers between devices, swap(): return lax.all_to_all(x, 'dp', 0, 0, tiled=True)  137 us
    ppermute x24, starting transfers between devices, relay(): return lax.ppermute(x, ('section', 'tensor'), pairs)  66.2 us
    ppermute x6, waiting for transfers between devices, tensor_sum(): lax.ppermute(x, 'tensor', [(t, t ^ k) for t in range(tensors)])  56.1 us
    all_to_all x2, blocking collectives, swap(): return lax.all_to_all(x, 'dp', 0, 0, tiled=True)  42.4 us
    ppermute x6, starting transfers between devices, tensor_sum(): lax.ppermute(x, 'tensor', [(t, t ^ k) for t in range(tensors)])  30.8 us
    ppermute x24, waiting for transfers between devices, relay(): return lax.ppermute(x, ('section', 'tensor'), pairs)  27.7 us
    all_to_all x5, starting transfers between devices, swap(): return lax.all_to_all(x, 'dp', 0, 0, tiled=True)  20.5 us
    psum x1, waiting for transfers between devices, on_device(): lax.psum(lax.dot_general(basis, basis, (((0,), (0,)), ((), ())), precisio...  16.2 us
  transfers between devices with their start and end apart: 36, of which 23 were waited for; matrix products, arithmetic and copies ran while one was open for 5% of the time, Pallas kernels for 0%

profile of v1, /device:TPU:1, one launch (start us, length us, event | category | flops | bytes accessed | tf_op | source)
XLA Modules:
  0.0 487.2 jit_solution(12995375043876978206)
XLA Ops:
  8.6 5.4 %fusion = f32[256,3584]{1,0:T(8,128)S(1)} fusion(bf16[1,3584,1024]{2,1,0:T(8,128)(2,1)} %param.7, bf16[1024,128]{1,0:T(8,128)(2,1)S(1)} %get-tuple-element.29, bf16[1024,128]{1,0:T(8,128)(2,1)S(1)} %get-tuple-element.28), kind=kOutput, calls=%fused_computation.3 | convolution fusion | flops 1880096768 | bytes 11534336 | tf_op jit(solution)/shard_map/dot_general | solution.py:25
  16.7 28.5 %all_to_all.35 = bf16[8,32,3584]{2,1,0:T(8,128)(2,1)S(1)} all-to-all(bf16[8,32,3584]{2,1,0:T(8,128)(2,1)S(1)} %pad_maximum_fusion), channel_id=1, replica_groups=mesh['section'=4,'dp'=8,'tensor'=4] {'dp'}, dimensions={0} | all-to-all | bytes 3670016 | tf_op jit(solution)/shard_map/all_to_all | solution.py:137
  53.7 12.8 %convolution_convert_fusion.1 = bf16[1024,3584]{1,0:T(8,128)(2,1)} fusion(bf16[1024,1024]{1,0:T(8,128)(2,1)S(1)} %bitcast.65, bf16[1,1024,3584]{2,1,0:T(8,128)(2,1)} %param.6), kind=kOutput, calls=%fused_computation.2 | convolution fusion | flops 7519862784 | bytes 16777216 | tf_op jit(solution)/shard_map/dot_general | solution.py:21
  66.5 9.7 %all-to-all-done.2 = bf16[8,32,3584]{2,1,0:T(8,128)(2,1)S(1)} async-done(((bf16[8,32,3584]{2,1,0:T(8,128)(2,1)}), bf16[8,32,3584]{2,1,0:T(8,128)(2,1)S(1)}, u32[]{:S(2)}, u32[]{:S(2)}) %all-to-all-start.2) | async-done | bytes 1835040 | tf_op jit(solution)/shard_map/all_to_all | solution.py:137
  77.4 4.9 %all-to-all-start = ((bf16[8,128,3584]{2,1,0:T(8,128)(2,1)}), bf16[8,128,3584]{2,1,0:T(8,128)(2,1)}, u32[]{:S(2)}, u32[]{:S(2)}) async-start(bf16[8,128,3584]{2,1,0:T(8,128)(2,1)} %bitcast.60), calls=%async_computation | async-start | bytes 14680064 | tf_op jit(solution)/shard_map/all_to_all | solution.py:137
  85.6 97.3 %all-to-all-done = bf16[8,128,3584]{2,1,0:T(8,128)(2,1)} async-done(((bf16[8,128,3584]{2,1,0:T(8,128)(2,1)}), bf16[8,128,3584]{2,1,0:T(8,128)(2,1)}, u32[]{:S(2)}, u32[]{:S(2)}) %all-to-all-start) | async-done | bytes 7340064 | tf_op jit(solution)/shard_map/all_to_all | solution.py:137
  182.9 4.3 convert_reduce_fusion.base_ref
  192.5 5.9 %collective-permute-start.1 = (f32[128,128]{1,0:T(8,128)S(1)}, f32[128,128]{1,0:T(8,128)S(1)}, u32[]{:S(2)}, u32[]{:S(2)}) collective-permute-start(f32[128,128]{1,0:T(8,128)S(1)} %shard_map.84), channel_id=1, source_target_pairs={{0,33},{1,32},{2,35},{3,34},{32,65},{33,64},{34,67},{35,66},{64,97... | collective-permute-start | bytes 196616 | tf_op jit(solution)/shard_map/ppermute | solution.py:126
  198.4 5.6 %collective-permute-start.2 = (f32[128,128]{1,0:T(8,128)S(1)}, f32[128,128]{1,0:T(8,128)S(1)}, u32[]{:S(2)}, u32[]{:S(2)}) collective-permute-start(f32[128,128]{1,0:T(8,128)S(1)} %shard_map.84), channel_id=1, source_target_pairs={{0,34},{1,35},{2,32},{3,33},{32,66},{33,67},{34,64},{35,65},{64,98... | collective-permute-start | bytes 196616 | tf_op jit(solution)/shard_map/ppermute | solution.py:126
  206.3 16.2 %all-reduce.2.cloned.1.call-done.gram_ref = f32[128,128]{1,0:T(8,128)} async-done(((f32[128,128]{1,0:T(8,128)}), f32[128,128]{1,0:T(8,128)}) %all-reduce.2.cloned.1.call-update) | async-done | bytes 65552 | tf_op jit(solution)/shard_map/psum | solution.py:162
  229.0 9.1 %collective-permute-start.5 = (f32[128,128]{1,0:T(8,128)S(1)}, f32[128,128]{1,0:T(8,128)S(1)}, u32[]{:S(2)}, u32[]{:S(2)}) collective-permute-start(f32[128,128]{1,0:T(8,128)S(1)} %shard_map.85), channel_id=1, source_target_pairs={{0,33},{1,32},{2,35},{3,34},{32,65},{33,64},{34,67},{35,66},{64,97... | collective-permute-start | bytes 196616 | tf_op jit(solution)/shard_map/ppermute | solution.py:126
  238.1 5.0 %collective-permute-start.6 = (f32[128,128]{1,0:T(8,128)S(1)}, f32[128,128]{1,0:T(8,128)S(1)}, u32[]{:S(2)}, u32[]{:S(2)}) collective-permute-start(f32[128,128]{1,0:T(8,128)S(1)} %shard_map.85), channel_id=1, source_target_pairs={{0,34},{1,35},{2,32},{3,33},{32,66},{33,67},{34,64},{35,65},{64,98... | collective-permute-start | bytes 196616 | tf_op jit(solution)/shard_map/ppermute | solution.py:126
  248.4 5.3 %collective-permute-start.8 = (f32[128,128]{1,0:T(8,128)S(1)}, f32[128,128]{1,0:T(8,128)S(1)}, u32[]{:S(2)}, u32[]{:S(2)}) collective-permute-start(f32[128,128]{1,0:T(8,128)S(1)} %shard_map.86), channel_id=1, source_target_pairs={{0,32},{1,33},{2,34},{3,35},{32,64},{33,65},{34,66},{35,67},{64,96... | collective-permute-start | bytes 196616 | tf_op jit(solution)/shard_map/ppermute | solution.py:126
  314.8 3.7 all-to-all-start.5
  318.5 14.4 %all-to-all-done.5 = bf16[8,16,3584]{2,1,0:T(8,128)(2,1)S(1)} async-done(((bf16[8,16,3584]{2,1,0:T(8,128)(2,1)}), bf16[8,16,3584]{2,1,0:T(8,128)(2,1)S(1)}, u32[]{:S(2)}, u32[]{:S(2)}) %all-to-all-start.5) | async-done | bytes 917536 | tf_op jit(solution)/shard_map/all_to_all | solution.py:137
  337.1 5.6 %all-to-all-done.3 = bf16[8,128,128]{2,1,0:T(8,128)(2,1)S(1)} async-done(((bf16[8,128,128]{2,1,0:T(8,128)(2,1)}), bf16[8,128,128]{2,1,0:T(8,128)(2,1)S(1)}, u32[]{:S(2)}, u32[]{:S(2)}) %all-to-all-start.3) | async-done | bytes 262176 | tf_op jit(solution)/shard_map/all_to_all | solution.py:137
  342.8 13.9 %all_to_all.36 = bf16[8,16,3584]{2,1,0:T(8,128)(2,1)S(1)} all-to-all(bf16[8,16,3584]{2,1,0:T(8,128)(2,1)S(1)} %broadcast_in_dim.37), channel_id=1, replica_groups=mesh['section'=4,'dp'=8,'tensor'=4] {'dp'}, dimensions={0} | all-to-all | bytes 1835008 | tf_op jit(solution)/shard_map/all_to_all | solution.py:137
  356.7 3.7 broadcast_in_dim.17
  360.4 4.9 %all-to-all-start.4 = ((bf16[8,128,3584]{2,1,0:T(8,128)(2,1)}), bf16[8,128,3584]{2,1,0:T(8,128)(2,1)}, u32[]{:S(2)}, u32[]{:S(2)}) async-start(bf16[8,128,3584]{2,1,0:T(8,128)(2,1)} %broadcast_in_dim.17), calls=%async_computation.4 | async-start | bytes 14680064 | tf_op jit(solution)/shard_map/all_to_all | solution.py:137
  367.1 5.3 %collective-permute-start.14 = (f32[128,128]{1,0:T(8,128)S(1)}, f32[128,128]{1,0:T(8,128)S(1)}, u32[]{:S(2)}, u32[]{:S(2)}) collective-permute-start(f32[128,128]{1,0:T(8,128)S(1)} %get-tuple-element.11), channel_id=1, source_target_pairs={{0,3},{1,2},{2,1},{3,0},{4,7},{5,6},{6,5},{7,4},{8,11},{9,10},{10,... | collective-permute-start | bytes 196616 | tf_op jit(solution)/shard_map/ppermute | solution.py:131
  376.0 52.2 %collective-permute-done.13 = f32[128,128]{1,0:T(8,128)S(1)} collective-permute-done((f32[128,128]{1,0:T(8,128)S(1)}, f32[128,128]{1,0:T(8,128)S(1)}, u32[]{:S(2)}, u32[]{:S(2)}) %collective-permute-start.13) | collective-permute-done | bytes 65568 | tf_op jit(solution)/shard_map/ppermute | solution.py:131
  428.2 20.0 %collective-permute-start.27 = (f32[128,128]{1,0:T(8,128)S(1)}, f32[128,128]{1,0:T(8,128)S(1)}, u32[]{:S(2)}, u32[]{:S(2)}) collective-permute-start(f32[128,128]{1,0:T(8,128)S(1)} %get-tuple-element.14), channel_id=1, source_target_pairs={{0,1},{1,0},{2,3},{3,2},{4,5},{5,4},{6,7},{7,6},{8,9},{9,8},{10,11... | collective-permute-start | bytes 196616 | tf_op jit(solution)/shard_map/ppermute | solution.py:131
  455.4 9.7 %all-to-all-done.4 = bf16[8,128,3584]{2,1,0:T(8,128)(2,1)} async-done(((bf16[8,128,3584]{2,1,0:T(8,128)(2,1)}), bf16[8,128,3584]{2,1,0:T(8,128)(2,1)}, u32[]{:S(2)}, u32[]{:S(2)}) %all-to-all-start.4) | async-done | bytes 7340064 | tf_op jit(solution)/shard_map/all_to_all | solution.py:137
  465.0 15.3 %fusion.5 = bf16[1,1024,3584]{2,1,0:T(8,128)(2,1)} fusion(bf16[1024,3584]{1,0:T(8,128)(2,1)} %bitcast.15, bf16[1024,1024]{1,0:T(8,128)(2,1)} %bitcast.66, bf16[1024,128]{1,0:T(8,128)(2,1)S(1)} %bitcast.67, f32[1024,128]{1,0:T(8,128)S(1)} %copy-done.12), kind=kOutput, calls=%fused_computation.8 | convolution fusion | flops 7791575040 | bytes 17563648 | tf_op jit(solution)/shard_map/dot_general | solution.py:208
  (122 shorter events, 114.0 us)
Async XLA Ops:
  46.9 29.3 %all-to-all-start.2 = ((bf16[8,32,3584]{2,1,0:T(8,128)(2,1)}), bf16[8,32,3584]{2,1,0:T(8,128)(2,1)S(1)}, u32[]{:S(2)}, u32[]{:S(2)}) async-start(bf16[8,32,3584]{2,1,0:T(8,128)(2,1)} %broadcast_in_dim.15), calls=%async_computation.2 | async-start | bytes 3670016 | tf_op jit(solution)/shard_map/all_to_all | solution.py:137
  77.4 105.5 %all-to-all-start = ((bf16[8,128,3584]{2,1,0:T(8,128)(2,1)}), bf16[8,128,3584]{2,1,0:T(8,128)(2,1)}, u32[]{:S(2)}, u32[]{:S(2)}) async-start(bf16[8,128,3584]{2,1,0:T(8,128)(2,1)} %bitcast.60), calls=%async_computation | async-start | bytes 14680064 | tf_op jit(solution)/shard_map/all_to_all | solution.py:137
  82.3 140.2 %all-reduce.2.cloned.1.call-start = ((), (), s32[]{:S(2)}) async-start(), calls=%async_computation.7 | async-start | bytes 131072 | tf_op jit(solution)/shard_map/psum | solution.py:162
  189.0 33.5 %collective-permute-start = (f32[128,128]{1,0:T(8,128)S(1)}, f32[128,128]{1,0:T(8,128)S(1)}, u32[]{:S(2)}, u32[]{:S(2)}) collective-permute-start(f32[128,128]{1,0:T(8,128)S(1)} %shard_map.84), channel_id=1, source_target_pairs={{0,32},{1,33},{2,34},{3,35},{32,64},{33,65},{34,66},{35,67},{64,96... | collective-permute-start | bytes 196616 | tf_op jit(solution)/shard_map/ppermute | solution.py:126
  192.5 29.9 %collective-permute-start.1 = (f32[128,128]{1,0:T(8,128)S(1)}, f32[128,128]{1,0:T(8,128)S(1)}, u32[]{:S(2)}, u32[]{:S(2)}) collective-permute-start(f32[128,128]{1,0:T(8,128)S(1)} %shard_map.84), channel_id=1, source_target_pairs={{0,33},{1,32},{2,35},{3,34},{32,65},{33,64},{34,67},{35,66},{64,97... | collective-permute-start | bytes 196616 | tf_op jit(solution)/shard_map/ppermute | solution.py:126
  198.4 24.0 %collective-permute-start.2 = (f32[128,128]{1,0:T(8,128)S(1)}, f32[128,128]{1,0:T(8,128)S(1)}, u32[]{:S(2)}, u32[]{:S(2)}) collective-permute-start(f32[128,128]{1,0:T(8,128)S(1)} %shard_map.84), channel_id=1, source_target_pairs={{0,34},{1,35},{2,32},{3,33},{32,66},{33,67},{34,64},{35,65},{64,98... | collective-permute-start | bytes 196616 | tf_op jit(solution)/shard_map/ppermute | solution.py:126
  204.0 18.4 %collective-permute-start.3 = (f32[128,128]{1,0:T(8,128)S(1)}, f32[128,128]{1,0:T(8,128)S(1)}, u32[]{:S(2)}, u32[]{:S(2)}) collective-permute-start(f32[128,128]{1,0:T(8,128)S(1)} %shard_map.84), channel_id=1, source_target_pairs={{0,35},{1,34},{2,33},{3,32},{32,67},{33,66},{34,65},{35,64},{64,99... | collective-permute-start | bytes 196616 | tf_op jit(solution)/shard_map/ppermute | solution.py:126
  225.6 20.2 %collective-permute-start.4 = (f32[128,128]{1,0:T(8,128)S(1)}, f32[128,128]{1,0:T(8,128)S(1)}, u32[]{:S(2)}, u32[]{:S(2)}) collective-permute-start(f32[128,128]{1,0:T(8,128)S(1)} %shard_map.85), channel_id=1, source_target_pairs={{0,32},{1,33},{2,34},{3,35},{32,64},{33,65},{34,66},{35,67},{64,96... | collective-permute-start | bytes 196616 | tf_op jit(solution)/shard_map/ppermute | solution.py:126
  229.0 16.8 %collective-permute-start.5 = (f32[128,128]{1,0:T(8,128)S(1)}, f32[128,128]{1,0:T(8,128)S(1)}, u32[]{:S(2)}, u32[]{:S(2)}) collective-permute-start(f32[128,128]{1,0:T(8,128)S(1)} %shard_map.85), channel_id=1, source_target_pairs={{0,33},{1,32},{2,35},{3,34},{32,65},{33,64},{34,67},{35,66},{64,97... | collective-permute-start | bytes 196616 | tf_op jit(solution)/shard_map/ppermute | solution.py:126
  248.4 13.3 %collective-permute-start.8 = (f32[128,128]{1,0:T(8,128)S(1)}, f32[128,128]{1,0:T(8,128)S(1)}, u32[]{:S(2)}, u32[]{:S(2)}) collective-permute-start(f32[128,128]{1,0:T(8,128)S(1)} %shard_map.86), channel_id=1, source_target_pairs={{0,32},{1,33},{2,34},{3,35},{32,64},{33,65},{34,66},{35,67},{64,96... | collective-permute-start | bytes 196616 | tf_op jit(solution)/shard_map/ppermute | solution.py:126
  268.4 9.4 %collective-permute-start.18 = (f32[128,128]{1,0:T(8,128)S(1)}, f32[128,128]{1,0:T(8,128)S(1)}, u32[]{:S(2)}, u32[]{:S(2)}) collective-permute-start(f32[128,128]{1,0:T(8,128)S(1)} %shard_map.88), channel_id=1, source_target_pairs={{32,3},{33,2},{34,1},{35,0},{64,35},{65,34},{66,33},{67,32},{96,67... | collective-permute-start | bytes 196616 | tf_op jit(solution)/shard_map/ppermute | solution.py:126
  269.7 9.7 %collective-permute-start.15 = (f32[128,128]{1,0:T(8,128)S(1)}, f32[128,128]{1,0:T(8,128)S(1)}, u32[]{:S(2)}, u32[]{:S(2)}) collective-permute-start(f32[128,128]{1,0:T(8,128)S(1)} %shard_map.88), channel_id=1, source_target_pairs={{32,0},{33,1},{34,2},{35,3},{64,32},{65,33},{66,34},{67,35},{96,64... | collective-permute-start | bytes 196616 | tf_op jit(solution)/shard_map/ppermute | solution.py:126
  271.0 9.6 %collective-permute-start.16 = (f32[128,128]{1,0:T(8,128)S(1)}, f32[128,128]{1,0:T(8,128)S(1)}, u32[]{:S(2)}, u32[]{:S(2)}) collective-permute-start(f32[128,128]{1,0:T(8,128)S(1)} %shard_map.88), channel_id=1, source_target_pairs={{32,1},{33,0},{34,3},{35,2},{64,33},{65,32},{66,35},{67,34},{96,65... | collective-permute-start | bytes 196616 | tf_op jit(solution)/shard_map/ppermute | solution.py:126
  286.2 9.5 %collective-permute-start.19 = (f32[128,128]{1,0:T(8,128)S(1)}, f32[128,128]{1,0:T(8,128)S(1)}, u32[]{:S(2)}, u32[]{:S(2)}) collective-permute-start(f32[128,128]{1,0:T(8,128)S(1)} %shard_map.89), channel_id=1, source_target_pairs={{32,0},{33,1},{34,2},{35,3},{64,32},{65,33},{66,34},{67,35},{96,64... | collective-permute-start | bytes 196616 | tf_op jit(solution)/shard_map/ppermute | solution.py:126
  287.5 9.5 %collective-permute-start.20 = (f32[128,128]{1,0:T(8,128)S(1)}, f32[128,128]{1,0:T(8,128)S(1)}, u32[]{:S(2)}, u32[]{:S(2)}) collective-permute-start(f32[128,128]{1,0:T(8,128)S(1)} %shard_map.89), channel_id=1, source_target_pairs={{32,1},{33,0},{34,3},{35,2},{64,33},{65,32},{66,35},{67,34},{96,65... | collective-permute-start | bytes 196616 | tf_op jit(solution)/shard_map/ppermute | solution.py:126
  301.0 9.3 %collective-permute-start.23 = (f32[128,128]{1,0:T(8,128)S(1)}, f32[128,128]{1,0:T(8,128)S(1)}, u32[]{:S(2)}, u32[]{:S(2)}) collective-permute-start(f32[128,128]{1,0:T(8,128)S(1)} %shard_map.90), channel_id=1, source_target_pairs={{32,0},{33,1},{34,2},{35,3},{64,32},{65,33},{66,34},{67,35},{96,64... | collective-permute-start | bytes 196616 | tf_op jit(solution)/shard_map/ppermute | solution.py:126
  314.8 18.1 %all-to-all-start.5 = ((bf16[8,16,3584]{2,1,0:T(8,128)(2,1)}), bf16[8,16,3584]{2,1,0:T(8,128)(2,1)S(1)}, u32[]{:S(2)}, u32[]{:S(2)}) async-start(bf16[8,16,3584]{2,1,0:T(8,128)(2,1)} %bitcast.57), calls=%async_computation.5 | async-start | bytes 1835008 | tf_op jit(solution)/shard_map/all_to_all | solution.py:137
  360.4 104.7 %all-to-all-start.4 = ((bf16[8,128,3584]{2,1,0:T(8,128)(2,1)}), bf16[8,128,3584]{2,1,0:T(8,128)(2,1)}, u32[]{:S(2)}, u32[]{:S(2)}) async-start(bf16[8,128,3584]{2,1,0:T(8,128)(2,1)} %broadcast_in_dim.17), calls=%async_computation.4 | async-start | bytes 14680064 | tf_op jit(solution)/shard_map/all_to_all | solution.py:137
  365.3 62.9 %collective-permute-start.13 = (f32[128,128]{1,0:T(8,128)S(1)}, f32[128,128]{1,0:T(8,128)S(1)}, u32[]{:S(2)}, u32[]{:S(2)}) collective-permute-start(f32[128,128]{1,0:T(8,128)S(1)} %get-tuple-element.11), channel_id=1, source_target_pairs={{0,2},{1,3},{2,0},{3,1},{4,6},{5,7},{6,4},{7,5},{8,10},{9,11},{10,... | collective-permute-start | bytes 196616 | tf_op jit(solution)/shard_map/ppermute | solution.py:131
  367.1 83.6 %collective-permute-start.14 = (f32[128,128]{1,0:T(8,128)S(1)}, f32[128,128]{1,0:T(8,128)S(1)}, u32[]{:S(2)}, u32[]{:S(2)}) collective-permute-start(f32[128,128]{1,0:T(8,128)S(1)} %get-tuple-element.11), channel_id=1, source_target_pairs={{0,3},{1,2},{2,1},{3,0},{4,7},{5,6},{6,5},{7,4},{8,11},{9,10},{10,... | collective-permute-start | bytes 196616 | tf_op jit(solution)/shard_map/ppermute | solution.py:131
  372.3 78.4 %collective-permute-start.12 = (f32[128,128]{1,0:T(8,128)S(1)}, f32[128,128]{1,0:T(8,128)S(1)}, u32[]{:S(2)}, u32[]{:S(2)}) collective-permute-start(f32[128,128]{1,0:T(8,128)S(1)} %get-tuple-element.11), channel_id=1, source_target_pairs={{0,1},{1,0},{2,3},{3,2},{4,5},{5,4},{6,7},{7,6},{8,9},{9,8},{10,11... | collective-permute-start | bytes 196616 | tf_op jit(solution)/shard_map/ppermute | solution.py:131
  372.3 79.0 %collective-permute-start.28 = (f32[128,128]{1,0:T(8,128)S(1)}, f32[128,128]{1,0:T(8,128)S(1)}, u32[]{:S(2)}, u32[]{:S(2)}) collective-permute-start(f32[128,128]{1,0:T(8,128)S(1)} %get-tuple-element.14), channel_id=1, source_target_pairs={{0,2},{1,3},{2,0},{3,1},{4,6},{5,7},{6,4},{7,5},{8,10},{9,11},{10,... | collective-permute-start | bytes 196616 | tf_op jit(solution)/shard_map/ppermute | solution.py:131
  374.0 78.8 %collective-permute-start.29 = (f32[128,128]{1,0:T(8,128)S(1)}, f32[128,128]{1,0:T(8,128)S(1)}, u32[]{:S(2)}, u32[]{:S(2)}) collective-permute-start(f32[128,128]{1,0:T(8,128)S(1)} %get-tuple-element.14), channel_id=1, source_target_pairs={{0,3},{1,2},{2,1},{3,0},{4,7},{5,6},{6,5},{7,4},{8,11},{9,10},{10,... | collective-permute-start | bytes 196616 | tf_op jit(solution)/shard_map/ppermute | solution.py:131
  428.2 24.6 %collective-permute-start.27 = (f32[128,128]{1,0:T(8,128)S(1)}, f32[128,128]{1,0:T(8,128)S(1)}, u32[]{:S(2)}, u32[]{:S(2)}) collective-permute-start(f32[128,128]{1,0:T(8,128)S(1)} %get-tuple-element.14), channel_id=1, source_target_pairs={{0,1},{1,0},{2,3},{3,2},{4,5},{5,4},{6,7},{7,6},{8,9},{9,8},{10,11... | collective-permute-start | bytes 196616 | tf_op jit(solution)/shard_map/ppermute | solution.py:131
  (30 other events, 362.2 us)
Sparse Core Ops, SparseCore 0:
  86.2 136.2 all-reduce.1

commit v2 on v1

v2 whole, which is shorter than its diff:
```python
import jax
import jax.numpy as jnp
from jax import lax
from jax.experimental import pallas as pl
from jax.experimental.pallas import tpu as pltpu
from jax.sharding import PartitionSpec as P

BF = jnp.bfloat16
F32 = jnp.float32
HIGHEST = lax.Precision.HIGHEST
NT = (((1,), (1,)), ((), ()))
CHUNK = 512
X_SIZE = 4
RELATIVE = ((0, 0), (0, 1), (-1, 0), (-1, 1), (1, 0), (1, 1), (2, 0), (2, 1))
PARAMS = pltpu.CompilerParams(vmem_limit_bytes=48 * 1024 * 1024)


def split2(x):
    hi = x.astype(BF)
    return hi, (x - hi.astype(F32)).astype(BF)


def mm(a, b):
    return jnp.dot(a, b, preferred_element_type=F32)


def mm_nt(a, b):
    return lax.dot_general(a, b, NT, preferred_element_type=F32)


def sigma(v):
    return 0.5 * jnp.tanh(0.5 * v) + 0.5


def wide(x):
    return jnp.concatenate(split2(x), axis=1)


def tall(x):
    return jnp.concatenate(split2(x), axis=0)


def twice(x):
    return jnp.concatenate([x, x], axis=0)


def chunks_of(width):
    return [slice(i, i + CHUNK) for i in range(0, width, CHUNK)]


def gram_share(x, gram):
    return 0.25 * jnp.dot(x, gram, precision=HIGHEST, preferred_element_type=F32)


def first_kernel(base_ref, down_ref, part_ref):
    acc = jnp.zeros(part_ref.shape, F32)
    for cols in chunks_of(base_ref.shape[1]):
        pre = base_ref[:, cols]
        hidden = (pre * sigma(pre)).astype(BF)
        acc += mm_nt(hidden, down_ref[:, cols])
    part_ref[...] = acc


def forward_kernel(base_ref, up_ref, down_ref, gram_ref, r0, r1, part_ref):
    c = r0[...] + r1[...]
    cw = wide(c)
    acc = gram_share(c, gram_ref[...])
    for cols in chunks_of(base_ref.shape[1]):
        pre = base_ref[:, cols] + mm(cw, twice(up_ref[:, cols]))
        hidden = (pre * sigma(pre)).astype(BF)
        acc += mm_nt(hidden, down_ref[:, cols])
    part_ref[...] = acc


def middle_kernel(base_ref, up_ref, down_ref, gram_ref, r0, r1, c_ref, part_ref, slope_ref):
    c = r0[...] + r1[...]
    c_ref[...] = c.astype(BF)
    cw = wide(c)
    acc = gram_share(c, gram_ref[...])
    for cols in chunks_of(base_ref.shape[1]):
        pre = base_ref[:, cols] + mm(cw, twice(up_ref[:, cols]))
        sig = sigma(pre)
        hidden = (pre * sig).astype(BF)
        slope_ref[:, cols] = sig * (1.0 + pre * (1.0 - sig))
        acc += mm_nt(hidden, down_ref[:, cols])
    part_ref[...] = acc


def backward_kernel(last_ref, slope_ref, up_ref, down_ref, gram_ref, cot_ref, r0, r1, g_ref, part_ref):
    g = jnp.where(last_ref[0] == 1, cot_ref[...], r0[...] + r1[...])
    g_ref[...] = g
    gw = wide(g)
    acc = gram_share(g, gram_ref[...])
    for cols in chunks_of(slope_ref.shape[1]):
        g_pre = mm(gw, twice(down_ref[:, cols])) * slope_ref[:, cols]
        hi, lo = split2(g_pre)
        acc += mm_nt(hi, up_ref[:, cols]) + mm_nt(lo, up_ref[:, cols])
    part_ref[...] = acc


def call(kernel, outs, *args):
    return pl.pallas_call(kernel, out_shape=outs, compiler_params=PARAMS)(*args)


def proj_kernel(place_ref, basis_ref, w_in_ref, w_out_ref, *refs):
    outs, (basis_t, both) = refs[:-2], refs[-2:]
    rank = basis_ref.shape[1]
    rows = rank // len(RELATIVE)

    @pl.when(pl.program_id(0) == 0)
    def _():
        basis_t[...] = tall(basis_ref[...].T)

    up = mm(basis_t[...], w_in_ref[...])
    down = mm_nt(basis_t[...], w_out_ref[...])
    both[:rank] = up[:rank] + up[rank:]
    both[rank:] = down[:rank] + down[rank:]
    for j, out in enumerate(outs):
        start = pl.multiple_of(place_ref[j] * rows, rows)
        out[:rows] = both[pl.ds(start, rows)].astype(BF)
        out[rows:] = both[pl.ds(rank + start, rows)].astype(BF)


def project(place, basis, w_in, w_out):
    width, rank = basis.shape
    hid = w_in.shape[1]
    rows = 2 * rank // len(RELATIVE)
    count = len(RELATIVE)
    return pl.pallas_call(
        proj_kernel,
        out_shape=[jax.ShapeDtypeStruct((rows, hid), BF)] * count,
        grid_spec=pltpu.PrefetchScalarGridSpec(
            num_scalar_prefetch=1,
            grid=(hid // CHUNK,),
            in_specs=[
                pl.BlockSpec((width, rank), lambda i, p: (0, 0)),
                pl.BlockSpec((width, CHUNK), lambda i, p: (0, i)),
                pl.BlockSpec((CHUNK, width), lambda i, p: (i, 0)),
            ],
            out_specs=[pl.BlockSpec((rows, CHUNK), lambda i, p: (0, i))] * count,
            scratch_shapes=[pltpu.VMEM((2 * rank, width), BF), pltpu.VMEM((2 * rank, CHUNK), F32)],
        ),
        compiler_params=PARAMS,
    )(place, basis, w_in, w_out)


def base_specs(base, dp):
    micro, tokens, width = base.shape
    return [
        pl.BlockSpec((micro, tokens // dp, width), lambda i, p, j=j: (0, p[j], 0))
        for j in range(len(RELATIVE))
    ]


def product_kernel(place_ref, *refs):
    count = len(RELATIVE)
    bases, w_ref, outs = refs[:count], refs[count], refs[count + 1 :]
    own = bases[0].shape[0] * bases[0].shape[1]
    for j in range(0, count, 2):
        rows = jnp.concatenate([b[...].reshape(own, b.shape[2]) for b in bases[j : j + 2]], axis=0)
        res = mm(rows, w_ref[...]).astype(BF)
        outs[j][...] = res[:own]
        outs[j + 1][...] = res[own:]


def product(place, base, w_in, dp):
    micro, tokens, width = base.shape
    hid = w_in.shape[1]
    own = micro * tokens // dp
    count = len(RELATIVE)
    return pl.pallas_call(
        product_kernel,
        out_shape=[jax.ShapeDtypeStruct((own, hid), BF)] * count,
        grid_spec=pltpu.PrefetchScalarGridSpec(
            num_scalar_prefetch=1,
            grid=(hid // CHUNK,),
            in_specs=base_specs(base, dp) + [pl.BlockSpec((width, CHUNK), lambda i, p: (0, i))],
            out_specs=[pl.BlockSpec((own, CHUNK), lambda i, p: (0, i))] * count,
        ),
        compiler_params=PARAMS,
    )(place, *([base] * count), w_in)


def assemble_kernel(place_ref, *refs):
    pieces, (up_ref, down_ref) = refs[:-2], refs[-2:]
    rows = up_ref.shape[1]
    flat = jnp.concatenate([p[...] for p in pieces], axis=0)
    for j in range(len(RELATIVE)):
        up_ref[place_ref[j]] = flat[2 * j * rows : (2 * j + 1) * rows]
        down_ref[place_ref[j]] = flat[(2 * j + 1) * rows : (2 * j + 2) * rows]


def assemble(place, pieces, rank, hid):
    count = len(RELATIVE)
    shape = (count, rank // count, hid)
    up, down = pl.pallas_call(
        assemble_kernel,
        out_shape=[jax.ShapeDtypeStruct(shape, BF)] * 2,
        grid_spec=pltpu.PrefetchScalarGridSpec(
            num_scalar_prefetch=1,
            grid=(hid // CHUNK,),
            in_specs=[pl.BlockSpec((p.shape[0], CHUNK), lambda i, p: (0, i)) for p in pieces],
            out_specs=[pl.BlockSpec((count, rank // count, CHUNK), lambda i, p: (0, 0, i))] * 2,
        ),
        compiler_params=PARAMS,
    )(place, *pieces)
    return up.reshape(rank, hid), down.reshape(rank, hid)


def prepare_kernel(place_ref, *refs):
    count = len(RELATIVE)
    bases, refs = refs[:count], refs[count:]
    basis_ref, c_refs, up_ref, pieces = refs[0], refs[1:5], refs[5], refs[6:-3]
    xt_ref, hidden_ref, slope_ref = refs[-3:]
    own = bases[0].shape[0] * bases[0].shape[1]

    @pl.when(pl.program_id(0) == 0)
    def _():
        basis = basis_ref[...].astype(BF)
        for j, b in enumerate(bases):
            c = c_refs[j // 2][(j % 2) * own : (j % 2 + 1) * own]
            x = b[...].reshape(own, b.shape[2]).astype(F32) + mm_nt(c, basis)
            xt_ref[:, j * own : (j + 1) * own] = x.T.astype(BF)

    up = up_ref[...]
    base_pre = jnp.concatenate([p[...] for p in pieces], axis=0)
    for j in range(count):
        rows = slice(j * own, (j + 1) * own)
        c = c_refs[j // 2][(j % 2) * own : (j % 2 + 1) * own]
        pre = base_pre[rows].astype(F32) + mm(c, up)
        sig = sigma(pre)
        hidden_ref[rows] = (pre * sig).astype(BF)
        slope_ref[rows] = (sig * (1.0 + pre * (1.0 - sig))).astype(BF)


def prepare(place, base, dp, basis, c_pieces, up, pieces):
    micro, tokens, width = base.shape
    hid = up.shape[1]
    every = micro * tokens
    whole = lambda a: pl.BlockSpec(a.shape, lambda i, p: (0, 0))
    column = lambda rows: pl.BlockSpec((rows, CHUNK), lambda i, p: (0, i))
    return pl.pallas_call(
        prepare_kernel,
        out_shape=[
            jax.ShapeDtypeStruct((width, every), BF),
            jax.ShapeDtypeStruct((every, hid), BF),
            jax.ShapeDtypeStruct((every, hid), BF),
        ],
        grid_spec=pltpu.PrefetchScalarGridSpec(
            num_scalar_prefetch=1,
            grid=(hid // CHUNK,),
            in_specs=base_specs(base, dp)
            + [whole(basis)]
            + [whole(c) for c in c_pieces]
            + [column(up.shape[0])]
            + [column(p.shape[0]) for p in pieces],
            out_specs=[
                pl.BlockSpec((width, every), lambda i, p: (0, 0)),
                column(every),
                column(every),
            ],
        ),
        compiler_params=PARAMS,
    )(place, *([base] * len(RELATIVE)), basis, *c_pieces, up, *pieces)


def finish_kernel(place_ref, g_ref, down_ref, xt_ref, hidden_ref, slope_ref, grad_ref, dc_ref, gw, gt):
    rank = down_ref.shape[0]
    own = g_ref.shape[1]

    @pl.when(pl.program_id(0) == 0)
    def _():
        for j in range(len(RELATIVE)):
            g = g_ref[place_ref[j]]
            gw[j * own : (j + 1) * own] = wide(g)
            gt[:, j * own : (j + 1) * own] = tall(g.T)

    g_pre = mm(gw[...], twice(down_ref[...])) * slope_ref[...].astype(F32)
    grad_ref[...] = mm(xt_ref[...], g_pre.astype(BF)).astype(BF)
    dc = mm(gt[...], hidden_ref[...])
    dc_ref[...] = (dc[:rank] + dc[rank:]).T


def finish(place, g_all, down, xt, hidden, slope):
    rank, hid = down.shape
    width, every = xt.shape
    column = lambda rows: pl.BlockSpec((rows, CHUNK), lambda i, p: (0, i))
    return pl.pallas_call(
        finish_kernel,
        out_shape=[jax.ShapeDtypeStruct((width, hid), BF), jax.ShapeDtypeStruct((hid, rank), F32)],
        grid_spec=pltpu.PrefetchScalarGridSpec(
            num_scalar_prefetch=1,
            grid=(hid // CHUNK,),
            in_specs=[
                pl.BlockSpec(g_all.shape, lambda i, p: (0, 0, 0)),
                column(rank),
                pl.BlockSpec(xt.shape, lambda i, p: (0, 0)),
                column(every),
                column(every),
            ],
            out_specs=[column(width), pl.BlockSpec((CHUNK, rank), lambda i, p: (i, 0))],
            scratch_shapes=[pltpu.VMEM((every, 2 * rank), BF), pltpu.VMEM((2 * rank, every), BF)],
        ),
        compiler_params=PARAMS,
    )(place, g_all, down, xt, hidden, slope)


def to_dp(x, dx, dy):
    size = lax.axis_size("dp")
    pairs = [(i, ((i // 2 + dx) % X_SIZE) * 2 + ((i % 2) ^ dy)) for i in range(size)]
    return lax.ppermute(x, "dp", pairs)


def to_tensor(x, k):
    size = lax.axis_size("tensor")
    return lax.ppermute(x, "tensor", [(t, t ^ k) for t in range(size)])


def hop(part, by):
    sections, tensors = lax.axis_size("section"), lax.axis_size("tensor")
    pair_sum = part + to_tensor(part, 1)
    pairs = [
        (s * tensors + t, (s + by) * tensors + (t ^ (2 * (t % 2))))
        for s in range(sections)
        for t in range(tensors)
        if 0 <= s + by < sections
    ]
    got = lax.ppermute(pair_sum, ("section", "tensor"), pairs)
    return got, to_tensor(got, 1)


def cat(*xs):
    return jnp.concatenate(xs, axis=0)


def plus(x, *ys):
    total = x.astype(F32)
    for start, y in ys:
        pads = ((start, x.shape[0] - start - y.shape[0]), (0, 0))
        total = total + jnp.pad(y.astype(F32), pads)
    return total.astype(x.dtype)


def reduce_blocks(blocks):
    b = dict(zip(RELATIVE, blocks))
    n = blocks[0].shape[0]
    h, q = n // 2, n // 4
    far = b[2, 1]
    u0, u1, v = to_dp(far[:q], 1, 0), to_dp(far[q:h], -1, 0), to_dp(far[h:], 0, 1)
    up = to_dp(cat(b[2, 0][:h], plus(b[1, 1][:h], (0, u0))), 1, 0)
    down = to_dp(cat(plus(b[2, 0][h:], (0, v)), plus(b[-1, 1][:h], (q, u1))), -1, 0)
    side = to_dp(cat(b[1, 1][h:], b[-1, 1][h:]), 0, 1)
    e1 = to_dp(plus(b[1, 0], (0, up[:h]), (h, side[:h])), 1, 0)
    e2 = to_dp(plus(b[-1, 0], (h, down[:h]), (h, side[h:])), -1, 0)
    e3 = to_dp(plus(b[0, 1], (0, up[h:]), (0, down[h:])), 0, 1)
    f = lambda a: a.astype(F32)
    return (f(b[0, 0]) + f(e1)) + (f(e2) + f(e3))


def gather_1(g):
    return to_dp(g, 1, 0), to_dp(g, -1, 0), to_dp(g, 0, 1)


def gather_2(got):
    left, right, side = got
    h = left.shape[0] // 2
    return (
        to_dp(cat(side[:h], left[:h]), 1, 0),
        to_dp(cat(side[:h], right[h:]), -1, 0),
        to_dp(cat(left[h:], right[h:]), 0, 1),
    )


def gather_3(got):
    left, right, side = got
    h = left.shape[0] // 2
    q = h // 2
    return to_dp(left[:q], 1, 0), to_dp(right[q:h], -1, 0), to_dp(right[h:], 0, 1)


def gathered(g, s1, s2, s3):
    (left, right, side), (am_t0, ap_t1, bm_bp), (u0, u1, v) = s1, s2, s3
    h = g.shape[0] // 2
    return [
        g, side, left, am_t0[:h], bm_bp[:h], right, ap_t1[:h], bm_bp[h:],
        am_t0[h:], ap_t1[h:], u0, u1, v,
    ]


def tie(*xs):
    return lax.optimization_barrier(xs)


def on_device(base, w_in, w_out, basis, cotangent):
    dp = lax.axis_size("dp")
    sections = lax.axis_size("section")
    last = (lax.axis_index("section") == sections - 1).astype(jnp.int32).reshape(1)
    d = lax.axis_index("dp")
    place = jnp.stack(
        [((d // 2 + dx) % X_SIZE) * 2 + (d % 2 + dy) % 2 for dx, dy in RELATIVE]
    ).astype(jnp.int32)
    micro, tokens, width = base.shape
    rows = tokens // dp
    own = micro * rows
    rank = basis.shape[1]
    w_in, w_out = w_in[0], w_out[0]
    hid = w_in.shape[1]
    tok = jax.ShapeDtypeStruct((own, rank), F32)

    gram = lax.psum(
        lax.dot_general(basis, basis, (((0,), (0,)), ((), ())), precision=HIGHEST), "dp"
    )
    proj = reduce_blocks(project(place, basis, w_in, w_out)).astype(BF)
    base_pre = reduce_blocks(product(place, base, w_in, dp))
    p1 = gather_1(proj)
    p2 = gather_2(p1)
    p3 = gather_3(p2)
    up, down = assemble(place, gathered(proj, p1, p2, p3), rank, hid)

    base_half = base_pre.astype(BF)
    s1 = gather_1(base_half)
    part = call(first_kernel, tok, base_pre, down)
    got = hop(part, 1)
    part = call(forward_kernel, tok, base_pre, up, down, gram, *got)
    got = hop(part, 1)
    got, s1 = tie(got, s1)
    s2 = gather_2(s1)
    part = call(forward_kernel, tok, base_pre, up, down, gram, *got)
    got = hop(part, 1)
    c_in, coef_part, slope = call(
        middle_kernel,
        (jax.ShapeDtypeStruct((own, rank), BF), tok, jax.ShapeDtypeStruct((own, hid), F32)),
        base_pre, up, down, gram, *got,
    )

    def back(got):
        return call(backward_kernel, (tok, tok), last_ref, slope, up, down, gram, cot, *got)

    last_ref = last
    cot = cotangent.reshape(own, rank)
    c_pair = cat(c_in, to_dp(c_in, 0, 1))
    _, part = back((cot, cot))
    got = hop(part, -1)
    got, s2, c_pair = tie(got, s2, c_pair)
    s3 = gather_3(s2)
    c_far = [to_dp(c_pair, dx, 0) for dx in (1, -1, 2)]
    _, part = back(got)
    got = hop(part, -1)
    got, s3, c_far = tie(got, s3, c_far)
    xt, hidden_all, slope_all = prepare(
        place, base, dp, basis, [c_pair, *c_far], up, gathered(base_half, s1, s2, s3)
    )
    _, part = back(got)
    got = hop(part, -1)
    g_out, grad_part = back(got)
    g_all = lax.all_to_all(jnp.broadcast_to(g_out[None], (dp, own, rank)), "dp", 0, 0, tiled=True)
    grad_up, down_coefs = finish(place, g_all, down, xt, hidden_all, slope_all)
    parts = cat(coef_part, grad_part)
    parts = parts + to_tensor(parts, 1)
    parts = (parts + to_tensor(parts, 2)).reshape(2, 1, micro, rows, rank)
    return parts[0], parts[1], grad_up[None], down_coefs[None]


def solution(mesh):
    return jax.shard_map(
        on_device,
        mesh=mesh,
        in_specs=(
            P(None, None, "dp"),
            P("section", "dp", "tensor"),
            P("section", "tensor", "dp"),
            P("dp", None),
            P(None, "dp", None),
        ),
        out_specs=(
            P("section", None, "dp", None),
            P("section", None, "dp", None),
            P("section", "dp", "tensor"),
            P("section", "tensor", None),
        ),
        check_vma=False,
    )
```

time: 493 us -> 368 us (0.75); the launches traced: 487 us -> 367 us
  waiting for transfers between devices: 237 us -> 172 us
  Pallas kernels: 8.86 us -> 66.1 us
  blocking collectives: 42.4 us -> 0 us
  matrix products: 37.2 us -> 1.64 us
  starting transfers between devices: 117 us -> 86.7 us
    all_to_all x5 -> x1, waiting for transfers between devices: 137 us -> 0.01 us  [on_device(): lax.all_to_all(jnp.broadcast_to(g_out[None], (dp, own, rank)), 'dp', 0, 0...]
    pallas_call x8 -> x13, Pallas kernels: 8.86 us -> 66.1 us  [the longest x1 16.6 us: finish(): pl.pallas_call(finish_kernel, out_shape=[jax.ShapeDtypeStruct((width, hid...]
    psum x1, waiting for transfers between devices: 16.2 us -> 66 us  [on_device(): lax.psum(lax.dot_general(basis, basis, (((0,), (0,)), ((), ())), precisio...]
    all_to_all x2 -> x0, blocking collectives: 42.4 us -> none  [swap(): return lax.all_to_all(x, 'dp', 0, 0, tiled=True)]
    dot_general x4 -> x0, matrix products: 35.6 us -> none  [the longest x1 15.3 us: on_device(): lax.dot_general(inputs, g_all, (((0,), (0,)), ((), ())), preferred_elemen...]
    ppermute x30 -> x60, waiting for transfers between devices: 83.9 us -> 106 us  [the longest x40 65.7 us: to_dp(): return lax.ppermute(x, 'dp', pairs)]
    all_to_all x5 -> x1, starting transfers between devices: 20.5 us -> 4.88 us  [on_device(): lax.all_to_all(jnp.broadcast_to(g_out[None], (dp, own, rank)), 'dp', 0, 0...]
    ppermute x30 -> x60, starting transfers between devices: 97 us -> 81.8 us  [the longest x40 41.7 us: to_dp(): return lax.ppermute(x, 'dp', pairs)]
  transfers between devices with their start and end apart: 36 -> 62, of which waited for: 23 -> 31; matrix products, arithmetic and copies ran while one was open for 5% -> 3% of each run, Pallas kernels for 0% -> 10%
where the time goes in v2:
time: 368 us; the launch traced here: 367 us
  waiting for transfers between devices  172 us (47%)
  starting transfers between devices  86.7 us (24%)
  Pallas kernels  66.1 us (18%)
  local copies, waits for them, and re-layouts  20.6 us (6%)
  between operations  14.9 us (4%)
  other arithmetic  4.91 us (1%)
    psum x1, waiting for transfers between devices, on_device(): lax.psum(lax.dot_general(basis, basis, (((0,), (0,)), ((), ())), precisio...  66 us
    ppermute x40, waiting for transfers between devices, to_dp(): return lax.ppermute(x, 'dp', pairs)  65.7 us
    ppermute x40, starting transfers between devices, to_dp(): return lax.ppermute(x, 'dp', pairs)  41.7 us
    ppermute x6, waiting for transfers between devices, hop(): got = lax.ppermute(pair_sum, ('section', 'tensor'), pairs)  30.2 us
    ppermute x6, starting transfers between devices, hop(): got = lax.ppermute(pair_sum, ('section', 'tensor'), pairs)  21.3 us
    ppermute x14, starting transfers between devices, to_tensor(): return lax.ppermute(x, 'tensor', [(t, t ^ k) for t in range(size)])  18.7 us
    pallas_call x1, Pallas kernels, finish(): pl.pallas_call(finish_kernel, out_shape=[jax.ShapeDtypeStruct((width, hid...  16.6 us
    pallas_call x1, Pallas kernels, prepare(): pl.pallas_call(prepare_kernel, out_shape=[jax.ShapeDtypeStruct((width, ev...  14.4 us
  transfers between devices with their start and end apart: 62, of which 31 were waited for; matrix products, arithmetic and copies ran while one was open for 3% of the time, Pallas kernels for 10%

profile of v2, /device:TPU:1, one launch (start us, length us, event | category | flops | bytes accessed | tf_op | source)
XLA Modules:
  0.0 367.2 jit_solution(16076977871009581756)
XLA Ops:
  8.4 10.2 %shard_map.85 = (bf16[32,3584]{1,0:T(8,128)(2,1)S(1)}, bf16[32,3584]{1,0:T(8,128)(2,1)S(1)}, bf16[32,3584]{1,0:T(8,128)(2,1)S(1)}, bf16[32,3584]{1,0:T(8,128)(2,...) custom-call(s32[8]{0:T(128)S(1)} %stack.35.place_ref, ...), custom_call_target="tpu_custom_call" | custom-call | tf_op jit(solution)/shard_map/pallas_call | solution.py:129
  23.8 13.0 %shard_map.84 = (bf16[128,3584]{1,0:T(8,128)(2,1)S(1)}, bf16[128,3584]{1,0:T(8,128)(2,1)S(1)}, bf16[128,3584]{1,0:T(8,128)(2,1)S(1)}, bf16[128,3584]{1,0:T(8,128...) custom-call(s32[8]{0:T(128)S(1)} %stack.35.place_ref, ...), custom_call_target="tpu_custom_call" | custom-call | tf_op jit(solution)/shard_map/pallas_call | solution.py:171
  45.2 3.1 collective-permute-start.15
  51.4 3.2 collective-permute-start.16
  56.2 20.0 %collective-permute-done.12 = bf16[32,3584]{1,0:T(8,128)(2,1)S(1)} collective-permute-done((bf16[32,3584]{1,0:T(8,128)(2,1)S(1)}, bf16[32,3584]{1,0:T(8,128)(2,1)S(1)}, u32[]{:S(2)}, u32[]{:S(2)}) %collective-permute-start.12) | collective-permute-done | bytes 229408 | tf_op jit(solution)/shard_map/ppermute | solution.py:311
  76.8 2.7 collective-permute-start.6
  79.6 3.2 collective-permute-done.19.refs_2_
  84.3 16.2 %collective-permute-done.21.refs_5_ = bf16[32,3584]{1,0:T(8,128)(2,1)S(1)} collective-permute-done((bf16[32,3584]{1,0:T(8,128)(2,1)S(1)}, bf16[32,3584]{1,0:T(8,128)(2,1)S(1)}, u32[]{:S(2)}, u32[]{:S(2)}) %collective-permute-start.21) | collective-permute-done | bytes 229408 | tf_op jit(solution)/shard_map/ppermute | solution.py:311
  100.6 3.5 collective-permute-start.23
  106.8 2.9 collective-permute-start.7
  111.8 16.7 %collective-permute-done.3 = bf16[128,3584]{1,0:T(8,128)(2,1)S(1)} collective-permute-done((bf16[128,3584]{1,0:T(8,128)(2,1)S(1)}, bf16[128,3584]{1,0:T(8,128)(2,1)S(1)}, u32[]{:S(2)}, u32[]{:S(2)}) %collective-permute-start.3) | collective-permute-done | bytes 917536 | tf_op jit(solution)/shard_map/ppermute | solution.py:311
  135.7 8.0 %collective-permute-start.27 = (f32[128,128]{1,0:T(8,128)S(1)}, f32[128,128]{1,0:T(8,128)S(1)}, u32[]{:S(2)}, u32[]{:S(2)}) collective-permute-start(f32[128,128]{1,0:T(8,128)S(1)} %shard_map.87), channel_id=1, source_target_pairs={{0,1},{1,0},{2,3},{3,2},{4,5},{5,4},{6,7},{7,6},{8,9},{9,8},{10,11... | collective-permute-start | bytes 196616 | tf_op jit(solution)/shard_map/ppermute | solution.py:316
  144.6 6.0 %collective-permute-start.28 = (f32[128,128]{1,0:T(8,128)S(1)}, f32[128,128]{1,0:T(8,128)S(1)}, u32[]{:S(2)}, u32[]{:S(2)}) collective-permute-start(f32[128,128]{1,0:T(8,128)S(1)} %add.251), channel_id=1, source_target_pairs={{0,32},{1,35},{2,34},{3,33},{32,64},{33,67},{34,66},{35,65},{64,96... | collective-permute-start | bytes 196616 | tf_op jit(solution)/shard_map/ppermute | solution.py:328
  152.5 66.0 %all-reduce.16.cloned.1.call-done.gram_ref = f32[128,128]{1,0:T(8,128)} async-done(((f32[128,128]{1,0:T(8,128)}), f32[128,128]{1,0:T(8,128)}) %all-reduce.16.cloned.1.call-update) | async-done | bytes 65552 | tf_op jit(solution)/shard_map/psum | solution.py:410
  221.6 5.9 %collective-permute-start.30 = (f32[128,128]{1,0:T(8,128)S(1)}, f32[128,128]{1,0:T(8,128)S(1)}, u32[]{:S(2)}, u32[]{:S(2)}) collective-permute-start(f32[128,128]{1,0:T(8,128)S(1)} %shard_map.88), channel_id=1, source_target_pairs={{0,1},{1,0},{2,3},{3,2},{4,5},{5,4},{6,7},{7,6},{8,9},{9,8},{10,11... | collective-permute-start | bytes 196616 | tf_op jit(solution)/shard_map/ppermute | solution.py:316
  228.4 5.3 %collective-permute-start.31 = (f32[128,128]{1,0:T(8,128)S(1)}, f32[128,128]{1,0:T(8,128)S(1)}, u32[]{:S(2)}, u32[]{:S(2)}) collective-permute-start(f32[128,128]{1,0:T(8,128)S(1)} %add.252), channel_id=1, source_target_pairs={{0,32},{1,35},{2,34},{3,33},{32,64},{33,67},{34,66},{35,65},{64,96... | collective-permute-start | bytes 196616 | tf_op jit(solution)/shard_map/ppermute | solution.py:328
  245.4 6.1 %collective-permute-start.37 = (f32[128,128]{1,0:T(8,128)S(1)}, f32[128,128]{1,0:T(8,128)S(1)}, u32[]{:S(2)}, u32[]{:S(2)}) collective-permute-start(f32[128,128]{1,0:T(8,128)S(1)} %add.253), channel_id=1, source_target_pairs={{0,32},{1,35},{2,34},{3,33},{32,64},{33,67},{34,66},{35,65},{64,96... | collective-permute-start | bytes 196616 | tf_op jit(solution)/shard_map/ppermute | solution.py:328
  251.5 10.9 %collective-permute-done.37.r0 = f32[128,128]{1,0:T(8,128)S(1)} collective-permute-done((f32[128,128]{1,0:T(8,128)S(1)}, f32[128,128]{1,0:T(8,128)S(1)}, u32[]{:S(2)}, u32[]{:S(2)}) %collective-permute-start.37) | collective-permute-done | bytes 65568 | tf_op jit(solution)/shard_map/ppermute | solution.py:328
  272.5 4.9 %collective-permute-done.40.r0 = f32[128,128]{1,0:T(8,128)S(1)} collective-permute-done((f32[128,128]{1,0:T(8,128)S(1)}, f32[128,128]{1,0:T(8,128)S(1)}, u32[]{:S(2)}, u32[]{:S(2)}) %collective-permute-start.40) | collective-permute-done | bytes 65568 | tf_op jit(solution)/shard_map/ppermute | solution.py:328
  294.4 6.6 %collective-permute-done.47.r0 = f32[128,128]{1,0:T(8,128)S(1)} collective-permute-done((f32[128,128]{1,0:T(8,128)S(1)}, f32[128,128]{1,0:T(8,128)S(1)}, u32[]{:S(2)}, u32[]{:S(2)}) %collective-permute-start.47) | collective-permute-done | bytes 65568 | tf_op jit(solution)/shard_map/ppermute | solution.py:328
  307.4 6.1 %collective-permute-done.56.r0 = f32[128,128]{1,0:T(8,128)S(1)} collective-permute-done((f32[128,128]{1,0:T(8,128)S(1)}, f32[128,128]{1,0:T(8,128)S(1)}, u32[]{:S(2)}, u32[]{:S(2)}) %collective-permute-start.56) | collective-permute-done | bytes 65568 | tf_op jit(solution)/shard_map/ppermute | solution.py:328
  317.9 4.9 %all-to-all-start = ((f32[8,128,128]{2,1,0:T(8,128)}), f32[8,128,128]{2,1,0:T(8,128)S(1)}, u32[]{:S(2)}, u32[]{:S(2)}) async-start(f32[8,128,128]{2,1,0:T(8,128)} %broadcast_in_dim.12), calls=%async_computation | async-start | bytes 1048576 | tf_op jit(solution)/shard_map/all_to_all | solution.py:456
  327.0 14.4 %shard_map.95 = (bf16[1024,1024]{1,0:T(8,128)(2,1)}, bf16[1024,3584]{1,0:T(8,128)(2,1)}, bf16[1024,3584]{1,0:T(8,128)(2,1)}) custom-call(s32[8]{0:T(128)S(1)} %stack.35.place_ref, bf16[4,256,1024]{2,1,0:T(8,128)(2,1)} %refs_7_.3, bf16[4,256,1024]{2,1,0:T(8,128)(2,1)} %refs_7_.3, bf16[4,256,1024]{2,1,0:T(8,128)(2,1)} %refs_7_.3, ...), custom_call_target="tpu_custom_call" | custom-call | tf_op jit(solution)/shard_map/pallas_call | solution.py:242
  343.8 16.6 %shard_map.96 = (bf16[1024,3584]{1,0:T(8,128)(2,1)}, f32[3584,128]{1,0:T(8,128)}) custom-call(s32[8]{0:T(128)S(1)} %stack.35.place_ref, f32[8,128,128]{2,1,0:T(8,128)S(1)} %all-to-all-done.g_ref, bf16[128,3584]{1,0:T(8,128)(2,1)S(1)} %bitcast.28, bf16[1024,1024]{1,0:T(8,128)(2,1)S(1)} %copy-done.8, bf16[1024,3584]{1,0:T(8,128)(2,1)} %get-tuple-element.100.hidden_ref, ...), custom_call_target="tpu_custom_call" | custom-call | tf_op jit(solution)/shard_map/pallas_call | solution.py:288
  (233 shorter events, 95.8 us)
Async XLA Ops:
  7.2 211.3 %all-reduce.16.cloned.1.call-start = ((), (), s32[]{:S(2)}) async-start(), calls=%async_computation.1 | async-start | bytes 131072 | tf_op jit(solution)/shard_map/psum | solution.py:410
  20.8 21.5 %collective-permute-start.14 = (bf16[8,3584]{1,0:T(8,128)(2,1)S(1)}, bf16[8,3584]{1,0:T(8,128)(2,1)S(1)}, u32[]{:S(2)}, u32[]{:S(2)}) collective-permute-start(bf16[8,3584]{1,0:T(8,128)(2,1)S(1)} %get-tuple-element.136), channel_id=1, source_target_pairs={{0,24},{4,28},{8,0},{12,4},{16,8},{20,12},{24,16},{28,20},{1,25},{... | collective-permute-start | bytes 172040 | tf_op jit(solution)/shard_map/ppermute | solution.py:311
  22.2 21.6 %collective-permute-start.13 = (bf16[16,3584]{1,0:T(8,128)(2,1)S(1)}, bf16[16,3584]{1,0:T(8,128)(2,1)S(1)}, u32[]{:S(2)}, u32[]{:S(2)}) collective-permute-start(bf16[16,3584]{1,0:T(8,128)(2,1)S(1)} %slice.195), channel_id=1, source_target_pairs={{0,4},{4,0},{8,12},{12,8},{16,20},{20,16},{24,28},{28,24},{1,5},{5... | collective-permute-start | bytes 344072 | tf_op jit(solution)/shard_map/ppermute | solution.py:311
  23.7 24.7 %collective-permute-start.11 = (bf16[32,3584]{1,0:T(8,128)(2,1)S(1)}, bf16[32,3584]{1,0:T(8,128)(2,1)S(1)}, u32[]{:S(2)}, u32[]{:S(2)}) collective-permute-start(bf16[32,3584]{1,0:T(8,128)(2,1)S(1)} %pad_maximum_fusion.10), channel_id=1, source_target_pairs={{0,4},{4,0},{8,12},{12,8},{16,20},{20,16},{24,28},{28,24},{1,5},{5... | collective-permute-start | bytes 688136 | tf_op jit(solution)/shard_map/ppermute | solution.py:311
  43.8 61.8 %collective-permute-start.2 = (bf16[128,3584]{1,0:T(8,128)(2,1)S(1)}, bf16[128,3584]{1,0:T(8,128)(2,1)S(1)}, u32[]{:S(2)}, u32[]{:S(2)}) collective-permute-start(bf16[128,3584]{1,0:T(8,128)(2,1)S(1)} %pad_maximum_fusion.4), channel_id=1, source_target_pairs={{0,4},{4,0},{8,12},{12,8},{16,20},{20,16},{24,28},{28,24},{1,5},{5... | collective-permute-start | bytes 2752520 | tf_op jit(solution)/shard_map/ppermute | solution.py:311
  48.4 57.2 %collective-permute-start.1 = (bf16[128,3584]{1,0:T(8,128)(2,1)S(1)}, bf16[128,3584]{1,0:T(8,128)(2,1)S(1)}, u32[]{:S(2)}, u32[]{:S(2)}) collective-permute-start(bf16[128,3584]{1,0:T(8,128)(2,1)S(1)} %pad_maximum_fusion.3), channel_id=1, source_target_pairs={{0,8},{4,12},{8,16},{12,20},{16,24},{20,28},{24,0},{28,4},{1,9},{5... | collective-permute-start | bytes 2752520 | tf_op jit(solution)/shard_map/ppermute | solution.py:311
  50.7 25.5 %collective-permute-start.12 = (bf16[32,3584]{1,0:T(8,128)(2,1)S(1)}, bf16[32,3584]{1,0:T(8,128)(2,1)S(1)}, u32[]{:S(2)}, u32[]{:S(2)}) collective-permute-start(bf16[32,3584]{1,0:T(8,128)(2,1)S(1)} %add_convert_fusion.9), channel_id=1, source_target_pairs={{0,8},{4,12},{8,16},{12,20},{16,24},{20,28},{24,0},{28,4},{1,9},{5... | collective-permute-start | bytes 688136 | tf_op jit(solution)/shard_map/ppermute | solution.py:311
  51.4 24.8 %collective-permute-start.16 = (bf16[32,3584]{1,0:T(8,128)(2,1)S(1)}, bf16[32,3584]{1,0:T(8,128)(2,1)S(1)}, u32[]{:S(2)}, u32[]{:S(2)}) collective-permute-start(bf16[32,3584]{1,0:T(8,128)(2,1)S(1)} %add_convert_fusion.8), channel_id=1, source_target_pairs={{0,24},{4,28},{8,0},{12,4},{16,8},{20,12},{24,16},{28,20},{1,25},{... | collective-permute-start | bytes 688136 | tf_op jit(solution)/shard_map/ppermute | solution.py:311
  54.6 21.9 %collective-permute-start.17 = (bf16[32,3584]{1,0:T(8,128)(2,1)S(1)}, bf16[32,3584]{1,0:T(8,128)(2,1)S(1)}, u32[]{:S(2)}, u32[]{:S(2)}) collective-permute-start(bf16[32,3584]{1,0:T(8,128)(2,1)S(1)} %add_convert_fusion.7), channel_id=1, source_target_pairs={{0,4},{4,0},{8,12},{12,8},{16,20},{20,16},{24,28},{28,24},{1,5},{5... | collective-permute-start | bytes 688136 | tf_op jit(solution)/shard_map/ppermute | solution.py:311
  76.8 29.8 %collective-permute-start.6 = (bf16[128,3584]{1,0:T(8,128)(2,1)S(1)}, bf16[128,3584]{1,0:T(8,128)(2,1)S(1)}, u32[]{:S(2)}, u32[]{:S(2)}) collective-permute-start(bf16[128,3584]{1,0:T(8,128)(2,1)S(1)} %pad_maximum_fusion.5), channel_id=1, source_target_pairs={{0,24},{4,28},{8,0},{12,4},{16,8},{20,12},{24,16},{28,20},{1,25},{... | collective-permute-start | bytes 2752520 | tf_op jit(solution)/shard_map/ppermute | solution.py:311
  79.5 21.0 %collective-permute-start.21 = (bf16[32,3584]{1,0:T(8,128)(2,1)S(1)}, bf16[32,3584]{1,0:T(8,128)(2,1)S(1)}, u32[]{:S(2)}, u32[]{:S(2)}) collective-permute-start(bf16[32,3584]{1,0:T(8,128)(2,1)S(1)} %add_convert_fusion.6.refs_0_), channel_id=1, source_target_pairs={{0,24},{4,28},{8,0},{12,4},{16,8},{20,12},{24,16},{28,20},{1,25},{... | collective-permute-start | bytes 688136 | tf_op jit(solution)/shard_map/ppermute | solution.py:311
  104.1 27.0 %collective-permute-start.22 = (bf16[32,3584]{1,0:T(8,128)(2,1)S(1)}, bf16[32,3584]{1,0:T(8,128)(2,1)S(1)}, u32[]{:S(2)}, u32[]{:S(2)}) collective-permute-start(bf16[32,3584]{1,0:T(8,128)(2,1)S(1)} %get-tuple-element.140), channel_id=1, source_target_pairs={{0,4},{4,0},{8,12},{12,8},{16,20},{20,16},{24,28},{28,24},{1,5},{5... | collective-permute-start | bytes 688136 | tf_op jit(solution)/shard_map/ppermute | solution.py:311
  106.1 22.4 %collective-permute-start.3 = (bf16[128,3584]{1,0:T(8,128)(2,1)S(1)}, bf16[128,3584]{1,0:T(8,128)(2,1)S(1)}, u32[]{:S(2)}, u32[]{:S(2)}) collective-permute-start(bf16[128,3584]{1,0:T(8,128)(2,1)S(1)} %add_convert_fusion.2), channel_id=1, source_target_pairs={{0,8},{4,12},{8,16},{12,20},{16,24},{20,28},{24,0},{28,4},{1,9},{5... | collective-permute-start | bytes 2752520 | tf_op jit(solution)/shard_map/ppermute | solution.py:311
  106.8 21.7 %collective-permute-start.7 = (bf16[128,3584]{1,0:T(8,128)(2,1)S(1)}, bf16[128,3584]{1,0:T(8,128)(2,1)S(1)}, u32[]{:S(2)}, u32[]{:S(2)}) collective-permute-start(bf16[128,3584]{1,0:T(8,128)(2,1)S(1)} %add_convert_fusion.1), channel_id=1, source_target_pairs={{0,24},{4,28},{8,0},{12,4},{16,8},{20,12},{24,16},{28,20},{1,25},{... | collective-permute-start | bytes 2752520 | tf_op jit(solution)/shard_map/ppermute | solution.py:311
  111.6 21.6 %collective-permute-start.25 = (bf16[8,3584]{1,0:T(8,128)(2,1)S(1)}, bf16[8,3584]{1,0:T(8,128)(2,1)S(1)}, u32[]{:S(2)}, u32[]{:S(2)}) collective-permute-start(bf16[8,3584]{1,0:T(8,128)(2,1)S(1)} %slice.249), channel_id=1, source_target_pairs={{0,24},{4,28},{8,0},{12,4},{16,8},{20,12},{24,16},{28,20},{1,25},{... | collective-permute-start | bytes 172040 | tf_op jit(solution)/shard_map/ppermute | solution.py:311
  130.3 106.0 %collective-permute-start.35 = (bf16[128,3584]{1,0:T(8,128)(2,1)S(1)}, bf16[128,3584]{1,0:T(8,128)(2,1)}, u32[]{:S(2)}, u32[]{:S(2)}) collective-permute-start(bf16[128,3584]{1,0:T(8,128)(2,1)S(1)} %get-tuple-element.104.refs_14_), channel_id=1, source_target_pairs={{0,4},{4,0},{8,12},{12,8},{16,20},{20,16},{24,28},{28,24},{1,5},{5... | collective-permute-start | bytes 2752520 | tf_op jit(solution)/shard_map/ppermute | solution.py:311
  131.1 105.3 %collective-permute-start.34 = (bf16[128,3584]{1,0:T(8,128)(2,1)S(1)}, bf16[128,3584]{1,0:T(8,128)(2,1)}, u32[]{:S(2)}, u32[]{:S(2)}) collective-permute-start(bf16[128,3584]{1,0:T(8,128)(2,1)S(1)} %get-tuple-element.104.refs_14_), channel_id=1, source_target_pairs={{0,24},{4,28},{8,0},{12,4},{16,8},{20,12},{24,16},{28,20},{1,25},{... | collective-permute-start | bytes 2752520 | tf_op jit(solution)/shard_map/ppermute | solution.py:311
  133.2 103.1 %collective-permute-start.33 = (bf16[128,3584]{1,0:T(8,128)(2,1)S(1)}, bf16[128,3584]{1,0:T(8,128)(2,1)}, u32[]{:S(2)}, u32[]{:S(2)}) collective-permute-start(bf16[128,3584]{1,0:T(8,128)(2,1)S(1)} %get-tuple-element.104.refs_14_), channel_id=1, source_target_pairs={{0,8},{4,12},{8,16},{12,20},{16,24},{20,28},{24,0},{28,4},{1,9},{5... | collective-permute-start | bytes 2752520 | tf_op jit(solution)/shard_map/ppermute | solution.py:311
  152.5 66.0 %collective-permute-start.29 = (f32[128,128]{1,0:T(8,128)S(1)}, f32[128,128]{1,0:T(8,128)S(1)}, u32[]{:S(2)}, u32[]{:S(2)}) collective-permute-start(f32[128,128]{1,0:T(8,128)S(1)} %collective-permute-done.28.r0), channel_id=1, source_target_pairs={{0,1},{1,0},{2,3},{3,2},{4,5},{5,4},{6,7},{7,6},{8,9},{9,8},{10,11... | collective-permute-start | bytes 196616 | tf_op jit(solution)/shard_map/ppermute | solution.py:316
  241.4 37.3 %collective-permute-start.44 = (bf16[128,3584]{1,0:T(8,128)(2,1)}, bf16[128,3584]{1,0:T(8,128)(2,1)}, u32[]{:S(2)}, u32[]{:S(2)}) collective-permute-start(bf16[128,3584]{1,0:T(8,128)(2,1)} %get-tuple-element.120), channel_id=1, source_target_pairs={{0,4},{4,0},{8,12},{12,8},{16,20},{20,16},{24,28},{28,24},{1,5},{5... | collective-permute-start | bytes 2752520 | tf_op jit(solution)/shard_map/ppermute | solution.py:311
  241.4 37.3 %collective-permute-start.43 = (bf16[128,3584]{1,0:T(8,128)(2,1)}, bf16[128,3584]{1,0:T(8,128)(2,1)}, u32[]{:S(2)}, u32[]{:S(2)}) collective-permute-start(bf16[128,3584]{1,0:T(8,128)(2,1)} %get-tuple-element.121), channel_id=1, source_target_pairs={{0,24},{4,28},{8,0},{12,4},{16,8},{20,12},{24,16},{28,20},{1,25},{... | collective-permute-start | bytes 2752520 | tf_op jit(solution)/shard_map/ppermute | solution.py:311
  242.3 36.3 %collective-permute-start.42 = (bf16[128,3584]{1,0:T(8,128)(2,1)}, bf16[128,3584]{1,0:T(8,128)(2,1)}, u32[]{:S(2)}, u32[]{:S(2)}) collective-permute-start(bf16[128,3584]{1,0:T(8,128)(2,1)} %get-tuple-element.122), channel_id=1, source_target_pairs={{0,8},{4,12},{8,16},{12,20},{16,24},{20,28},{24,0},{28,4},{1,9},{5... | collective-permute-start | bytes 2752520 | tf_op jit(solution)/shard_map/ppermute | solution.py:311
  279.9 22.9 %collective-permute-start.51 = (bf16[64,3584]{1,0:T(8,128)(2,1)S(1)}, bf16[64,3584]{1,0:T(8,128)(2,1)S(1)}, u32[]{:S(2)}, u32[]{:S(2)}) collective-permute-start(bf16[64,3584]{1,0:T(8,128)(2,1)S(1)} %get-tuple-element.111.refs_23_), channel_id=1, source_target_pairs={{0,4},{4,0},{8,12},{12,8},{16,20},{20,16},{24,28},{28,24},{1,5},{5... | collective-permute-start | bytes 1376264 | tf_op jit(solution)/shard_map/ppermute | solution.py:311
  317.9 24.3 %all-to-all-start = ((f32[8,128,128]{2,1,0:T(8,128)}), f32[8,128,128]{2,1,0:T(8,128)S(1)}, u32[]{:S(2)}, u32[]{:S(2)}) async-start(f32[8,128,128]{2,1,0:T(8,128)} %broadcast_in_dim.12), calls=%async_computation | async-start | bytes 1048576 | tf_op jit(solution)/shard_map/all_to_all | solution.py:456
  (64 other events, 418.1 us)
Sparse Core Ops, SparseCore 0:
  152.4 66.0 all-reduce.15

commit v3 on v2

v3 whole, which is shorter than its diff:
```python
import functools

import jax
import jax.numpy as jnp
from jax import lax
from jax.experimental import pallas as pl
from jax.experimental.pallas import tpu as pltpu
from jax.sharding import PartitionSpec as P

BF = jnp.bfloat16
F32 = jnp.float32
HIGHEST = lax.Precision.HIGHEST
NT = (((1,), (1,)), ((), ()))
CHUNK = 512
X_SIZE = 4
RELATIVE = ((0, 0), (0, 1), (-1, 0), (-1, 1), (1, 0), (1, 1), (2, 0), (2, 1))
EARLY, LATE = (7, 6, 3, 5), (2, 4, 1, 0)
PARAMS = pltpu.CompilerParams(vmem_limit_bytes=48 * 1024 * 1024)
SMALL = pltpu.CompilerParams(vmem_limit_bytes=16 * 1024 * 1024)


def split2(x):
    hi = x.astype(BF)
    return hi, (x - hi.astype(F32)).astype(BF)


def mm(a, b):
    return jnp.dot(a, b, preferred_element_type=F32)


def mm_nt(a, b):
    return lax.dot_general(a, b, NT, preferred_element_type=F32)


def sigma(v):
    return 0.5 * jnp.tanh(0.5 * v) + 0.5


def wide(x):
    return jnp.concatenate(split2(x), axis=1)


def tall(x):
    return jnp.concatenate(split2(x), axis=0)


def twice(x):
    return jnp.concatenate([x, x], axis=0)


def chunks_of(width):
    return [slice(i, i + CHUNK) for i in range(0, width, CHUNK)]


def gram_share(x, gram):
    return 0.25 * jnp.dot(x, gram, precision=HIGHEST, preferred_element_type=F32)


def first_kernel(base_ref, down_ref, part_ref):
    acc = jnp.zeros(part_ref.shape, F32)
    for cols in chunks_of(base_ref.shape[1]):
        pre = base_ref[:, cols]
        hidden = (pre * sigma(pre)).astype(BF)
        acc += mm_nt(hidden, down_ref[:, cols])
    part_ref[...] = acc


def forward_kernel(base_ref, up_ref, down_ref, gram_ref, r0, r1, part_ref):
    c = r0[...] + r1[...]
    cw = wide(c)
    acc = gram_share(c, gram_ref[...])
    for cols in chunks_of(base_ref.shape[1]):
        pre = base_ref[:, cols] + mm(cw, twice(up_ref[:, cols]))
        hidden = (pre * sigma(pre)).astype(BF)
        acc += mm_nt(hidden, down_ref[:, cols])
    part_ref[...] = acc


def middle_kernel(base_ref, up_ref, down_ref, gram_ref, r0, r1, c_ref, part_ref, slope_ref):
    c = r0[...] + r1[...]
    c_ref[...] = c.astype(BF)
    cw = wide(c)
    acc = gram_share(c, gram_ref[...])
    for cols in chunks_of(base_ref.shape[1]):
        pre = base_ref[:, cols] + mm(cw, twice(up_ref[:, cols]))
        sig = sigma(pre)
        hidden = (pre * sig).astype(BF)
        slope_ref[:, cols] = sig * (1.0 + pre * (1.0 - sig))
        acc += mm_nt(hidden, down_ref[:, cols])
    part_ref[...] = acc


def backward_kernel(last_ref, slope_ref, up_ref, down_ref, gram_ref, cot_ref, r0, r1, g_ref, part_ref):
    g = jnp.where(last_ref[0] == 1, cot_ref[...], r0[...] + r1[...])
    g_ref[...] = g
    gw = wide(g)
    acc = gram_share(g, gram_ref[...])
    for cols in chunks_of(slope_ref.shape[1]):
        g_pre = mm(gw, twice(down_ref[:, cols])) * slope_ref[:, cols]
        hi, lo = split2(g_pre)
        acc += mm_nt(hi, up_ref[:, cols]) + mm_nt(lo, up_ref[:, cols])
    part_ref[...] = acc


def call(kernel, outs, *args):
    return pl.pallas_call(kernel, out_shape=outs, compiler_params=SMALL)(*args)


def base_specs(base, dp, blocks):
    micro, tokens, width = base.shape
    return [
        pl.BlockSpec((micro, tokens // dp, width), lambda i, p, j=j: (0, p[j], 0)) for j in blocks
    ]


def product_kernel(count, with_basis, place_ref, *refs):
    bases, w_ref, refs = refs[:count], refs[count], refs[count + 1 :]
    own = bases[0].shape[0] * bases[0].shape[1]
    if with_basis:
        basis_ref, w_out_ref, refs = refs[0], refs[1], refs[2:]
        rank = basis_ref.shape[1]
    outs, rows = refs[:-1], refs[-1]

    @pl.when(pl.program_id(0) == 0)
    def _():
        for j, b in enumerate(bases):
            rows[j * own : (j + 1) * own] = b[...].reshape(own, b.shape[2])
        if with_basis:
            rows[count * own :] = tall(basis_ref[...].T)

    res = mm(rows[...], w_ref[...])
    for j in range(count):
        outs[j][...] = res[j * own : (j + 1) * own].astype(BF)
    if with_basis:
        up, both = outs[count:]
        up[...] = (res[count * own : count * own + rank] + res[count * own + rank :]).astype(BF)
        down = mm(w_out_ref[...], wide(basis_ref[...]))
        both[...] = (down[:, :rank] + down[:, rank:]).T.astype(BF)


def product(place, base, w_in, dp, blocks, basis=None, w_out=None):
    micro, tokens, width = base.shape
    hid = w_in.shape[1]
    own = micro * tokens // dp
    count = len(blocks)
    column = lambda rows: pl.BlockSpec((rows, CHUNK), lambda i, p: (0, i))
    in_specs = base_specs(base, dp, blocks) + [column(width)]
    shapes, height, more = [own] * count, own * count, ()
    if basis is not None:
        rank = basis.shape[1]
        in_specs += [
            pl.BlockSpec(basis.shape, lambda i, p: (0, 0)),
            pl.BlockSpec((CHUNK, width), lambda i, p: (i, 0)),
        ]
        shapes, height, more = shapes + [rank, rank], height + 2 * rank, (basis, w_out)
    return pl.pallas_call(
        functools.partial(product_kernel, count, basis is not None),
        out_shape=[jax.ShapeDtypeStruct((rows, hid), BF) for rows in shapes],
        grid_spec=pltpu.PrefetchScalarGridSpec(
            num_scalar_prefetch=1,
            grid=(hid // CHUNK,),
            in_specs=in_specs,
            out_specs=[column(rows) for rows in shapes],
            scratch_shapes=[pltpu.VMEM((height, width), BF)],
        ),
        compiler_params=PARAMS,
    )(place, *([base] * count), w_in, *more)


def assemble_kernel(steps, place_ref, *refs):
    pieces, (up_ref, down_ref, gram_ref) = refs[:-3], refs[-3:]
    rows = up_ref.shape[1]
    step = pl.program_id(0)
    flat = jnp.concatenate([p[...] for p in pieces], axis=0)

    @pl.when(step < steps)
    def _():
        for j in range(len(RELATIVE)):
            up_ref[place_ref[j]] = flat[2 * j * rows : (2 * j + 1) * rows]
            down_ref[place_ref[j]] = flat[(2 * j + 1) * rows : (2 * j + 2) * rows]

    @pl.when(step >= steps)
    def _():
        total = flat[: 2 * rows].astype(F32)
        for j in range(1, len(RELATIVE)):
            total += flat[2 * j * rows : (2 * j + 2) * rows].astype(F32)
        gram_ref[...] = jnp.where(step == steps, total, gram_ref[...] + total)


def assemble(place, pieces, rank, hid):
    count = len(RELATIVE)
    steps = hid // CHUNK
    rows = rank // count
    shape = (count, rows, hid)
    spec = pl.BlockSpec((count, rows, CHUNK), lambda i, p: (0, 0, jnp.minimum(i, steps - 1)))
    up, down, gram = pl.pallas_call(
        functools.partial(assemble_kernel, steps),
        out_shape=[jax.ShapeDtypeStruct(shape, BF)] * 2
        + [jax.ShapeDtypeStruct((2 * rows, CHUNK), F32)],
        grid_spec=pltpu.PrefetchScalarGridSpec(
            num_scalar_prefetch=1,
            grid=(pieces[0][0].shape[1] // CHUNK,),
            in_specs=piece_specs(pieces),
            out_specs=[spec, spec, pl.BlockSpec((2 * rows, CHUNK), lambda i, p: (0, 0))],
        ),
        compiler_params=SMALL,
    )(place, *[a for a, _, _ in pieces])
    return up.reshape(rank, hid), down.reshape(rank, hid), gram.reshape(rank, rank)


def copy_kernel(plan, count, *refs):
    for out, parts in zip(refs[count:], plan):
        out[...] = jnp.concatenate([refs[k][a:b] for k, a, b in parts], axis=0)


def copies(arrays, plan):
    hid = arrays[0].shape[1]
    heights = [sum(b - a for _, a, b in parts) for parts in plan]
    column = lambda rows: pl.BlockSpec((rows, CHUNK), lambda i: (0, i))
    return pl.pallas_call(
        functools.partial(copy_kernel, plan, len(arrays)),
        out_shape=[jax.ShapeDtypeStruct((rows, hid), BF) for rows in heights],
        grid=(hid // CHUNK,),
        in_specs=[column(a.shape[0]) for a in arrays],
        out_specs=[column(rows) for rows in heights],
        compiler_params=SMALL,
    )(*arrays)


def prepare_kernel(count, place_ref, *refs):
    bases, refs = refs[:count], refs[count:]
    half = count // 2
    basis_ref, c_refs, up_ref, pieces = refs[0], refs[1 : 1 + half], refs[1 + half], refs[2 + half : -3]
    xt_ref, hidden_ref, slope_ref = refs[-3:]
    own = bases[0].shape[0] * bases[0].shape[1]

    @pl.when(pl.program_id(0) == 0)
    def _():
        basis = basis_ref[...].astype(BF)
        for j, b in enumerate(bases):
            c = c_refs[j // 2][(j % 2) * own : (j % 2 + 1) * own]
            x = b[...].reshape(own, b.shape[2]).astype(F32) + mm_nt(c, basis)
            xt_ref[:, j * own : (j + 1) * own] = x.T.astype(BF)

    up = up_ref[...]
    start = 0
    c_all = jnp.concatenate([c[...] for c in c_refs], axis=0)
    for p in pieces:
        rows = slice(start, start + p.shape[0])
        start += p.shape[0]
        pre = p[...].astype(F32) + mm(c_all[rows], up)
        sig = sigma(pre)
        hidden = pre * sig
        hidden_ref[rows] = hidden.astype(BF)
        slope_ref[rows] = (sig + hidden * (1.0 - sig)).astype(BF)


def prepare(place, base, dp, blocks, basis, c_pieces, up, pieces):
    micro, tokens, width = base.shape
    hid = up.shape[1]
    every = micro * tokens // dp * len(blocks)
    whole = lambda a: pl.BlockSpec(a.shape, lambda i, p: (0, 0))
    column = lambda rows: pl.BlockSpec((rows, CHUNK), lambda i, p: (0, i))
    return pl.pallas_call(
        functools.partial(prepare_kernel, len(blocks)),
        out_shape=[
            jax.ShapeDtypeStruct((width, every), BF),
            jax.ShapeDtypeStruct((every, hid), BF),
            jax.ShapeDtypeStruct((every, hid), BF),
        ],
        grid_spec=pltpu.PrefetchScalarGridSpec(
            num_scalar_prefetch=1,
            grid=(hid // CHUNK,),
            in_specs=base_specs(base, dp, blocks)
            + [whole(basis)]
            + [whole(c) for c in c_pieces]
            + [column(up.shape[0])]
            + piece_specs(pieces),
            out_specs=[
                pl.BlockSpec((width, every), lambda i, p: (0, 0)),
                column(every),
                column(every),
            ],
        ),
        compiler_params=PARAMS,
    )(place, *([base] * len(blocks)), basis, *c_pieces, up, *[a for a, _, _ in pieces])


def finish_kernel(place_ref, g_ref, down_ref, xt0, hidden0, slope0, xt1, hidden1, slope1, *refs):
    grad_ref, dc_ref, gw, gt = refs
    rank = down_ref.shape[0]
    own = g_ref.shape[1]

    @pl.when(pl.program_id(0) == 0)
    def _():
        for j in range(len(RELATIVE)):
            g = g_ref[place_ref[j]]
            gw[j * own : (j + 1) * own] = wide(g)
            gt[:, j * own : (j + 1) * own] = tall(g.T)

    h = gw.shape[0] // 2
    down2 = twice(down_ref[...])
    low = (mm(gw[:h], down2) * slope0[...].astype(F32)).astype(BF)
    high = (mm(gw[h:], down2) * slope1[...].astype(F32)).astype(BF)
    grad_ref[...] = (mm(xt0[...], low) + mm(xt1[...], high)).astype(BF)
    dc = mm(gt[:, :h], hidden0[...]) + mm(gt[:, h:], hidden1[...])
    dc_ref[...] = (dc[:rank] + dc[rank:]).T


def finish(place, g_all, down, first, second):
    rank, hid = down.shape
    width, every = first[0].shape
    column = lambda rows: pl.BlockSpec((rows, CHUNK), lambda i, p: (0, i))
    part = [pl.BlockSpec((width, every), lambda i, p: (0, 0)), column(every), column(every)]
    return pl.pallas_call(
        finish_kernel,
        out_shape=[jax.ShapeDtypeStruct((width, hid), BF), jax.ShapeDtypeStruct((hid, rank), F32)],
        grid_spec=pltpu.PrefetchScalarGridSpec(
            num_scalar_prefetch=1,
            grid=(hid // CHUNK,),
            in_specs=[pl.BlockSpec(g_all.shape, lambda i, p: (0, 0, 0)), column(rank)] + part + part,
            out_specs=[column(width), pl.BlockSpec((CHUNK, rank), lambda i, p: (i, 0))],
            scratch_shapes=[
                pltpu.VMEM((2 * every, 2 * rank), BF),
                pltpu.VMEM((2 * rank, 2 * every), BF),
            ],
        ),
        compiler_params=PARAMS,
    )(place, g_all, down, *first, *second)


def to_dp(x, dx, dy):
    size = lax.axis_size("dp")
    pairs = [(i, ((i // 2 + dx) % X_SIZE) * 2 + ((i % 2) ^ dy)) for i in range(size)]
    return lax.ppermute(x, "dp", pairs)


def to_tensor(x, k):
    size = lax.axis_size("tensor")
    return lax.ppermute(x, "tensor", [(t, t ^ k) for t in range(size)])


def hop(part, by, *beside):
    sections, tensors = lax.axis_size("section"), lax.axis_size("tensor")
    pair_sum = part + to_tensor(part, 1)
    pair_sum, *beside = tie(pair_sum, *beside)
    pairs = [
        (s * tensors + t, (s + by) * tensors + (t ^ (2 * (t % 2))))
        for s in range(sections)
        for t in range(tensors)
        if 0 <= s + by < sections
    ]
    got = lax.ppermute(pair_sum, ("section", "tensor"), pairs)
    return (got, to_tensor(got, 1), *beside)


def cat(*xs):
    return jnp.concatenate(xs, axis=0)


def plus(x, *ys):
    total = x.astype(F32)
    for start, y in ys:
        pads = ((start, x.shape[0] - start - y.shape[0]), (0, 0))
        total = total + jnp.pad(y.astype(F32), pads)
    return total.astype(x.dtype)


def reduce_blocks(blocks):
    b = dict(zip(RELATIVE, blocks))
    n = blocks[0].shape[0]
    h, q = n // 2, n // 4
    far = b[2, 1]
    u0, u1, v = to_dp(far[:q], 1, 0), to_dp(far[q:h], -1, 0), to_dp(far[h:], 0, 1)
    up = to_dp(cat(b[2, 0][:h], plus(b[1, 1][:h], (0, u0))), 1, 0)
    down = to_dp(cat(plus(b[2, 0][h:], (0, v)), plus(b[-1, 1][:h], (q, u1))), -1, 0)
    side = to_dp(cat(b[1, 1][h:], b[-1, 1][h:]), 0, 1)
    e1 = to_dp(plus(b[1, 0], (0, up[:h]), (h, side[:h])), 1, 0)
    e2 = to_dp(plus(b[-1, 0], (h, down[:h]), (h, side[h:])), -1, 0)
    e3 = to_dp(plus(b[0, 1], (0, up[h:]), (0, down[h:])), 0, 1)
    f = lambda a: a.astype(F32)
    return (f(b[0, 0]) + f(e1)) + (f(e2) + f(e3))


def gather_1(g):
    return to_dp(g, 1, 0), to_dp(g, -1, 0), to_dp(g, 0, 1)


def gather_2(got):
    n = got[0].shape[0]
    h = n // 2
    left, right, side = copies(
        got, [[(2, 0, h), (0, 0, h)], [(2, 0, h), (1, h, n)], [(0, h, n), (1, h, n)]]
    )
    return to_dp(left, 1, 0), to_dp(right, -1, 0), to_dp(side, 0, 1)


def gather_3(got):
    h = got[0].shape[0] // 2
    q = h // 2
    left, right, side = copies(got, [[(0, 0, q)], [(1, q, h)], [(1, h, 2 * h)]])
    return to_dp(left, 1, 0), to_dp(right, -1, 0), to_dp(side, 0, 1)


def gathered(g, s1, s2, s3):
    (left, right, side), (am_t0, ap_t1, bm_bp), (u0, u1, v) = s1, s2, s3
    whole = lambda a: (a, 0, a.shape[0])
    low = lambda a: (a, 0, a.shape[0] // 2)
    high = lambda a: (a, 1, a.shape[0] // 2)
    return (
        [whole(g), whole(side), whole(left), low(am_t0), low(bm_bp)],
        [
            whole(right), low(ap_t1), high(bm_bp), high(am_t0), high(ap_t1),
            whole(u0), whole(u1), whole(v),
        ],
    )


def piece_specs(pieces):
    return [pl.BlockSpec((n, CHUNK), lambda i, p, k=k: (k, i)) for _, k, n in pieces]


def tie(*xs):
    return lax.optimization_barrier(xs)


def on_device(base, w_in, w_out, basis, cotangent):
    dp = lax.axis_size("dp")
    sections = lax.axis_size("section")
    last = (lax.axis_index("section") == sections - 1).astype(jnp.int32).reshape(1)
    d = lax.axis_index("dp")
    place = jnp.stack(
        [((d // 2 + dx) % X_SIZE) * 2 + (d % 2 + dy) % 2 for dx, dy in RELATIVE]
    ).astype(jnp.int32)
    micro, tokens, width = base.shape
    rows = tokens // dp
    own = micro * rows
    rank = basis.shape[1]
    w_in, w_out = w_in[0], w_out[0]
    hid = w_in.shape[1]
    tok = jax.ShapeDtypeStruct((own, rank), F32)

    blocks = [None] * len(RELATIVE)
    *early, up_part, down_part = product(place, base, w_in, dp, EARLY, basis, w_out)
    for j, block in zip(EARLY, early):
        blocks[j] = block
    for j, block in zip(LATE, product(place, base, w_in, dp, LATE)):
        blocks[j] = block
    share = rank // dp
    proj = reduce_blocks(
        [
            cat(*(lax.dynamic_slice_in_dim(x, place[j] * share, share) for x in (up_part, down_part)))
            for j in range(len(RELATIVE))
        ]
    ).astype(BF)
    gram_part = lax.dot_general(basis, basis, (((0,), (0,)), ((), ())), precision=HIGHEST)
    gram_part = split2(gram_part.reshape(2 * share, -1))
    proj = jnp.concatenate([proj, *gram_part], axis=1)
    base_pre = reduce_blocks(blocks)
    p1 = gather_1(proj)
    p2 = gather_2(p1)
    p3 = gather_3(p2)
    up, down, gram = assemble(place, sum(gathered(proj, p1, p2, p3), []), rank, hid)

    base_half = base_pre.astype(BF)
    s1 = gather_1(base_half)
    part = call(first_kernel, tok, base_pre, down)
    got = hop(part, 1)
    part = call(forward_kernel, tok, base_pre, up, down, gram, *got)
    got = hop(part, 1)
    part = call(forward_kernel, tok, base_pre, up, down, gram, *got)
    *got, s1 = hop(part, 1, s1)
    s2 = gather_2(s1)
    c_in, coef_part, slope = call(
        middle_kernel,
        (jax.ShapeDtypeStruct((own, rank), BF), tok, jax.ShapeDtypeStruct((own, hid), F32)),
        base_pre, up, down, gram, *got,
    )
    cot = cotangent.reshape(own, rank)

    def back(got):
        return call(backward_kernel, (tok, tok), last, slope, up, down, gram, cot, *got)

    c_pair = cat(c_in, to_dp(c_in, 0, 1))
    _, part = back((cot, cot))
    got = hop(part, -1)
    _, part = back(got)
    *got, s2, c_pair = hop(part, -1, s2, c_pair)
    s3 = gather_3(s2)
    c_far = [to_dp(c_pair, dx, 0) for dx in (-1, 1, 2)]
    _, part = back(got)
    *got, s2, s3, c_far = hop(part, -1, s2, s3, c_far)
    left, right, far = c_far[1], c_far[0], c_far[2]
    pieces = gathered(base_half, s1, s2, s3)
    first = prepare(place, base, dp, range(4), basis, [c_pair, left], up, pieces[0])
    *got, first = tie(*got, first)
    second = prepare(place, base, dp, range(4, 8), basis, [right, far], up, pieces[1])
    g_out = jnp.where(last[0] == 1, cot, got[0] + got[1])
    g_all = lax.all_to_all(jnp.broadcast_to(g_out[None], (dp, own, rank)), "dp", 0, 0, tiled=True)
    _, grad_part = back(got)
    grad_up, down_coefs = finish(place, g_all, down, first, second)
    parts = cat(coef_part, grad_part)
    parts = parts + to_tensor(parts, 1)
    parts = (parts + to_tensor(parts, 2)).reshape(2, 1, micro, rows, rank)
    return parts[0], parts[1], grad_up[None], down_coefs[None]


def solution(mesh):
    return jax.shard_map(
        on_device,
        mesh=mesh,
        in_specs=(
            P(None, None, "dp"),
            P("section", "dp", "tensor"),
            P("section", "tensor", "dp"),
            P("dp", None),
            P(None, "dp", None),
        ),
        out_specs=(
            P("section", None, "dp", None),
            P("section", None, "dp", None),
            P("section", "dp", "tensor"),
            P("section", "tensor", None),
        ),
        check_vma=False,
    )
```

time: 368 us -> 348 us (0.946)
  waiting for transfers between devices: 172 us -> 144 us
  Pallas kernels: 66.1 us -> 82.2 us
  between operations: 14.9 us -> 1.56 us
  local copies, waits for them, and re-layouts: 20.6 us -> 25.4 us
    psum x1 -> x0, waiting for transfers between devices: 66 us -> none  [on_device(): lax.psum(lax.dot_general(basis, basis, (((0,), (0,)), ((), ())), precisio...]
    ppermute x40, waiting for transfers between devices: 65.7 us -> 91.6 us  [to_dp(): return lax.ppermute(x, 'dp', pairs)]
    pallas_call x12 -> x17, Pallas kernels: 49.5 us -> 64.8 us  [the longest x2 21.7 us: product(): pl.pallas_call(functools.partial(product_kernel, count, basis is not None...]
    ppermute x6, waiting for transfers between devices: 30.2 us -> 41.7 us  [hop(): got = lax.ppermute(pair_sum, ('section', 'tensor'), pairs)]
    unnamed x51 -> x75, local copies, waits for them, and re-layouts: 8.84 us -> 19.8 us
    slice x15 -> x0, local copies, waits for them, and re-layouts: 8.09 us -> none  [the longest x2 1.57 us: gathered(): am_t0[h:]]
  transfers between devices with their start and end apart: 62 -> 61, of which waited for: 31 -> 29; matrix products, arithmetic and copies ran while one was open for 3% -> 4% of each run, Pallas kernels for 10% -> 12%
where the time goes in v3:
time: 348 us; the launch traced here: 347 us
  waiting for transfers between devices  144 us (41%)
  starting transfers between devices  84.3 us (24%)
  Pallas kernels  82.2 us (24%)
  local copies, waits for them, and re-layouts  25.4 us (7%)
  other arithmetic  7.94 us (2%)
    ppermute x40, waiting for transfers between devices, to_dp(): return lax.ppermute(x, 'dp', pairs)  91.6 us
    ppermute x6, waiting for transfers between devices, hop(): got = lax.ppermute(pair_sum, ('section', 'tensor'), pairs)  41.7 us
    ppermute x40, starting transfers between devices, to_dp(): return lax.ppermute(x, 'dp', pairs)  41.3 us
    ppermute x6, starting transfers between devices, hop(): got = lax.ppermute(pair_sum, ('section', 'tensor'), pairs)  23 us
    pallas_call x2, Pallas kernels, product(): pl.pallas_call(functools.partial(product_kernel, count, basis is not None...  21.7 us
    pallas_call x2, Pallas kernels, prepare(): pl.pallas_call(functools.partial(prepare_kernel, len(blocks)), out_shape=...  19.9 us
    unnamed x75, local copies, waits for them, and re-layouts  19.8 us
    pallas_call x1, Pallas kernels, finish(): pl.pallas_call(finish_kernel, out_shape=[jax.ShapeDtypeStruct((width, hid...  17.3 us
  transfers between devices with their start and end apart: 61, of which 29 were waited for; matrix products, arithmetic and copies ran while one was open for 4% of the time, Pallas kernels for 12%

profile of v3, /device:TPU:1, one launch (start us, length us, event | category | flops | bytes accessed | tf_op | source)
XLA Modules:
  0.0 346.5 jit_solution(7517496536861692140)
XLA Ops:
  1.9 13.1 %shard_map.85 = (bf16[128,3584]{1,0:T(8,128)(2,1)S(1)}, bf16[128,3584]{1,0:T(8,128)(2,1)S(1)}, bf16[128,3584]{1,0:T(8,128)(2,1)S(1)}, bf16[128,3584]{1,0:T(8,128...) custom-call(s32[8]{0:T(128)S(1)} %stack.35.place_ref, bf16[4,256,1024]{2,1,0:T(8,128)(2,1)} %refs_3_.7, ...), custom_call_target="tpu_custom_call" | custom-call | tf_op jit(solution)/shard_map/pallas_call | solution.py:156
  31.5 8.6 %shard_map.84 = (bf16[128,3584]{1,0:T(8,128)(2,1)S(1)}, bf16[128,3584]{1,0:T(8,128)(2,1)S(1)}, bf16[128,3584]{1,0:T(8,128)(2,1)S(1)}, bf16[128,3584]{1,0:T(8,128)(2,1)S(1)}) custom-call(s32[8]{0:T(128)S(1)} %stack.35.place_ref, bf16[4,256,1024]{2,1,0:T(8,128)(2,1)S(1)} %copy-done, bf16[4,256,1024]{2,1,0:T(8,128)(2,1)S(1)} %copy-done, ...), custom_call_target="tpu_custom_call" | custom-call | tf_op jit(solution)/shard_map/pallas_call | solution.py:156
  51.0 3.2 collective-permute-start.16
  57.0 19.6 %collective-permute-done.12 = bf16[32,3584]{1,0:T(8,128)(2,1)S(1)} collective-permute-done((bf16[32,3584]{1,0:T(8,128)(2,1)S(1)}, bf16[32,3584]{1,0:T(8,128)(2,1)S(1)}, u32[]{:S(2)}, u32[]{:S(2)}) %collective-permute-start.12) | collective-permute-done | bytes 229408 | tf_op jit(solution)/shard_map/ppermute | solution.py:335
  78.8 15.8 %collective-permute-done.6 = bf16[128,3584]{1,0:T(8,128)(2,1)S(1)} collective-permute-done((bf16[128,3584]{1,0:T(8,128)(2,1)S(1)}, bf16[128,3584]{1,0:T(8,128)(2,1)S(1)}, u32[]{:S(2)}, u32[]{:S(2)}) %collective-permute-start.6) | collective-permute-done | bytes 917536 | tf_op jit(solution)/shard_map/ppermute | solution.py:335
  99.9 19.8 %collective-permute-done.20.refs_1_.refs_5_ = bf16[32,4608]{1,0:T(8,128)(2,1)S(1)} collective-permute-done((bf16[32,4608]{1,0:T(8,128)(2,1)S(1)}, bf16[32,4608]{1,0:T(8,128)(2,1)S(1)}, u32[]{:S(2)}, u32[]{:S(2)}) %collective-permute-start.20) | collective-permute-done | bytes 294944 | tf_op jit(solution)/shard_map/ppermute | solution.py:335
  121.2 4.1 %collective-permute-done.18.refs_2_.refs_1_ = bf16[32,4608]{1,0:T(8,128)(2,1)S(1)} collective-permute-done((bf16[32,4608]{1,0:T(8,128)(2,1)S(1)}, bf16[32,4608]{1,0:T(8,128)(2,1)S(1)}, u32[]{:S(2)}, u32[]{:S(2)}) %collective-permute-start.18) | collective-permute-done | bytes 294944 | tf_op jit(solution)/shard_map/ppermute | solution.py:335
  133.3 17.1 %collective-permute-done.22.refs_2_.refs_4_.refs_7_ = bf16[32,4608]{1,0:T(8,128)(2,1)S(1)} collective-permute-done((bf16[32,4608]{1,0:T(8,128)(2,1)S(1)}, bf16[32,4608]{1,0:T(8,128)(2,1)S(1)}, u32[]{:S(2)}, u32[]{:S(2)}) %collective-permute-start.22) | collective-permute-done | bytes 294944 | tf_op jit(solution)/shard_map/ppermute | solution.py:335
  152.4 4.1 %collective-permute-done.24.refs_10_ = bf16[8,4608]{1,0:T(8,128)(2,1)S(1)} collective-permute-done((bf16[8,4608]{1,0:T(8,128)(2,1)S(1)}, bf16[8,4608]{1,0:T(8,128)(2,1)S(1)}, u32[]{:S(2)}, u32[]{:S(2)}) %collective-permute-start.24) | collective-permute-done | bytes 73760 | tf_op jit(solution)/shard_map/ppermute | solution.py:335
  156.5 3.2 collective-permute-done.25.refs_11_
  162.1 10.3 %collective-permute-start.27 = (f32[128,128]{1,0:T(8,128)S(1)}, f32[128,128]{1,0:T(8,128)S(1)}, u32[]{:S(2)}, u32[]{:S(2)}) collective-permute-start(f32[128,128]{1,0:T(8,128)S(1)} %shard_map.89), channel_id=1, source_target_pairs={{0,1},{1,0},{2,3},{3,2},{4,5},{5,4},{6,7},{7,6},{8,9},{9,8},{10,11... | collective-permute-start | bytes 196616 | tf_op jit(solution)/shard_map/ppermute | solution.py:340
  173.3 6.4 %collective-permute-start.28 = (f32[128,128]{1,0:T(8,128)S(1)}, f32[128,128]{1,0:T(8,128)S(1)}, u32[]{:S(2)}, u32[]{:S(2)}) collective-permute-start(f32[128,128]{1,0:T(8,128)S(1)} %add.292), channel_id=1, source_target_pairs={{0,32},{1,35},{2,34},{3,33},{32,64},{33,67},{34,66},{35,65},{64,96... | collective-permute-start | bytes 196616 | tf_op jit(solution)/shard_map/ppermute | solution.py:353
  185.9 6.1 %collective-permute-start.31 = (f32[128,128]{1,0:T(8,128)S(1)}, f32[128,128]{1,0:T(8,128)S(1)}, u32[]{:S(2)}, u32[]{:S(2)}) collective-permute-start(f32[128,128]{1,0:T(8,128)S(1)} %add.293), channel_id=1, source_target_pairs={{0,32},{1,35},{2,34},{3,33},{32,64},{33,67},{34,66},{35,65},{64,96... | collective-permute-start | bytes 196616 | tf_op jit(solution)/shard_map/ppermute | solution.py:353
  196.7 5.7 %shard_map.95 = (bf16[128,3584]{1,0:T(8,128)(2,1)}, bf16[128,3584]{1,0:T(8,128)(2,1)}, bf16[128,3584]{1,0:T(8,128)(2,1)}) custom-call(bf16[128,3584]{1,0:T(8,128)(2,1)} %collective-permute-done.34.refs_0_.refs_10_, bf16[128,3584]{1,0:T(8,128)(2,1)} %collective-permute-done.35.refs_1_.refs_8_, bf16[128,3584]{1,0:T(8,128)(2,1)} %collective-permute-done.36.refs_2_.refs_9_), custom_call_target="tpu_custom_call" | custom-call | tf_op jit(solution)/shard_map/pallas_call | solution.py:220
  205.5 6.7 %collective-permute-start.37 = (f32[128,128]{1,0:T(8,128)S(1)}, f32[128,128]{1,0:T(8,128)S(1)}, u32[]{:S(2)}, u32[]{:S(2)}) collective-permute-start(f32[128,128]{1,0:T(8,128)S(1)} %add.294), channel_id=1, source_target_pairs={{0,32},{1,35},{2,34},{3,33},{32,64},{33,67},{34,66},{35,65},{64,96... | collective-permute-start | bytes 196616 | tf_op jit(solution)/shard_map/ppermute | solution.py:353
  212.2 13.9 %collective-permute-done.37.r0 = f32[128,128]{1,0:T(8,128)S(1)} collective-permute-done((f32[128,128]{1,0:T(8,128)S(1)}, f32[128,128]{1,0:T(8,128)S(1)}, u32[]{:S(2)}, u32[]{:S(2)}) %collective-permute-start.37) | collective-permute-done | bytes 65568 | tf_op jit(solution)/shard_map/ppermute | solution.py:353
  234.4 7.1 %collective-permute-done.40.r0 = f32[128,128]{1,0:T(8,128)S(1)} collective-permute-done((f32[128,128]{1,0:T(8,128)S(1)}, f32[128,128]{1,0:T(8,128)S(1)}, u32[]{:S(2)}, u32[]{:S(2)}) %collective-permute-start.40) | collective-permute-done | bytes 65568 | tf_op jit(solution)/shard_map/ppermute | solution.py:353
  245.9 4.1 %shard_map.97 = (bf16[32,3584]{1,0:T(8,128)(2,1)S(1)}, bf16[32,3584]{1,0:T(8,128)(2,1)S(1)}, bf16[64,3584]{1,0:T(8,128)(2,1)S(1)}) custom-call(bf16[128,3584]{1,0:T(8,128)(2,1)S(1)} %collective-permute-done.43.refs_0_.refs_11_, bf16[128,3584]{1,0:T(8,128)(2,1)} %collective-permute-done.44.refs_1_.refs_9_.refs_12_, ...), custom_call_target="tpu_custom_call" | custom-call | tf_op jit(solution)/shard_map/pallas_call | solution.py:220
  254.8 11.8 %collective-permute-done.47.r0 = f32[128,128]{1,0:T(8,128)S(1)} collective-permute-done((f32[128,128]{1,0:T(8,128)S(1)}, f32[128,128]{1,0:T(8,128)S(1)}, u32[]{:S(2)}, u32[]{:S(2)}) %collective-permute-start.47) | collective-permute-done | bytes 65568 | tf_op jit(solution)/shard_map/ppermute | solution.py:353
  280.3 6.3 %collective-permute-done.56.r0 = f32[128,128]{1,0:T(8,128)S(1)} collective-permute-done((f32[128,128]{1,0:T(8,128)}, f32[128,128]{1,0:T(8,128)S(1)}, u32[]{:S(2)}, u32[]{:S(2)}) %collective-permute-start.56) | collective-permute-done | bytes 65568 | tf_op jit(solution)/shard_map/ppermute | solution.py:353
  291.6 9.9 %shard_map.98 = (bf16[1024,512]{1,0:T(8,128)(2,1)}, bf16[512,3584]{1,0:T(8,128)(2,1)}, bf16[512,3584]{1,0:T(8,128)(2,1)}) custom-call(s32[8]{0:T(128)S(1)} %stack.35.place_ref, bf16[4,256,1024]{2,1,0:T(8,128)(2,1)} %refs_3_.7, bf16[4,256,1024]{2,1,0:T(8,128)(2,1)} %refs_3_.7, bf16[4,256,1024]{2,1,0:T(8,128)(2,1)} %refs_3_.7, bf16[4,256,1024]{2,1,0:T(8,128)(2,1)} %refs_3_.7, ...), custom_call_target="tpu_custom_call" | custom-call | tf_op jit(solution)/shard_map/pallas_call | solution.py:264
  305.0 4.1 %all-to-all-start = ((f32[8,128,128]{2,1,0:T(8,128)}), f32[8,128,128]{2,1,0:T(8,128)}, u32[]{:S(2)}, u32[]{:S(2)}) async-start(f32[8,128,128]{2,1,0:T(8,128)} %broadcast_in_dim.12), calls=%async_computation | async-start | bytes 1048576 | tf_op jit(solution)/shard_map/all_to_all | solution.py:499
  316.0 10.0 %shard_map.100 = (bf16[1024,512]{1,0:T(8,128)(2,1)}, bf16[512,3584]{1,0:T(8,128)(2,1)}, bf16[512,3584]{1,0:T(8,128)(2,1)}) custom-call(s32[8]{0:T(128)S(1)} %stack.35.place_ref, bf16[4,256,1024]{2,1,0:T(8,128)(2,1)} %refs_3_.7, bf16[4,256,1024]{2,1,0:T(8,128)(2,1)} %refs_3_.7, bf16[4,256,1024]{2,1,0:T(8,128)(2,1)} %refs_3_.7, bf16[4,256,1024]{2,1,0:T(8,128)(2,1)} %refs_3_.7, ...), custom_call_target="tpu_custom_call" | custom-call | tf_op jit(solution)/shard_map/pallas_call | solution.py:264
  329.2 17.3 %shard_map.101 = (bf16[1024,3584]{1,0:T(8,128)(2,1)}, f32[3584,128]{1,0:T(8,128)}) custom-call(s32[8]{0:T(128)S(1)} %stack.35.place_ref, f32[8,128,128]{2,1,0:T(8,128)} %all-to-all-done.g_ref, bf16[128,3584]{1,0:T(8,128)(2,1)S(1)} %bitcast.38, bf16[1024,512]{1,0:T(8,128)(2,1)S(1)} %copy-done.11, bf16[512,3584]{1,0:T(8,128)(2,1)} %get-tuple-element.119.hidden0, ...), custom_call_target="tpu_custom_call" | custom-call | tf_op jit(solution)/shard_map/pallas_call | solution.py:315
  (244 shorter events, 116.6 us)
Async XLA Ops:
  17.5 22.8 %collective-permute-start.9 = (bf16[8,3584]{1,0:T(8,128)(2,1)}, bf16[8,3584]{1,0:T(8,128)(2,1)S(1)}, u32[]{:S(2)}, u32[]{:S(2)}) collective-permute-start(bf16[8,3584]{1,0:T(8,128)(2,1)} %get-tuple-element.150), channel_id=1, source_target_pairs={{0,8},{4,12},{8,16},{12,20},{16,24},{20,28},{24,0},{28,4},{1,9},{5... | collective-permute-start | bytes 172040 | tf_op jit(solution)/shard_map/ppermute | solution.py:335
  21.6 22.5 %collective-permute-start = (bf16[32,3584]{1,0:T(8,128)(2,1)}, bf16[32,3584]{1,0:T(8,128)(2,1)}, u32[]{:S(2)}, u32[]{:S(2)}) collective-permute-start(bf16[32,3584]{1,0:T(8,128)(2,1)} %get-tuple-element.156), channel_id=1, source_target_pairs={{0,8},{4,12},{8,16},{12,20},{16,24},{20,28},{24,0},{28,4},{1,9},{5... | collective-permute-start | bytes 688136 | tf_op jit(solution)/shard_map/ppermute | solution.py:335
  21.8 23.4 %collective-permute-start.5 = (bf16[32,3584]{1,0:T(8,128)(2,1)}, bf16[32,3584]{1,0:T(8,128)(2,1)}, u32[]{:S(2)}, u32[]{:S(2)}) collective-permute-start(bf16[32,3584]{1,0:T(8,128)(2,1)} %get-tuple-element.157), channel_id=1, source_target_pairs={{0,24},{4,28},{8,0},{12,4},{16,8},{20,12},{24,16},{28,20},{1,25},{... | collective-permute-start | bytes 688136 | tf_op jit(solution)/shard_map/ppermute | solution.py:335
  25.1 29.1 %collective-permute-start.4 = (bf16[64,3584]{1,0:T(8,128)(2,1)}, bf16[64,3584]{1,0:T(8,128)(2,1)}, u32[]{:S(2)}, u32[]{:S(2)}) collective-permute-start(bf16[64,3584]{1,0:T(8,128)(2,1)} %slice.82), channel_id=1, source_target_pairs={{0,4},{4,0},{8,12},{12,8},{16,20},{20,16},{24,28},{28,24},{1,5},{5... | collective-permute-start | bytes 1376264 | tf_op jit(solution)/shard_map/ppermute | solution.py:335
  44.0 32.7 %collective-permute-start.2 = (bf16[128,3584]{1,0:T(8,128)(2,1)S(1)}, bf16[128,3584]{1,0:T(8,128)(2,1)S(1)}, u32[]{:S(2)}, u32[]{:S(2)}) collective-permute-start(bf16[128,3584]{1,0:T(8,128)(2,1)S(1)} %pad_maximum_fusion.1), channel_id=1, source_target_pairs={{0,4},{4,0},{8,12},{12,8},{16,20},{20,16},{24,28},{28,24},{1,5},{5... | collective-permute-start | bytes 2752520 | tf_op jit(solution)/shard_map/ppermute | solution.py:335
  49.0 27.8 %collective-permute-start.1 = (bf16[128,3584]{1,0:T(8,128)(2,1)S(1)}, bf16[128,3584]{1,0:T(8,128)(2,1)S(1)}, u32[]{:S(2)}, u32[]{:S(2)}) collective-permute-start(bf16[128,3584]{1,0:T(8,128)(2,1)S(1)} %pad_maximum_fusion), channel_id=1, source_target_pairs={{0,8},{4,12},{8,16},{12,20},{16,24},{20,28},{24,0},{28,4},{1,9},{5... | collective-permute-start | bytes 2752520 | tf_op jit(solution)/shard_map/ppermute | solution.py:335
  50.4 26.2 %collective-permute-start.12 = (bf16[32,3584]{1,0:T(8,128)(2,1)S(1)}, bf16[32,3584]{1,0:T(8,128)(2,1)S(1)}, u32[]{:S(2)}, u32[]{:S(2)}) collective-permute-start(bf16[32,3584]{1,0:T(8,128)(2,1)S(1)} %add_convert_fusion.9), channel_id=1, source_target_pairs={{0,8},{4,12},{8,16},{12,20},{16,24},{20,28},{24,0},{28,4},{1,9},{5... | collective-permute-start | bytes 688136 | tf_op jit(solution)/shard_map/ppermute | solution.py:335
  51.0 25.6 %collective-permute-start.16 = (bf16[32,3584]{1,0:T(8,128)(2,1)S(1)}, bf16[32,3584]{1,0:T(8,128)(2,1)S(1)}, u32[]{:S(2)}, u32[]{:S(2)}) collective-permute-start(bf16[32,3584]{1,0:T(8,128)(2,1)S(1)} %add_convert_fusion.8), channel_id=1, source_target_pairs={{0,24},{4,28},{8,0},{12,4},{16,8},{20,12},{24,16},{28,20},{1,25},{... | collective-permute-start | bytes 688136 | tf_op jit(solution)/shard_map/ppermute | solution.py:335
  54.2 22.4 %collective-permute-start.17 = (bf16[32,3584]{1,0:T(8,128)(2,1)S(1)}, bf16[32,3584]{1,0:T(8,128)(2,1)S(1)}, u32[]{:S(2)}, u32[]{:S(2)}) collective-permute-start(bf16[32,3584]{1,0:T(8,128)(2,1)S(1)} %add_convert_fusion.7), channel_id=1, source_target_pairs={{0,4},{4,0},{8,12},{12,8},{16,20},{20,16},{24,28},{28,24},{1,5},{5... | collective-permute-start | bytes 688136 | tf_op jit(solution)/shard_map/ppermute | solution.py:335
  77.3 48.5 %collective-permute-start.3 = (bf16[128,3584]{1,0:T(8,128)(2,1)S(1)}, bf16[128,3584]{1,0:T(8,128)(2,1)S(1)}, u32[]{:S(2)}, u32[]{:S(2)}) collective-permute-start(bf16[128,3584]{1,0:T(8,128)(2,1)S(1)} %add_convert_fusion.2), channel_id=1, source_target_pairs={{0,8},{4,12},{8,16},{12,20},{16,24},{20,28},{24,0},{28,4},{1,9},{5... | collective-permute-start | bytes 2752520 | tf_op jit(solution)/shard_map/ppermute | solution.py:335
  94.8 31.0 %collective-permute-start.7 = (bf16[128,3584]{1,0:T(8,128)(2,1)S(1)}, bf16[128,3584]{1,0:T(8,128)(2,1)S(1)}, u32[]{:S(2)}, u32[]{:S(2)}) collective-permute-start(bf16[128,3584]{1,0:T(8,128)(2,1)S(1)} %add_convert_fusion.1), channel_id=1, source_target_pairs={{0,24},{4,28},{8,0},{12,4},{16,8},{20,12},{24,16},{28,20},{1,25},{... | collective-permute-start | bytes 2752520 | tf_op jit(solution)/shard_map/ppermute | solution.py:335
  96.6 29.3 %collective-permute-start.8 = (bf16[128,3584]{1,0:T(8,128)(2,1)S(1)}, bf16[128,3584]{1,0:T(8,128)(2,1)S(1)}, u32[]{:S(2)}, u32[]{:S(2)}) collective-permute-start(bf16[128,3584]{1,0:T(8,128)(2,1)S(1)} %add_convert_fusion), channel_id=1, source_target_pairs={{0,4},{4,0},{8,12},{12,8},{16,20},{20,16},{24,28},{28,24},{1,5},{5... | collective-permute-start | bytes 2752520 | tf_op jit(solution)/shard_map/ppermute | solution.py:335
  98.4 21.3 %collective-permute-start.20 = (bf16[32,4608]{1,0:T(8,128)(2,1)S(1)}, bf16[32,4608]{1,0:T(8,128)(2,1)S(1)}, u32[]{:S(2)}, u32[]{:S(2)}) collective-permute-start(bf16[32,4608]{1,0:T(8,128)(2,1)S(1)} %pad_maximum_fusion.3.refs_0_), channel_id=1, source_target_pairs={{0,24},{4,28},{8,0},{12,4},{16,8},{20,12},{24,16},{28,20},{1,25},{... | collective-permute-start | bytes 884744 | tf_op jit(solution)/shard_map/ppermute | solution.py:335
  99.2 22.0 %collective-permute-start.19 = (bf16[32,4608]{1,0:T(8,128)(2,1)S(1)}, bf16[32,4608]{1,0:T(8,128)(2,1)S(1)}, u32[]{:S(2)}, u32[]{:S(2)}) collective-permute-start(bf16[32,4608]{1,0:T(8,128)(2,1)S(1)} %pad_maximum_fusion.3.refs_0_), channel_id=1, source_target_pairs={{0,8},{4,12},{8,16},{12,20},{16,24},{20,28},{24,0},{28,4},{1,9},{5... | collective-permute-start | bytes 884744 | tf_op jit(solution)/shard_map/ppermute | solution.py:335
  126.3 70.4 %collective-permute-start.36 = (bf16[128,3584]{1,0:T(8,128)(2,1)S(1)}, bf16[128,3584]{1,0:T(8,128)(2,1)}, u32[]{:S(2)}, u32[]{:S(2)}) collective-permute-start(bf16[128,3584]{1,0:T(8,128)(2,1)S(1)} %get-tuple-element.132.refs_8_), channel_id=1, source_target_pairs={{0,4},{4,0},{8,12},{12,8},{16,20},{20,16},{24,28},{28,24},{1,5},{5... | collective-permute-start | bytes 2752520 | tf_op jit(solution)/shard_map/ppermute | solution.py:335
  127.9 68.8 %collective-permute-start.35 = (bf16[128,3584]{1,0:T(8,128)(2,1)S(1)}, bf16[128,3584]{1,0:T(8,128)(2,1)}, u32[]{:S(2)}, u32[]{:S(2)}) collective-permute-start(bf16[128,3584]{1,0:T(8,128)(2,1)S(1)} %get-tuple-element.132.refs_8_), channel_id=1, source_target_pairs={{0,24},{4,28},{8,0},{12,4},{16,8},{20,12},{24,16},{28,20},{1,25},{... | collective-permute-start | bytes 2752520 | tf_op jit(solution)/shard_map/ppermute | solution.py:335
  130.5 66.2 %collective-permute-start.34 = (bf16[128,3584]{1,0:T(8,128)(2,1)S(1)}, bf16[128,3584]{1,0:T(8,128)(2,1)}, u32[]{:S(2)}, u32[]{:S(2)}) collective-permute-start(bf16[128,3584]{1,0:T(8,128)(2,1)S(1)} %get-tuple-element.132.refs_8_), channel_id=1, source_target_pairs={{0,8},{4,12},{8,16},{12,20},{16,24},{20,28},{24,0},{28,4},{1,9},{5... | collective-permute-start | bytes 2752520 | tf_op jit(solution)/shard_map/ppermute | solution.py:335
  202.4 43.5 %collective-permute-start.43 = (bf16[128,3584]{1,0:T(8,128)(2,1)}, bf16[128,3584]{1,0:T(8,128)(2,1)S(1)}, u32[]{:S(2)}, u32[]{:S(2)}) collective-permute-start(bf16[128,3584]{1,0:T(8,128)(2,1)} %get-tuple-element.95), channel_id=1, source_target_pairs={{0,8},{4,12},{8,16},{12,20},{16,24},{20,28},{24,0},{28,4},{1,9},{5... | collective-permute-start | bytes 2752520 | tf_op jit(solution)/shard_map/ppermute | solution.py:335
  202.4 43.5 %collective-permute-start.44 = (bf16[128,3584]{1,0:T(8,128)(2,1)}, bf16[128,3584]{1,0:T(8,128)(2,1)}, u32[]{:S(2)}, u32[]{:S(2)}) collective-permute-start(bf16[128,3584]{1,0:T(8,128)(2,1)} %get-tuple-element.96), channel_id=1, source_target_pairs={{0,24},{4,28},{8,0},{12,4},{16,8},{20,12},{24,16},{28,20},{1,25},{... | collective-permute-start | bytes 2752520 | tf_op jit(solution)/shard_map/ppermute | solution.py:335
  205.1 40.8 %collective-permute-start.45 = (bf16[128,3584]{1,0:T(8,128)(2,1)}, bf16[128,3584]{1,0:T(8,128)(2,1)}, u32[]{:S(2)}, u32[]{:S(2)}) collective-permute-start(bf16[128,3584]{1,0:T(8,128)(2,1)} %get-tuple-element.97), channel_id=1, source_target_pairs={{0,4},{4,0},{8,12},{12,8},{16,20},{20,16},{24,28},{28,24},{1,5},{5... | collective-permute-start | bytes 2752520 | tf_op jit(solution)/shard_map/ppermute | solution.py:335
  250.0 28.2 %collective-permute-start.52 = (bf16[64,3584]{1,0:T(8,128)(2,1)S(1)}, bf16[64,3584]{1,0:T(8,128)(2,1)S(1)}, u32[]{:S(2)}, u32[]{:S(2)}) collective-permute-start(bf16[64,3584]{1,0:T(8,128)(2,1)S(1)} %get-tuple-element.106), channel_id=1, source_target_pairs={{0,4},{4,0},{8,12},{12,8},{16,20},{20,16},{24,28},{28,24},{1,5},{5... | collective-permute-start | bytes 1376264 | tf_op jit(solution)/shard_map/ppermute | solution.py:335
  252.1 24.8 %collective-permute-start.50 = (bf16[32,3584]{1,0:T(8,128)(2,1)S(1)}, bf16[32,3584]{1,0:T(8,128)(2,1)S(1)}, u32[]{:S(2)}, u32[]{:S(2)}) collective-permute-start(bf16[32,3584]{1,0:T(8,128)(2,1)S(1)} %get-tuple-element.104), channel_id=1, source_target_pairs={{0,8},{4,12},{8,16},{12,20},{16,24},{20,28},{24,0},{28,4},{1,9},{5... | collective-permute-start | bytes 688136 | tf_op jit(solution)/shard_map/ppermute | solution.py:335
  252.1 25.4 %collective-permute-start.51 = (bf16[32,3584]{1,0:T(8,128)(2,1)S(1)}, bf16[32,3584]{1,0:T(8,128)(2,1)S(1)}, u32[]{:S(2)}, u32[]{:S(2)}) collective-permute-start(bf16[32,3584]{1,0:T(8,128)(2,1)S(1)} %get-tuple-element.105), channel_id=1, source_target_pairs={{0,24},{4,28},{8,0},{12,4},{16,8},{20,12},{24,16},{28,20},{1,25},{... | collective-permute-start | bytes 688136 | tf_op jit(solution)/shard_map/ppermute | solution.py:335
  305.0 21.8 %all-to-all-start = ((f32[8,128,128]{2,1,0:T(8,128)}), f32[8,128,128]{2,1,0:T(8,128)}, u32[]{:S(2)}, u32[]{:S(2)}) async-start(f32[8,128,128]{2,1,0:T(8,128)} %broadcast_in_dim.12), calls=%async_computation | async-start | bytes 1048576 | tf_op jit(solution)/shard_map/all_to_all | solution.py:499
  (75 other events, 518.8 us)

commit v4 on v3

v4 whole, which is shorter than its diff:
```python
import functools

import jax
import jax.numpy as jnp
from jax import lax
from jax.experimental import pallas as pl
from jax.experimental.pallas import tpu as pltpu
from jax.sharding import PartitionSpec as P

BF = jnp.bfloat16
F32 = jnp.float32
HIGHEST = lax.Precision.HIGHEST
NT = (((1,), (1,)), ((), ()))
CHUNK = 512
X_SIZE = 4
RELATIVE = ((0, 0), (0, 1), (-1, 0), (-1, 1), (1, 0), (1, 1), (2, 0), (2, 1))
EARLY, LATE = (7, 6, 3, 5), (2, 4, 1, 0)
PARAMS = pltpu.CompilerParams(vmem_limit_bytes=48 * 1024 * 1024)
SMALL = pltpu.CompilerParams(vmem_limit_bytes=16 * 1024 * 1024)


def split2(x):
    hi = x.astype(BF)
    return hi, (x - hi.astype(F32)).astype(BF)


def mm(a, b):
    return jnp.dot(a, b, preferred_element_type=F32)


def mm_nt(a, b):
    return lax.dot_general(a, b, NT, preferred_element_type=F32)


def sigma(v):
    return 0.5 * jnp.tanh(0.5 * v) + 0.5


def wide(x):
    return jnp.concatenate(split2(x), axis=1)


def tall(x):
    return jnp.concatenate(split2(x), axis=0)


def twice(x):
    return jnp.concatenate([x, x], axis=0)


def chunks_of(width):
    return [slice(i, i + CHUNK) for i in range(0, width, CHUNK)]


def gram_share(x, gram):
    return 0.25 * jnp.dot(x, gram, precision=HIGHEST, preferred_element_type=F32)


def first_kernel(base_ref, down_ref, part_ref):
    acc = jnp.zeros(part_ref.shape, F32)
    for cols in chunks_of(base_ref.shape[1]):
        pre = base_ref[:, cols].astype(F32)
        hidden = (pre * sigma(pre)).astype(BF)
        acc += mm_nt(hidden, down_ref[:, cols])
    part_ref[...] = acc


def forward_kernel(base_ref, up_ref, down_ref, gram_ref, r0, r1, part_ref):
    c = r0[...] + r1[...]
    cw = wide(c)
    acc = gram_share(c, gram_ref[...])
    for cols in chunks_of(base_ref.shape[1]):
        pre = base_ref[:, cols].astype(F32) + mm(cw, twice(up_ref[:, cols]))
        hidden = (pre * sigma(pre)).astype(BF)
        acc += mm_nt(hidden, down_ref[:, cols])
    part_ref[...] = acc


def middle_kernel(base_ref, up_ref, down_ref, gram_ref, r0, r1, c_ref, part_ref, slope_ref):
    c = r0[...] + r1[...]
    c_ref[...] = c.astype(BF)
    cw = wide(c)
    acc = gram_share(c, gram_ref[...])
    for cols in chunks_of(base_ref.shape[1]):
        pre = base_ref[:, cols].astype(F32) + mm(cw, twice(up_ref[:, cols]))
        sig = sigma(pre)
        hidden = (pre * sig).astype(BF)
        slope_ref[:, cols] = (sig * (1.0 + pre * (1.0 - sig))).astype(BF)
        acc += mm_nt(hidden, down_ref[:, cols])
    part_ref[...] = acc


def backward_kernel(last_ref, slope_ref, up_ref, down_ref, gram_ref, cot_ref, r0, r1, g_ref, part_ref):
    g = jnp.where(last_ref[0] == 1, cot_ref[...], r0[...] + r1[...])
    g_ref[...] = g
    gw = wide(g)
    acc = gram_share(g, gram_ref[...])
    for cols in chunks_of(slope_ref.shape[1]):
        g_pre = mm(gw, twice(down_ref[:, cols])) * slope_ref[:, cols].astype(F32)
        hi, lo = split2(g_pre)
        acc += mm_nt(hi, up_ref[:, cols]) + mm_nt(lo, up_ref[:, cols])
    part_ref[...] = acc


def call(kernel, outs, *args):
    return pl.pallas_call(kernel, out_shape=outs, compiler_params=SMALL)(*args)


def base_specs(base, dp, blocks):
    micro, tokens, width = base.shape
    return [
        pl.BlockSpec((micro, tokens // dp, width), lambda i, p, j=j: (0, p[j], 0)) for j in blocks
    ]


def product_kernel(count, place_ref, *refs):
    bases, w_ref, outs, rows = refs[:count], refs[count], refs[count + 1 : -1], refs[-1]
    own = bases[0].shape[0] * bases[0].shape[1]

    @pl.when(pl.program_id(0) == 0)
    def _():
        for j, b in enumerate(bases):
            rows[j * own : (j + 1) * own] = b[...].reshape(own, b.shape[2])

    res = mm(rows[...], w_ref[...])
    for j, out in enumerate(outs):
        out[...] = res[j * own : (j + 1) * own].astype(BF)


def product(place, base, w_in, dp, blocks):
    micro, tokens, width = base.shape
    hid = w_in.shape[1]
    own = micro * tokens // dp
    count = len(blocks)
    column = lambda rows: pl.BlockSpec((rows, CHUNK), lambda i, p: (0, i))
    return pl.pallas_call(
        functools.partial(product_kernel, count),
        out_shape=[jax.ShapeDtypeStruct((own, hid), BF)] * count,
        grid_spec=pltpu.PrefetchScalarGridSpec(
            num_scalar_prefetch=1,
            grid=(hid // CHUNK,),
            in_specs=base_specs(base, dp, blocks) + [column(width)],
            out_specs=[column(own)] * count,
            scratch_shapes=[pltpu.VMEM((own * count, width), BF)],
        ),
        compiler_params=PARAMS,
    )(place, *([base] * count), w_in)


def project_kernel(basis_ref, w_in_ref, w_out_ref, out_ref, wide_ref, tall_ref):
    rank = basis_ref.shape[1]
    count, rows, cols = out_ref.shape
    share = rows // 2

    @pl.when(pl.program_id(0) == 0)
    def _():
        wide_ref[...] = wide(basis_ref[...])
        tall_ref[...] = tall(basis_ref[...].T)

    up = mm(tall_ref[...], w_in_ref[...])
    down = mm(w_out_ref[...], wide_ref[...])
    out_ref[:, :share] = (up[:rank] + up[rank:]).astype(BF).reshape(count, share, cols)
    down = (down[:, :rank] + down[:, rank:]).T
    out_ref[:, share:] = down.astype(BF).reshape(count, share, cols)


def project(basis, w_in, w_out, dp):
    width, rank = basis.shape
    hid = w_in.shape[1]
    rows = 2 * rank // dp
    return pl.pallas_call(
        project_kernel,
        out_shape=jax.ShapeDtypeStruct((dp, rows, hid), BF),
        grid=(hid // CHUNK,),
        in_specs=[
            pl.BlockSpec((width, rank), lambda i: (0, 0)),
            pl.BlockSpec((width, CHUNK), lambda i: (0, i)),
            pl.BlockSpec((CHUNK, width), lambda i: (i, 0)),
        ],
        out_specs=pl.BlockSpec((dp, rows, CHUNK), lambda i: (0, 0, i)),
        scratch_shapes=[pltpu.VMEM((width, 2 * rank), BF), pltpu.VMEM((2 * rank, width), BF)],
        compiler_params=PARAMS,
    )(basis, w_in, w_out)


def assemble_kernel(steps, all_ref, up_ref, down_ref, gram_ref):
    share = up_ref.shape[1]
    step = pl.program_id(0)

    @pl.when(step < steps)
    def _():
        up_ref[...] = all_ref[:, :share]
        down_ref[...] = all_ref[:, share:]

    @pl.when(step >= steps)
    def _():
        total = jnp.sum(all_ref[...].astype(F32), axis=0)
        gram_ref[...] = jnp.where(step == steps, total, gram_ref[...] + total)


def assemble(everyone, hid):
    count, rows, cols = everyone.shape
    steps = hid // CHUNK
    share = rows // 2
    rank = count * share
    spec = pl.BlockSpec((count, share, CHUNK), lambda i: (0, 0, jnp.minimum(i, steps - 1)))
    up, down, gram = pl.pallas_call(
        functools.partial(assemble_kernel, steps),
        out_shape=[jax.ShapeDtypeStruct((count, share, hid), BF)] * 2
        + [jax.ShapeDtypeStruct((rows, CHUNK), F32)],
        grid=(cols // CHUNK,),
        in_specs=[pl.BlockSpec((count, rows, CHUNK), lambda i: (0, 0, i))],
        out_specs=[spec, spec, pl.BlockSpec((rows, CHUNK), lambda i: (0, 0))],
        compiler_params=SMALL,
    )(everyone)
    return up.reshape(rank, hid), down.reshape(rank, hid), gram.reshape(rank, rank)


def copy_kernel(plan, count, *refs):
    for out, parts in zip(refs[count:], plan):
        out[...] = jnp.concatenate([refs[k][a:b] for k, a, b in parts], axis=0)


def copies(arrays, plan):
    hid = arrays[0].shape[1]
    heights = [sum(b - a for _, a, b in parts) for parts in plan]
    column = lambda rows: pl.BlockSpec((rows, CHUNK), lambda i: (0, i))
    return pl.pallas_call(
        functools.partial(copy_kernel, plan, len(arrays)),
        out_shape=[jax.ShapeDtypeStruct((rows, hid), BF) for rows in heights],
        grid=(hid // CHUNK,),
        in_specs=[column(a.shape[0]) for a in arrays],
        out_specs=[column(rows) for rows in heights],
        compiler_params=SMALL,
    )(*arrays)


def prepare_kernel(count, place_ref, *refs):
    bases, refs = refs[:count], refs[count:]
    half = count // 2
    basis_ref, c_refs, up_ref, pieces = refs[0], refs[1 : 1 + half], refs[1 + half], refs[2 + half : -3]
    xt_ref, hidden_ref, slope_ref = refs[-3:]
    own = bases[0].shape[0] * bases[0].shape[1]

    @pl.when(pl.program_id(0) == 0)
    def _():
        basis = basis_ref[...].astype(BF)
        for j, b in enumerate(bases):
            c = c_refs[j // 2][(j % 2) * own : (j % 2 + 1) * own]
            x = b[...].reshape(own, b.shape[2]).astype(F32) + mm_nt(c, basis)
            xt_ref[:, j * own : (j + 1) * own] = x.T.astype(BF)

    up = up_ref[...]
    start = 0
    c_all = jnp.concatenate([c[...] for c in c_refs], axis=0)
    for p in pieces:
        rows = slice(start, start + p.shape[0])
        start += p.shape[0]
        pre = p[...].astype(F32) + mm(c_all[rows], up)
        sig = sigma(pre)
        hidden = pre * sig
        hidden_ref[rows] = hidden.astype(BF)
        slope_ref[rows] = (sig + hidden * (1.0 - sig)).astype(BF)


def prepare(place, base, dp, blocks, basis, c_pieces, up, pieces):
    micro, tokens, width = base.shape
    hid = up.shape[1]
    every = micro * tokens // dp * len(blocks)
    whole = lambda a: pl.BlockSpec(a.shape, lambda i, p: (0, 0))
    column = lambda rows: pl.BlockSpec((rows, CHUNK), lambda i, p: (0, i))
    return pl.pallas_call(
        functools.partial(prepare_kernel, len(blocks)),
        out_shape=[
            jax.ShapeDtypeStruct((width, every), BF),
            jax.ShapeDtypeStruct((every, hid), BF),
            jax.ShapeDtypeStruct((every, hid), BF),
        ],
        grid_spec=pltpu.PrefetchScalarGridSpec(
            num_scalar_prefetch=1,
            grid=(hid // CHUNK,),
            in_specs=base_specs(base, dp, blocks)
            + [whole(basis)]
            + [whole(c) for c in c_pieces]
            + [column(up.shape[0])]
            + piece_specs(pieces),
            out_specs=[
                pl.BlockSpec((width, every), lambda i, p: (0, 0)),
                column(every),
                column(every),
            ],
        ),
        compiler_params=PARAMS,
    )(place, *([base] * len(blocks)), basis, *c_pieces, up, *[a for a, _, _ in pieces])


def finish_kernel(groups, place_ref, g_ref, down_ref, *refs):
    grad_ref, dc_ref, gw, gt = refs[-4:]
    rank = down_ref.shape[0]
    own = g_ref.shape[1]

    @pl.when(pl.program_id(0) == 0)
    def _():
        for j in range(len(RELATIVE)):
            g = g_ref[place_ref[j]]
            gw[j * own : (j + 1) * own] = wide(g)
            gt[:, j * own : (j + 1) * own] = tall(g.T)

    down2 = twice(down_ref[...])
    start, grad, dc = 0, 0.0, 0.0
    for k in range(groups):
        xt, hidden, slope = refs[3 * k : 3 * k + 3]
        stop = start + hidden.shape[0]
        g_pre = (mm(gw[start:stop], down2) * slope[...].astype(F32)).astype(BF)
        grad += mm(xt[...], g_pre)
        dc += mm(gt[:, start:stop], hidden[...])
        start = stop
    grad_ref[...] = grad.astype(BF)
    dc_ref[...] = (dc[:rank] + dc[rank:]).T


def finish(place, g_all, down, groups):
    rank, hid = down.shape
    width = groups[0][0].shape[0]
    every = sum(xt.shape[1] for xt, _, _ in groups)
    column = lambda rows: pl.BlockSpec((rows, CHUNK), lambda i, p: (0, i))
    specs = []
    for xt, hidden, slope in groups:
        specs += [pl.BlockSpec(xt.shape, lambda i, p: (0, 0)), column(hidden.shape[0]), column(hidden.shape[0])]
    return pl.pallas_call(
        functools.partial(finish_kernel, len(groups)),
        out_shape=[jax.ShapeDtypeStruct((width, hid), BF), jax.ShapeDtypeStruct((hid, rank), F32)],
        grid_spec=pltpu.PrefetchScalarGridSpec(
            num_scalar_prefetch=1,
            grid=(hid // CHUNK,),
            in_specs=[pl.BlockSpec(g_all.shape, lambda i, p: (0, 0, 0)), column(rank)] + specs,
            out_specs=[column(width), pl.BlockSpec((CHUNK, rank), lambda i, p: (i, 0))],
            scratch_shapes=[pltpu.VMEM((every, 2 * rank), BF), pltpu.VMEM((2 * rank, every), BF)],
        ),
        compiler_params=PARAMS,
    )(place, g_all, down, *sum((list(g) for g in groups), []))


def to_dp(x, dx, dy):
    size = lax.axis_size("dp")
    pairs = [(i, ((i // 2 + dx) % X_SIZE) * 2 + ((i % 2) ^ dy)) for i in range(size)]
    return lax.ppermute(x, "dp", pairs)


def to_tensor(x, k):
    size = lax.axis_size("tensor")
    return lax.ppermute(x, "tensor", [(t, t ^ k) for t in range(size)])


def hop(part, by, before=(), during=lambda: ()):
    sections, tensors = lax.axis_size("section"), lax.axis_size("tensor")
    pair_sum, before = tie(part + to_tensor(part, 1), before)
    pairs = [
        (s * tensors + t, (s + by) * tensors + (t ^ (2 * (t % 2))))
        for s in range(sections)
        for t in range(tensors)
        if 0 <= s + by < sections
    ]
    got = lax.ppermute(pair_sum, ("section", "tensor"), pairs)
    got, made = tie(got, during(*before))
    return (got, to_tensor(got, 1)), before, made


def cat(*xs):
    return jnp.concatenate(xs, axis=0)


def plus(x, *ys):
    total = x.astype(F32)
    for start, y in ys:
        pads = ((start, x.shape[0] - start - y.shape[0]), (0, 0))
        total = total + jnp.pad(y.astype(F32), pads)
    return total.astype(x.dtype)


def reduce_blocks(blocks):
    b = dict(zip(RELATIVE, blocks))
    n = blocks[0].shape[0]
    h, q = n // 2, n // 4
    far = b[2, 1]
    u0, u1, v = to_dp(far[:q], 1, 0), to_dp(far[q:h], -1, 0), to_dp(far[h:], 0, 1)
    up = to_dp(cat(b[2, 0][:h], plus(b[1, 1][:h], (0, u0))), 1, 0)
    down = to_dp(cat(plus(b[2, 0][h:], (0, v)), plus(b[-1, 1][:h], (q, u1))), -1, 0)
    side = to_dp(cat(b[1, 1][h:], b[-1, 1][h:]), 0, 1)
    e1 = to_dp(plus(b[1, 0], (0, up[:h]), (h, side[:h])), 1, 0)
    e2 = to_dp(plus(b[-1, 0], (h, down[:h]), (h, side[h:])), -1, 0)
    e3 = to_dp(plus(b[0, 1], (0, up[h:]), (0, down[h:])), 0, 1)
    f = lambda a: a.astype(F32)
    return (f(b[0, 0]) + f(e1)) + (f(e2) + f(e3))


def swap(x):
    return lax.all_to_all(x, "dp", 0, 0, tiled=True)


def whole(a):
    return a, 0, a.shape[0]


def low_half(a):
    return a, 0, a.shape[0] // 2


def high_half(a):
    return a, 1, a.shape[0] // 2


def piece_specs(pieces):
    return [pl.BlockSpec((n, CHUNK), lambda i, p, k=k: (k, i)) for _, k, n in pieces]


def tie(*xs):
    return lax.optimization_barrier(xs)


def on_device(base, w_in, w_out, basis, cotangent):
    dp = lax.axis_size("dp")
    sections = lax.axis_size("section")
    last = (lax.axis_index("section") == sections - 1).astype(jnp.int32).reshape(1)
    d = lax.axis_index("dp")
    place = jnp.stack(
        [((d // 2 + dx) % X_SIZE) * 2 + (d % 2 + dy) % 2 for dx, dy in RELATIVE]
    ).astype(jnp.int32)
    micro, tokens, width = base.shape
    rows = tokens // dp
    own = micro * rows
    rank = basis.shape[1]
    w_in, w_out = w_in[0], w_out[0]
    hid = w_in.shape[1]
    tok = jax.ShapeDtypeStruct((own, rank), F32)

    share = rank // dp
    proj = swap(project(basis, w_in, w_out, dp))
    proj = jnp.sum(proj.astype(F32), axis=0).astype(BF)
    gram_part = lax.dot_general(basis, basis, (((0,), (0,)), ((), ())), precision=HIGHEST)
    gram_part = split2(gram_part.reshape(2 * share, -1))
    proj = jnp.concatenate([proj, *gram_part], axis=1)
    proj = swap(jnp.broadcast_to(proj[None], (dp,) + proj.shape))
    blocks = [None] * len(RELATIVE)
    for group in (EARLY, LATE):
        for j, block in zip(group, product(place, base, w_in, dp, group)):
            blocks[j] = block
    own_pre = reduce_blocks(blocks).astype(BF)
    up, down, gram = assemble(proj, hid)

    h, q = own // 2, own // 4
    left, right = to_dp(own_pre, 1, 0), to_dp(own_pre, -1, 0)
    part = call(first_kernel, tok, own_pre, down)
    got, _, (low,) = hop(part, 1, (own_pre,), lambda a: copies([a], [[(0, 0, h)]]))
    side_low = to_dp(low, 0, 1)
    part = call(forward_kernel, tok, own_pre, up, down, gram, *got)
    got, _, (high,) = hop(part, 1, (own_pre,), lambda a: copies([a], [[(0, h, own)]]))
    side_high = to_dp(high, 0, 1)
    part = call(forward_kernel, tok, own_pre, up, down, gram, *got)
    got, (left, right, side_low), made = hop(
        part,
        1,
        (left, right, side_low),
        lambda *a: copies(a, [[(0, h, own)], [(2, 0, h), (0, 0, h)], [(2, 0, h), (1, h, own)]]),
    )
    left_high = to_dp(made[0], 0, 1)
    two_left, two_right = to_dp(made[1], 1, 0), to_dp(made[2], -1, 0)
    c_in, coef_part, slope = call(
        middle_kernel,
        (jax.ShapeDtypeStruct((own, rank), BF), tok, jax.ShapeDtypeStruct((own, hid), BF)),
        own_pre, up, down, gram, *got,
    )
    cot = cotangent.reshape(own, rank)

    def back(got):
        return call(backward_kernel, (tok, tok), last, slope, up, down, gram, cot, *got)

    c_side = to_dp(c_in, 0, 1)
    _, part = back((cot, cot))
    got, _, (high,) = hop(part, -1, (right,), lambda a: copies([a], [[(0, h, own)]]))
    (got, c_side) = tie(got, c_side)
    c_pair = cat(c_in, c_side)
    c_right, c_left, c_far = [to_dp(c_pair, dx, 0) for dx in (-1, 1, 2)]
    right_high = to_dp(high, 0, 1)
    _, part = back(got)

    def second(two_left, two_right, side_high, c_pair):
        made = copies(
            [two_left, two_right], [[(1, h, own)], [(0, 0, q)], [(1, q, h)]]
        )
        pieces = [whole(own_pre), whole(side_low), whole(side_high)]
        return made, prepare(place, base, dp, range(2), basis, [c_pair], up, pieces)

    got, (two_left, two_right, side_high, c_pair), (made, zero) = hop(
        part, -1, (two_left, two_right, side_high, c_pair), second
    )
    far_high = to_dp(made[0], 0, 1)
    far_0, far_1 = to_dp(made[1], 1, 0), to_dp(made[2], -1, 0)
    _, part = back(got)

    def third(left_high, right_high, c_left, c_right):
        pieces = [
            whole(left), low_half(two_left), whole(left_high),
            whole(right), low_half(two_right), whole(right_high),
        ]
        return prepare(place, base, dp, range(2, 6), basis, [c_left, c_right], up, pieces)

    got, _, one = hop(part, -1, (left_high, right_high, c_left, c_right), third)
    g_out = jnp.where(last[0] == 1, cot, got[0] + got[1])
    g_all = swap(jnp.broadcast_to(g_out[None], (dp, own, rank)))
    pieces = [high_half(two_left), high_half(two_right), whole(far_0), whole(far_1), whole(far_high)]
    two = prepare(place, base, dp, range(6, 8), basis, [c_far], up, pieces)
    _, grad_part = back(got)
    grad_up, down_coefs = finish(place, g_all, down, [zero, one, two])
    parts = cat(coef_part, grad_part)
    parts = parts + to_tensor(parts, 1)
    parts = (parts + to_tensor(parts, 2)).reshape(2, 1, micro, rows, rank)
    return parts[0], parts[1], grad_up[None], down_coefs[None]


def solution(mesh):
    return jax.shard_map(
        on_device,
        mesh=mesh,
        in_specs=(
            P(None, None, "dp"),
            P("section", "dp", "tensor"),
            P("section", "tensor", "dp"),
            P("dp", None),
            P(None, "dp", None),
        ),
        out_specs=(
            P("section", None, "dp", None),
            P("section", None, "dp", None),
            P("section", "dp", "tensor"),
            P("section", "tensor", None),
        ),
        check_vma=False,
    )
```

time: 348 us -> 311 us (0.89)
  waiting for transfers between devices: 144 us -> 89.6 us
  Pallas kernels: 82.2 us -> 103 us
  starting transfers between devices: 84.3 us -> 72.5 us
  local copies, waits for them, and re-layouts: 25.4 us -> 29.2 us
    ppermute x40 -> x24, waiting for transfers between devices: 91.6 us -> 54.6 us  [to_dp(): return lax.ppermute(x, 'dp', pairs)]
    ppermute x6, waiting for transfers between devices: 41.7 us -> 19.4 us  [hop(): got = lax.ppermute(pair_sum, ('section', 'tensor'), pairs)]
    ppermute x40 -> x24, starting transfers between devices: 41.3 us -> 23.7 us  [to_dp(): return lax.ppermute(x, 'dp', pairs)]
    all_to_all x1 -> x3, starting transfers between devices: 4.14 us -> 14 us  [swap(): return lax.all_to_all(x, 'dp', 0, 0, tiled=True)]
    pallas_call x4 -> x5, Pallas kernels: 10.5 us -> 16.9 us  [copies(): pl.pallas_call(functools.partial(copy_kernel, plan, len(arrays)), out_sha...]
    pallas_call x3 -> x4, Pallas kernels: 39 us -> 45.3 us  [the longest x1 18.2 us: finish(): pl.pallas_call(functools.partial(finish_kernel, len(groups)), out_shape=[...]
    all_to_all x1 -> x3, waiting for transfers between devices: 0.01 us -> 5.81 us  [swap(): return lax.all_to_all(x, 'dp', 0, 0, tiled=True)]
    pallas_call x2 -> x3, Pallas kernels: 19.9 us -> 24.9 us  [prepare(): pl.pallas_call(functools.partial(prepare_kernel, len(blocks)), out_shape=...]
  transfers between devices with their start and end apart: 61 -> 47, of which waited for: 29 -> 24; matrix products, arithmetic and copies ran while one was open for 4% -> 7% of each run, Pallas kernels for 12% -> 24%
where the time goes in v4:
time: 311 us; the launch traced here: 308 us
  Pallas kernels  103 us (33%)
  waiting for transfers between devices  89.6 us (29%)
  starting transfers between devices  72.5 us (23%)
  local copies, waits for them, and re-layouts  29.2 us (9%)
  other arithmetic  11.1 us (4%)
    ppermute x24, waiting for transfers between devices, to_dp(): return lax.ppermute(x, 'dp', pairs)  54.6 us
    pallas_call x3, Pallas kernels, prepare(): pl.pallas_call(functools.partial(prepare_kernel, len(blocks)), out_shape=...  24.9 us
    ppermute x24, starting transfers between devices, to_dp(): return lax.ppermute(x, 'dp', pairs)  23.7 us
    ppermute x6, starting transfers between devices, hop(): got = lax.ppermute(pair_sum, ('section', 'tensor'), pairs)  21.6 us
    unnamed x84, local copies, waits for them, and re-layouts  21.1 us
    ppermute x6, waiting for transfers between devices, hop(): got = lax.ppermute(pair_sum, ('section', 'tensor'), pairs)  19.4 us
    pallas_call x1, Pallas kernels, finish(): pl.pallas_call(functools.partial(finish_kernel, len(groups)), out_shape=[...  18.2 us
    pallas_call x2, Pallas kernels, product(): pl.pallas_call(functools.partial(product_kernel, count), out_shape=[jax.S...  17.3 us
  transfers between devices with their start and end apart: 47, of which 24 were waited for; matrix products, arithmetic and copies ran while one was open for 7% of the time, Pallas kernels for 24%

profile of v4, /device:TPU:1, one launch (start us, length us, event | category | flops | bytes accessed | tf_op | source)
XLA Modules:
  0.0 308.4 jit_solution(5324340921826169563)
XLA Ops:
  1.7 9.8 %shard_map.86 = bf16[8,32,3584]{2,1,0:T(8,128)(2,1)S(1)} custom-call(f32[1024,128]{1,0:T(8,128)S(1)} %copy-done.1, bf16[1024,3584]{1,0:T(8,128)(2,1)} %bitcast.46, bf16[3584,1024]{1,0:T(8,128)(2,1)} %bitcast.49), custom_call_target="tpu_custom_call" | custom-call | tf_op jit(solution)/shard_map/pallas_call | solution.py:171
  12.7 6.0 %all-to-all-start = ((bf16[8,32,3584]{2,1,0:T(8,128)(2,1)}), bf16[8,32,3584]{2,1,0:T(8,128)(2,1)}, u32[]{:S(2)}, u32[]{:S(2)}) async-start(bf16[8,32,3584]{2,1,0:T(8,128)(2,1)} %copy-done.5), calls=%async_computation | async-start | bytes 3670016 | tf_op jit(solution)/shard_map/all_to_all | solution.py:398
  18.8 8.7 %shard_map.85 = (bf16[128,3584]{1,0:T(8,128)(2,1)S(1)}, bf16[128,3584]{1,0:T(8,128)(2,1)S(1)}, bf16[128,3584]{1,0:T(8,128)(2,1)S(1)}, bf16[128,3584]{1,0:T(8,128)(2,1)S(1)}) custom-call(s32[8]{0:T(128)S(1)} %stack.35.place_ref, bf16[4,256,1024]{2,1,0:T(8,128)(2,1)S(1)} %copy-done, bf16[4,256,1024]{2,1,0:T(8,128)(2,1)S(1)} %copy-done, ...), custom_call_target="tpu_custom_call" | custom-call | tf_op jit(solution)/shard_map/pallas_call | solution.py:136
  36.1 8.7 %shard_map.84 = (bf16[128,3584]{1,0:T(8,128)(2,1)S(1)}, bf16[128,3584]{1,0:T(8,128)(2,1)S(1)}, bf16[128,3584]{1,0:T(8,128)(2,1)S(1)}, bf16[128,3584]{1,0:T(8,128)(2,1)S(1)}) custom-call(s32[8]{0:T(128)S(1)} %stack.35.place_ref, bf16[4,256,1024]{2,1,0:T(8,128)(2,1)S(1)} %copy-done, bf16[4,256,1024]{2,1,0:T(8,128)(2,1)S(1)} %copy-done, ...), custom_call_target="tpu_custom_call" | custom-call | tf_op jit(solution)/shard_map/pallas_call | solution.py:136
  56.8 14.6 %collective-permute-done.2 = bf16[128,3584]{1,0:T(8,128)(2,1)} collective-permute-done((bf16[128,3584]{1,0:T(8,128)(2,1)}, bf16[128,3584]{1,0:T(8,128)(2,1)}, u32[]{:S(2)}, u32[]{:S(2)}) %collective-permute-start.2) | collective-permute-done | bytes 917536 | tf_op jit(solution)/shard_map/ppermute | solution.py:347
  84.4 4.5 %all-to-all-start.1 = ((bf16[8,32,4608]{2,1,0:T(8,128)(2,1)}), bf16[8,32,4608]{2,1,0:T(8,128)(2,1)}, u32[]{:S(2)}, u32[]{:S(2)}) async-start(bf16[8,32,4608]{2,1,0:T(8,128)(2,1)} %broadcast_in_dim.8), calls=%async_computation.1 | async-start | bytes 4718592 | tf_op jit(solution)/shard_map/all_to_all | solution.py:398
  88.9 4.4 %collective-permute-done.3 = bf16[128,3584]{1,0:T(8,128)(2,1)S(1)} collective-permute-done((bf16[128,3584]{1,0:T(8,128)(2,1)S(1)}, bf16[128,3584]{1,0:T(8,128)(2,1)S(1)}, u32[]{:S(2)}, u32[]{:S(2)}) %collective-permute-start.3) | collective-permute-done | bytes 917536 | tf_op jit(solution)/shard_map/ppermute | solution.py:347
  95.4 18.9 %collective-permute-done.8 = bf16[128,3584]{1,0:T(8,128)(2,1)} collective-permute-done((bf16[128,3584]{1,0:T(8,128)(2,1)}, bf16[128,3584]{1,0:T(8,128)(2,1)}, u32[]{:S(2)}, u32[]{:S(2)}) %collective-permute-start.8) | collective-permute-done | bytes 917536 | tf_op jit(solution)/shard_map/ppermute | solution.py:347
  117.9 5.8 %all-to-all-done.1.all_ref = bf16[8,32,4608]{2,1,0:T(8,128)(2,1)} async-done(((bf16[8,32,4608]{2,1,0:T(8,128)(2,1)}), bf16[8,32,4608]{2,1,0:T(8,128)(2,1)}, u32[]{:S(2)}, u32[]{:S(2)}) %all-to-all-start.1) | async-done | bytes 2359328 | tf_op jit(solution)/shard_map/all_to_all | solution.py:398
  123.7 5.1 %shard_map.87 = (bf16[8,16,3584]{2,1,0:T(8,128)(2,1)S(1)}, bf16[8,16,3584]{2,1,0:T(8,128)(2,1)S(1)}, f32[32,512]{1,0:T(8,128)S(1)}) custom-call(bf16[8,32,4608]{2,1,0:T(8,128)(2,1)} %all-to-all-done.1.all_ref), custom_call_target="tpu_custom_call" | custom-call | tf_op jit(solution)/shard_map/pallas_call | solution.py:207
  129.3 5.5 %collective-permute-start.9 = (f32[128,128]{1,0:T(8,128)S(1)}, f32[128,128]{1,0:T(8,128)S(1)}, u32[]{:S(2)}, u32[]{:S(2)}) collective-permute-start(f32[128,128]{1,0:T(8,128)S(1)} %shard_map.88), channel_id=1, source_target_pairs={{0,1},{1,0},{2,3},{3,2},{4,5},{5,4},{6,7},{7,6},{8,9},{9,8},{10,11... | collective-permute-start | bytes 196616 | tf_op jit(solution)/shard_map/ppermute | solution.py:352
  135.8 5.9 %collective-permute-start.10 = (f32[128,128]{1,0:T(8,128)S(1)}, f32[128,128]{1,0:T(8,128)S(1)}, u32[]{:S(2)}, u32[]{:S(2)}) collective-permute-start(f32[128,128]{1,0:T(8,128)S(1)} %add.190), channel_id=1, source_target_pairs={{0,32},{1,35},{2,34},{3,33},{32,64},{33,67},{34,66},{35,65},{64,96... | collective-permute-start | bytes 196616 | tf_op jit(solution)/shard_map/ppermute | solution.py:364
  148.2 5.4 %collective-permute-start.13 = (f32[128,128]{1,0:T(8,128)S(1)}, f32[128,128]{1,0:T(8,128)S(1)}, u32[]{:S(2)}, u32[]{:S(2)}) collective-permute-start(f32[128,128]{1,0:T(8,128)S(1)} %add.191), channel_id=1, source_target_pairs={{0,32},{1,35},{2,34},{3,33},{32,64},{33,67},{34,66},{35,65},{64,96... | collective-permute-start | bytes 196616 | tf_op jit(solution)/shard_map/ppermute | solution.py:364
  158.9 6.2 %collective-permute-start.19 = (f32[128,128]{1,0:T(8,128)S(1)}, f32[128,128]{1,0:T(8,128)S(1)}, u32[]{:S(2)}, u32[]{:S(2)}) collective-permute-start(f32[128,128]{1,0:T(8,128)S(1)} %add.192), channel_id=1, source_target_pairs={{0,32},{1,35},{2,34},{3,33},{32,64},{33,67},{34,66},{35,65},{64,96... | collective-permute-start | bytes 196616 | tf_op jit(solution)/shard_map/ppermute | solution.py:364
  165.1 5.2 %shard_map.93 = (bf16[64,3584]{1,0:T(8,128)(2,1)S(1)}, bf16[128,3584]{1,0:T(8,128)(2,1)}, bf16[128,3584]{1,0:T(8,128)(2,1)}) custom-call(bf16[128,3584]{1,0:T(8,128)(2,1)} %collective-permute-done.16.refs_0_.refs_8_, bf16[128,3584]{1,0:T(8,128)(2,1)} %collective-permute-done.17.refs_1_.refs_0_.refs_11_, bf16[64,3584]{1,0:T(8,128)(2,1)} %collective-permute-done.18.refs_2_.refs_6_), custom_call_target="tpu_custom_call" | custom-call | tf_op jit(solution)/shard_map/pallas_call | solution.py:228
  181.4 3.7 %shard_map.96 = bf16[64,3584]{1,0:T(8,128)(2,1)S(1)} custom-call(bf16[128,3584]{1,0:T(8,128)(2,1)} %collective-permute-done.17.refs_1_.refs_0_.refs_11_), custom_call_target="tpu_custom_call" | custom-call | tf_op jit(solution)/shard_map/pallas_call | solution.py:228
  185.1 9.5 %collective-permute-done.22.r0 = f32[128,128]{1,0:T(8,128)S(1)} collective-permute-done((f32[128,128]{1,0:T(8,128)S(1)}, f32[128,128]{1,0:T(8,128)S(1)}, u32[]{:S(2)}, u32[]{:S(2)}) %collective-permute-start.22) | collective-permute-done | bytes 65568 | tf_op jit(solution)/shard_map/ppermute | solution.py:364
  203.8 5.0 %shard_map.98 = (bf16[64,3584]{1,0:T(8,128)(2,1)}, bf16[32,3584]{1,0:T(8,128)(2,1)}, bf16[32,3584]{1,0:T(8,128)(2,1)}) custom-call(bf16[128,3584]{1,0:T(8,128)(2,1)} %collective-permute-done.26.refs_0_.refs_9_.refs_5_, bf16[128,3584]{1,0:T(8,128)(2,1)} %collective-permute-done.27.refs_1_.refs_12_.refs_6_), custom_call_target="tpu_custom_call" | custom-call | tf_op jit(solution)/shard_map/pallas_call | solution.py:228
  208.9 7.0 %shard_map.99 = (bf16[1024,256]{1,0:T(8,128)(2,1)S(1)}, bf16[256,3584]{1,0:T(8,128)(2,1)S(1)}, bf16[256,3584]{1,0:T(8,128)(2,1)}) custom-call(s32[8]{0:T(128)S(1)} %stack.35.place_ref, bf16[4,256,1024]{2,1,0:T(8,128)(2,1)} %refs_1_.9, bf16[4,256,1024]{2,1,0:T(8,128)(2,1)} %refs_1_.9, f32[1024,128]{1,0:T(8,128)S(1)} %copy-done.2, ...), custom_call_target="tpu_custom_call" | custom-call | tf_op jit(solution)/shard_map/pallas_call | solution.py:272
  217.2 9.1 %collective-permute-done.29.r0 = f32[128,128]{1,0:T(8,128)S(1)} collective-permute-done((f32[128,128]{1,0:T(8,128)S(1)}, f32[128,128]{1,0:T(8,128)S(1)}, u32[]{:S(2)}, u32[]{:S(2)}) %collective-permute-start.29) | collective-permute-done | bytes 65568 | tf_op jit(solution)/shard_map/ppermute | solution.py:364
  241.8 10.2 %shard_map.101 = (bf16[1024,512]{1,0:T(8,128)(2,1)}, bf16[512,3584]{1,0:T(8,128)(2,1)}, bf16[512,3584]{1,0:T(8,128)(2,1)}) custom-call(s32[8]{0:T(128)S(1)} %stack.35.place_ref, bf16[4,256,1024]{2,1,0:T(8,128)(2,1)} %refs_1_.9, bf16[4,256,1024]{2,1,0:T(8,128)(2,1)} %refs_1_.9, bf16[4,256,1024]{2,1,0:T(8,128)(2,1)} %refs_1_.9, bf16[4,256,1024]{2,1,0:T(8,128)(2,1)} %refs_1_.9, ...), custom_call_target="tpu_custom_call" | custom-call | tf_op jit(solution)/shard_map/pallas_call | solution.py:272
  268.1 9.0 %collective-permute-done.40.refs_3_ = bf16[256,128]{1,0:T(8,128)(2,1)S(1)} collective-permute-done((bf16[256,128]{1,0:T(8,128)(2,1)S(1)}, bf16[256,128]{1,0:T(8,128)(2,1)S(1)}, u32[]{:S(2)}, u32[]{:S(2)}) %collective-permute-start.40) | collective-permute-done | bytes 65568 | tf_op jit(solution)/shard_map/ppermute | solution.py:347
  277.2 7.7 %shard_map.103 = (bf16[1024,256]{1,0:T(8,128)(2,1)S(1)}, bf16[256,3584]{1,0:T(8,128)(2,1)}, bf16[256,3584]{1,0:T(8,128)(2,1)}) custom-call(s32[8]{0:T(128)S(1)} %stack.35.place_ref, bf16[4,256,1024]{2,1,0:T(8,128)(2,1)} %refs_1_.9, bf16[4,256,1024]{2,1,0:T(8,128)(2,1)} %refs_1_.9, f32[1024,128]{1,0:T(8,128)S(1)} %copy-done.2, ...), custom_call_target="tpu_custom_call" | custom-call | tf_op jit(solution)/shard_map/pallas_call | solution.py:272
  290.2 18.2 %shard_map.104 = (bf16[1024,3584]{1,0:T(8,128)(2,1)}, f32[3584,128]{1,0:T(8,128)}) custom-call(s32[8]{0:T(128)S(1)} %stack.35.place_ref, f32[8,128,128]{2,1,0:T(8,128)S(1)} %all-to-all-done.2.g_ref, bf16[128,3584]{1,0:T(8,128)(2,1)S(1)} %bitcast.39, bf16[1024,256]{1,0:T(8,128)(2,1)S(1)} %copy-done.22, bf16[256,3584]{1,0:T(8,128)(2,1)S(1)} %copy-done.8, ...), custom_call_target="tpu_custom_call" | custom-call | tf_op jit(solution)/shard_map/pallas_call | solution.py:330
  (215 shorter events, 112.9 us)
Async XLA Ops:
  12.7 68.3 %all-to-all-start = ((bf16[8,32,3584]{2,1,0:T(8,128)(2,1)}), bf16[8,32,3584]{2,1,0:T(8,128)(2,1)}, u32[]{:S(2)}, u32[]{:S(2)}) async-start(bf16[8,32,3584]{2,1,0:T(8,128)(2,1)} %copy-done.5), calls=%async_computation | async-start | bytes 3670016 | tf_op jit(solution)/shard_map/all_to_all | solution.py:398
  28.4 22.0 %collective-permute-start = (bf16[32,3584]{1,0:T(8,128)(2,1)}, bf16[32,3584]{1,0:T(8,128)(2,1)}, u32[]{:S(2)}, u32[]{:S(2)}) collective-permute-start(bf16[32,3584]{1,0:T(8,128)(2,1)} %get-tuple-element.168), channel_id=1, source_target_pairs={{0,8},{4,12},{8,16},{12,20},{16,24},{20,28},{24,0},{28,4},{1,9},{5... | collective-permute-start | bytes 688136 | tf_op jit(solution)/shard_map/ppermute | solution.py:347
  29.8 22.2 %collective-permute-start.5 = (bf16[32,3584]{1,0:T(8,128)(2,1)}, bf16[32,3584]{1,0:T(8,128)(2,1)}, u32[]{:S(2)}, u32[]{:S(2)}) collective-permute-start(bf16[32,3584]{1,0:T(8,128)(2,1)} %get-tuple-element.169), channel_id=1, source_target_pairs={{0,24},{4,28},{8,0},{12,4},{16,8},{20,12},{24,16},{28,20},{1,25},{... | collective-permute-start | bytes 688136 | tf_op jit(solution)/shard_map/ppermute | solution.py:347
  31.8 21.2 %collective-permute-start.4 = (bf16[64,3584]{1,0:T(8,128)(2,1)}, bf16[64,3584]{1,0:T(8,128)(2,1)}, u32[]{:S(2)}, u32[]{:S(2)}) collective-permute-start(bf16[64,3584]{1,0:T(8,128)(2,1)} %slice.59), channel_id=1, source_target_pairs={{0,4},{4,0},{8,12},{12,8},{16,20},{20,16},{24,28},{28,24},{1,5},{5... | collective-permute-start | bytes 1376264 | tf_op jit(solution)/shard_map/ppermute | solution.py:347
  34.4 37.0 %collective-permute-start.2 = (bf16[128,3584]{1,0:T(8,128)(2,1)}, bf16[128,3584]{1,0:T(8,128)(2,1)}, u32[]{:S(2)}, u32[]{:S(2)}) collective-permute-start(bf16[128,3584]{1,0:T(8,128)(2,1)} %pad_maximum_fusion.1), channel_id=1, source_target_pairs={{0,4},{4,0},{8,12},{12,8},{16,20},{20,16},{24,28},{28,24},{1,5},{5... | collective-permute-start | bytes 2752520 | tf_op jit(solution)/shard_map/ppermute | solution.py:347
  51.7 21.0 %collective-permute-start.1 = (bf16[128,3584]{1,0:T(8,128)(2,1)S(1)}, bf16[128,3584]{1,0:T(8,128)(2,1)S(1)}, u32[]{:S(2)}, u32[]{:S(2)}) collective-permute-start(bf16[128,3584]{1,0:T(8,128)(2,1)S(1)} %pad_maximum_fusion), channel_id=1, source_target_pairs={{0,8},{4,12},{8,16},{12,20},{16,24},{20,28},{24,0},{28,4},{1,9},{5... | collective-permute-start | bytes 2752520 | tf_op jit(solution)/shard_map/ppermute | solution.py:347
  54.3 19.8 %collective-permute-start.6 = (bf16[128,3584]{1,0:T(8,128)(2,1)S(1)}, bf16[128,3584]{1,0:T(8,128)(2,1)S(1)}, u32[]{:S(2)}, u32[]{:S(2)}) collective-permute-start(bf16[128,3584]{1,0:T(8,128)(2,1)S(1)} %pad_maximum_fusion.2), channel_id=1, source_target_pairs={{0,24},{4,28},{8,0},{12,4},{16,8},{20,12},{24,16},{28,20},{1,25},{... | collective-permute-start | bytes 2752520 | tf_op jit(solution)/shard_map/ppermute | solution.py:347
  73.2 20.1 %collective-permute-start.3 = (bf16[128,3584]{1,0:T(8,128)(2,1)S(1)}, bf16[128,3584]{1,0:T(8,128)(2,1)S(1)}, u32[]{:S(2)}, u32[]{:S(2)}) collective-permute-start(bf16[128,3584]{1,0:T(8,128)(2,1)S(1)} %add_convert_fusion.3), channel_id=1, source_target_pairs={{0,8},{4,12},{8,16},{12,20},{16,24},{20,28},{24,0},{28,4},{1,9},{5... | collective-permute-start | bytes 2752520 | tf_op jit(solution)/shard_map/ppermute | solution.py:347
  75.5 19.9 %collective-permute-start.7 = (bf16[128,3584]{1,0:T(8,128)(2,1)}, bf16[128,3584]{1,0:T(8,128)(2,1)}, u32[]{:S(2)}, u32[]{:S(2)}) collective-permute-start(bf16[128,3584]{1,0:T(8,128)(2,1)} %add_convert_fusion.2), channel_id=1, source_target_pairs={{0,24},{4,28},{8,0},{12,4},{16,8},{20,12},{24,16},{28,20},{1,25},{... | collective-permute-start | bytes 2752520 | tf_op jit(solution)/shard_map/ppermute | solution.py:347
  79.8 34.5 %collective-permute-start.8 = (bf16[128,3584]{1,0:T(8,128)(2,1)}, bf16[128,3584]{1,0:T(8,128)(2,1)}, u32[]{:S(2)}, u32[]{:S(2)}) collective-permute-start(bf16[128,3584]{1,0:T(8,128)(2,1)} %add_convert_fusion.1), channel_id=1, source_target_pairs={{0,4},{4,0},{8,12},{12,8},{16,20},{20,16},{24,28},{28,24},{1,5},{5... | collective-permute-start | bytes 2752520 | tf_op jit(solution)/shard_map/ppermute | solution.py:347
  84.4 39.3 %all-to-all-start.1 = ((bf16[8,32,4608]{2,1,0:T(8,128)(2,1)}), bf16[8,32,4608]{2,1,0:T(8,128)(2,1)}, u32[]{:S(2)}, u32[]{:S(2)}) async-start(bf16[8,32,4608]{2,1,0:T(8,128)(2,1)} %broadcast_in_dim.8), calls=%async_computation.1 | async-start | bytes 4718592 | tf_op jit(solution)/shard_map/all_to_all | solution.py:398
  116.3 42.5 %collective-permute-start.17 = (bf16[128,3584]{1,0:T(8,128)(2,1)S(1)}, bf16[128,3584]{1,0:T(8,128)(2,1)}, u32[]{:S(2)}, u32[]{:S(2)}) collective-permute-start(bf16[128,3584]{1,0:T(8,128)(2,1)S(1)} %add_convert_fusion.base_ref.refs_0_.refs_5_), channel_id=1, source_target_pairs={{0,24},{4,28},{8,0},{12,4},{16,8},{20,12},{24,16},{28,20},{1,25},{... | collective-permute-start | bytes 2752520 | tf_op jit(solution)/shard_map/ppermute | solution.py:347
  116.4 42.4 %collective-permute-start.16 = (bf16[128,3584]{1,0:T(8,128)(2,1)S(1)}, bf16[128,3584]{1,0:T(8,128)(2,1)}, u32[]{:S(2)}, u32[]{:S(2)}) collective-permute-start(bf16[128,3584]{1,0:T(8,128)(2,1)S(1)} %add_convert_fusion.base_ref.refs_0_.refs_5_), channel_id=1, source_target_pairs={{0,8},{4,12},{8,16},{12,20},{16,24},{20,28},{24,0},{28,4},{1,9},{5... | collective-permute-start | bytes 2752520 | tf_op jit(solution)/shard_map/ppermute | solution.py:347
  171.1 31.4 %collective-permute-start.26 = (bf16[128,3584]{1,0:T(8,128)(2,1)}, bf16[128,3584]{1,0:T(8,128)(2,1)}, u32[]{:S(2)}, u32[]{:S(2)}) collective-permute-start(bf16[128,3584]{1,0:T(8,128)(2,1)} %get-tuple-element.119), channel_id=1, source_target_pairs={{0,8},{4,12},{8,16},{12,20},{16,24},{20,28},{24,0},{28,4},{1,9},{5... | collective-permute-start | bytes 2752520 | tf_op jit(solution)/shard_map/ppermute | solution.py:347
  172.0 30.6 %collective-permute-start.27 = (bf16[128,3584]{1,0:T(8,128)(2,1)}, bf16[128,3584]{1,0:T(8,128)(2,1)}, u32[]{:S(2)}, u32[]{:S(2)}) collective-permute-start(bf16[128,3584]{1,0:T(8,128)(2,1)} %get-tuple-element.120), channel_id=1, source_target_pairs={{0,24},{4,28},{8,0},{12,4},{16,8},{20,12},{24,16},{28,20},{1,25},{... | collective-permute-start | bytes 2752520 | tf_op jit(solution)/shard_map/ppermute | solution.py:347
  179.2 23.3 %collective-permute-start.28 = (bf16[64,3584]{1,0:T(8,128)(2,1)S(1)}, bf16[64,3584]{1,0:T(8,128)(2,1)S(1)}, u32[]{:S(2)}, u32[]{:S(2)}) collective-permute-start(bf16[64,3584]{1,0:T(8,128)(2,1)S(1)} %copy-done.26), channel_id=1, source_target_pairs={{0,4},{4,0},{8,12},{12,8},{16,20},{20,16},{24,28},{28,24},{1,5},{5... | collective-permute-start | bytes 1376264 | tf_op jit(solution)/shard_map/ppermute | solution.py:347
  201.0 34.0 %collective-permute-start.32 = (bf16[64,3584]{1,0:T(8,128)(2,1)S(1)}, bf16[64,3584]{1,0:T(8,128)(2,1)S(1)}, u32[]{:S(2)}, u32[]{:S(2)}) collective-permute-start(bf16[64,3584]{1,0:T(8,128)(2,1)S(1)} %copy-done.38), channel_id=1, source_target_pairs={{0,4},{4,0},{8,12},{12,8},{16,20},{20,16},{24,28},{28,24},{1,5},{5... | collective-permute-start | bytes 1376264 | tf_op jit(solution)/shard_map/ppermute | solution.py:347
  201.9 33.9 %collective-permute-start.33 = (bf16[64,3584]{1,0:T(8,128)(2,1)S(1)}, bf16[64,3584]{1,0:T(8,128)(2,1)S(1)}, u32[]{:S(2)}, u32[]{:S(2)}) collective-permute-start(bf16[64,3584]{1,0:T(8,128)(2,1)S(1)} %shard_map.96), channel_id=1, source_target_pairs={{0,4},{4,0},{8,12},{12,8},{16,20},{20,16},{24,28},{28,24},{1,5},{5... | collective-permute-start | bytes 1376264 | tf_op jit(solution)/shard_map/ppermute | solution.py:347
  202.5 23.7 %collective-permute-start.29 = (f32[128,128]{1,0:T(8,128)S(1)}, f32[128,128]{1,0:T(8,128)S(1)}, u32[]{:S(2)}, u32[]{:S(2)}) collective-permute-start(f32[128,128]{1,0:T(8,128)S(1)} %add.194), channel_id=1, source_target_pairs={{32,0},{33,3},{34,2},{35,1},{64,32},{65,35},{66,34},{67,33},{96,64... | collective-permute-start | bytes 196616 | tf_op jit(solution)/shard_map/ppermute | solution.py:364
  236.6 15.4 %collective-permute-start.36 = (f32[128,128]{1,0:T(8,128)S(1)}, f32[128,128]{1,0:T(8,128)S(1)}, u32[]{:S(2)}, u32[]{:S(2)}) collective-permute-start(f32[128,128]{1,0:T(8,128)S(1)} %add.195), channel_id=1, source_target_pairs={{32,0},{33,3},{34,2},{35,1},{64,32},{65,35},{66,34},{67,33},{96,64... | collective-permute-start | bytes 196616 | tf_op jit(solution)/shard_map/ppermute | solution.py:364
  253.9 23.3 %collective-permute-start.43 = (bf16[64,3584]{1,0:T(8,128)(2,1)}, bf16[64,3584]{1,0:T(8,128)(2,1)}, u32[]{:S(2)}, u32[]{:S(2)}) collective-permute-start(bf16[64,3584]{1,0:T(8,128)(2,1)} %get-tuple-element.156), channel_id=1, source_target_pairs={{0,4},{4,0},{8,12},{12,8},{16,20},{20,16},{24,28},{28,24},{1,5},{5... | collective-permute-start | bytes 1376264 | tf_op jit(solution)/shard_map/ppermute | solution.py:347
  257.9 28.5 %all-to-all-start.2 = ((f32[8,128,128]{2,1,0:T(8,128)}), f32[8,128,128]{2,1,0:T(8,128)S(1)}, u32[]{:S(2)}, u32[]{:S(2)}) async-start(f32[8,128,128]{2,1,0:T(8,128)} %broadcast_in_dim.9), calls=%async_computation.2 | async-start | bytes 1048576 | tf_op jit(solution)/shard_map/all_to_all | solution.py:398
  261.4 15.8 %collective-permute-start.41 = (bf16[32,3584]{1,0:T(8,128)(2,1)}, bf16[32,3584]{1,0:T(8,128)(2,1)S(1)}, u32[]{:S(2)}, u32[]{:S(2)}) collective-permute-start(bf16[32,3584]{1,0:T(8,128)(2,1)} %get-tuple-element.154), channel_id=1, source_target_pairs={{0,8},{4,12},{8,16},{12,20},{16,24},{20,28},{24,0},{28,4},{1,9},{5... | collective-permute-start | bytes 688136 | tf_op jit(solution)/shard_map/ppermute | solution.py:347
  264.2 21.5 %collective-permute-start.39 = (f32[256,128]{1,0:T(8,128)S(1)}, f32[256,128]{1,0:T(8,128)S(1)}, u32[]{:S(2)}, u32[]{:S(2)}) collective-permute-start(f32[256,128]{1,0:T(8,128)S(1)} %add.196), channel_id=1, source_target_pairs={{0,2},{1,3},{2,0},{3,1},{4,6},{5,7},{6,4},{7,5},{8,10},{9,11},{10,... | collective-permute-start | bytes 393224 | tf_op jit(solution)/shard_map/ppermute | solution.py:352
  (65 other events, 379.6 us)

commit v5 on v4

v5 whole, which is shorter than its diff:
```python
import functools

import jax
import jax.numpy as jnp
from jax import lax
from jax.experimental import pallas as pl
from jax.experimental.pallas import tpu as pltpu
from jax.sharding import PartitionSpec as P

BF = jnp.bfloat16
F32 = jnp.float32
HIGHEST = lax.Precision.HIGHEST
NT = (((1,), (1,)), ((), ()))
CHUNK = 512
X_SIZE = 4
RELATIVE = ((0, 0), (0, 1), (-1, 0), (-1, 1), (1, 0), (1, 1), (2, 0), (2, 1))
EARLY, LATE = (7, 6, 3, 5), (2, 4, 1, 0)
PARAMS = pltpu.CompilerParams(vmem_limit_bytes=60 * 1024 * 1024)
SMALL = pltpu.CompilerParams(vmem_limit_bytes=16 * 1024 * 1024)


def split2(x):
    hi = x.astype(BF)
    return hi, (x - hi.astype(F32)).astype(BF)


def mm(a, b):
    return jnp.dot(a, b, preferred_element_type=F32)


def mm_nt(a, b):
    return lax.dot_general(a, b, NT, preferred_element_type=F32)


def sigma(v):
    return 0.5 * jnp.tanh(0.5 * v) + 0.5


def wide(x):
    return jnp.concatenate(split2(x), axis=1)


def tall(x):
    return jnp.concatenate(split2(x), axis=0)


def twice(x):
    return jnp.concatenate([x, x], axis=0)


def chunks_of(width):
    return [slice(i, i + CHUNK) for i in range(0, width, CHUNK)]


def up_of(all_ref, cols):
    dp, rows, _ = all_ref.shape
    return all_ref[:, : rows // 2, cols].reshape(dp * rows // 2, -1)


def down_of(all_ref, cols):
    dp, rows, _ = all_ref.shape
    return all_ref[:, rows // 2 :, cols].reshape(dp * rows // 2, -1)


def gram_share(x, all_ref):
    rank = x.shape[1]
    cols = slice(all_ref.shape[2] - rank, all_ref.shape[2])
    gram = up_of(all_ref, cols).astype(F32) + down_of(all_ref, cols).astype(F32)
    return 0.25 * jnp.dot(x, gram, precision=HIGHEST, preferred_element_type=F32)


def first_kernel(base_ref, all_ref, part_ref):
    acc = jnp.zeros(part_ref.shape, F32)
    for cols in chunks_of(base_ref.shape[1]):
        pre = base_ref[:, cols].astype(F32)
        hidden = (pre * sigma(pre)).astype(BF)
        acc += mm_nt(hidden, down_of(all_ref, cols))
    part_ref[...] = acc


def forward_kernel(base_ref, all_ref, r0, r1, part_ref):
    c = r0[...] + r1[...]
    cw = wide(c)
    acc = gram_share(c, all_ref)
    for cols in chunks_of(base_ref.shape[1]):
        pre = base_ref[:, cols].astype(F32) + mm(cw, twice(up_of(all_ref, cols)))
        hidden = (pre * sigma(pre)).astype(BF)
        acc += mm_nt(hidden, down_of(all_ref, cols))
    part_ref[...] = acc


def middle_kernel(base_ref, all_ref, r0, r1, c_ref, part_ref, slope_ref):
    c = r0[...] + r1[...]
    c_ref[...] = c.astype(BF)
    cw = wide(c)
    acc = gram_share(c, all_ref)
    for cols in chunks_of(base_ref.shape[1]):
        pre = base_ref[:, cols].astype(F32) + mm(cw, twice(up_of(all_ref, cols)))
        sig = sigma(pre)
        hidden = (pre * sig).astype(BF)
        slope_ref[:, cols] = (sig * (1.0 + pre * (1.0 - sig))).astype(BF)
        acc += mm_nt(hidden, down_of(all_ref, cols))
    part_ref[...] = acc


def backward_kernel(last_ref, slope_ref, all_ref, cot_ref, r0, r1, part_ref):
    g = jnp.where(last_ref[0] == 1, cot_ref[...], r0[...] + r1[...])
    gw = wide(g)
    acc = gram_share(g, all_ref)
    for cols in chunks_of(slope_ref.shape[1]):
        g_pre = mm(gw, twice(down_of(all_ref, cols))) * slope_ref[:, cols].astype(F32)
        hi, lo = split2(g_pre)
        up = up_of(all_ref, cols)
        acc += mm_nt(hi, up) + mm_nt(lo, up)
    part_ref[...] = acc


def call(kernel, outs, *args):
    return pl.pallas_call(kernel, out_shape=outs, compiler_params=SMALL)(*args)


def base_specs(base, dp, blocks):
    micro, tokens, width = base.shape
    return [
        pl.BlockSpec((micro, tokens // dp, width), lambda i, p, j=j: (0, p[j], 0)) for j in blocks
    ]


def product_kernel(count, plan, place_ref, *refs):
    bases, w_ref, outs, rows = refs[:count], refs[count], refs[count + 1 : -1], refs[-1]
    own = bases[0].shape[0] * bases[0].shape[1]

    @pl.when(pl.program_id(0) == 0)
    def _():
        for j, b in enumerate(bases):
            rows[j * own : (j + 1) * own] = b[...].reshape(own, b.shape[2])

    res = mm(rows[...], w_ref[...])
    for out, parts in zip(outs, plan):
        start = 0
        for j, begin, end in parts:
            out[start : start + end - begin] = res[j * own + begin : j * own + end].astype(BF)
            start += end - begin


def product(place, base, w_in, dp, blocks, plan):
    micro, tokens, width = base.shape
    hid = w_in.shape[1]
    own = micro * tokens // dp
    count = len(blocks)
    heights = [sum(end - begin for _, begin, end in parts) for parts in plan]
    column = lambda rows: pl.BlockSpec((rows, CHUNK), lambda i, p: (0, i))
    return pl.pallas_call(
        functools.partial(product_kernel, count, plan),
        out_shape=[jax.ShapeDtypeStruct((rows, hid), BF) for rows in heights],
        grid_spec=pltpu.PrefetchScalarGridSpec(
            num_scalar_prefetch=1,
            grid=(hid // CHUNK,),
            in_specs=base_specs(base, dp, blocks) + [column(width)],
            out_specs=[column(rows) for rows in heights],
            scratch_shapes=[pltpu.VMEM((own * count, width), BF)],
        ),
        compiler_params=PARAMS,
    )(place, *([base] * count), w_in)


def project_kernel(basis_ref, w_in_ref, w_out_ref, out_ref, wide_ref, tall_ref):
    rank = basis_ref.shape[1]
    count, rows, cols = out_ref.shape
    share = rows // 2
    step = pl.program_id(0)

    @pl.when(step == 0)
    def _():
        basis = basis_ref[...]
        wide_ref[...] = wide(basis)
        tall_ref[...] = tall(basis.T)
        gram = jnp.dot(basis.T, basis, precision=HIGHEST, preferred_element_type=F32)
        hi, lo = split2(gram)
        out_ref[:, :share, cols - rank :] = hi.reshape(count, share, rank)
        out_ref[:, share:, cols - rank :] = lo.reshape(count, share, rank)

    here = pl.ds(pl.multiple_of(step * CHUNK, CHUNK), CHUNK)
    up = mm(tall_ref[...], w_in_ref[...])
    down = mm(w_out_ref[...], wide_ref[...])
    out_ref[:, :share, here] = (up[:rank] + up[rank:]).astype(BF).reshape(count, share, CHUNK)
    down = (down[:, :rank] + down[:, rank:]).T
    out_ref[:, share:, here] = down.astype(BF).reshape(count, share, CHUNK)


def project(basis, w_in, w_out, dp):
    width, rank = basis.shape
    hid = w_in.shape[1]
    shape = (dp, 2 * rank // dp, hid + rank)
    return pl.pallas_call(
        project_kernel,
        out_shape=jax.ShapeDtypeStruct(shape, BF),
        grid=(hid // CHUNK,),
        in_specs=[
            pl.BlockSpec((width, rank), lambda i: (0, 0)),
            pl.BlockSpec((width, CHUNK), lambda i: (0, i)),
            pl.BlockSpec((CHUNK, width), lambda i: (i, 0)),
        ],
        out_specs=pl.BlockSpec(shape, lambda i: (0, 0, 0)),
        scratch_shapes=[pltpu.VMEM((width, 2 * rank), BF), pltpu.VMEM((2 * rank, width), BF)],
        compiler_params=PARAMS,
    )(basis, w_in, w_out)


def fold_kernel(rank, x_ref, out_ref):
    count, rows, cols = x_ref.shape
    share = rows // 2
    total = x_ref[0].astype(F32)
    for d in range(1, count):
        total += x_ref[d].astype(F32)
    hi, lo = split2(total[:share, cols - rank :] + total[share:, cols - rank :])
    own = jnp.concatenate(
        [total[:, : cols - rank].astype(BF), jnp.concatenate([hi, lo], axis=0)], axis=1
    )
    for d in range(count):
        out_ref[d] = own


def turn_kernel(place_ref, *refs):
    bases, out = refs[:-1], refs[-1]
    own = bases[0].shape[0] * bases[0].shape[1]
    for j, b in enumerate(bases):
        rows = b[...].reshape(own, b.shape[2]).astype(F32)
        out[:, j * own : (j + 1) * own] = rows.T.astype(BF)


def turn(place, base, dp):
    micro, tokens, width = base.shape
    count = len(RELATIVE)
    shape = (width, micro * tokens)
    return pl.pallas_call(
        turn_kernel,
        out_shape=jax.ShapeDtypeStruct(shape, BF),
        grid_spec=pltpu.PrefetchScalarGridSpec(
            num_scalar_prefetch=1,
            grid=(1,),
            in_specs=base_specs(base, dp, range(count)),
            out_specs=pl.BlockSpec(shape, lambda i, p: (0, 0)),
        ),
        compiler_params=PARAMS,
    )(place, *([base] * count))


def finish_kernel(place_ref, ex_ref, all_ref, base_ref, basis_ref, *refs):
    pieces, (grad_ref, dc_ref, xt, gg, gt, cc, hidden, g_pre) = refs[:-8], refs[-8:]
    own, two = ex_ref.shape[1:]
    rank = two // 2

    @pl.when(pl.program_id(0) == 0)
    def _():
        basis = basis_ref[...].astype(BF)
        for j in range(len(RELATIVE)):
            ex = ex_ref[place_ref[j]]
            rows = slice(j * own, (j + 1) * own)
            g, c = ex[:, :rank], ex[:, rank:]
            gg[rows] = g
            cc[rows] = c
            gt[:, rows] = g.astype(F32).T.astype(BF)
            xt[:, rows] = (base_ref[:, rows].astype(F32) + mm_nt(basis, c)).astype(BF)

    every = slice(0, all_ref.shape[2])
    from_c = mm(cc[...], up_of(all_ref, every))
    g_hidden = mm(gg[...], down_of(all_ref, every))
    start = 0
    for p in pieces:
        rows = slice(start, start + p.shape[0])
        start += p.shape[0]
        pre = p[...].astype(F32) + from_c[rows]
        sig = sigma(pre)
        out = pre * sig
        hidden[rows] = out.astype(BF)
        g_pre[rows] = (g_hidden[rows] * (sig + out * (1.0 - sig))).astype(BF)
    grad_ref[...] = mm(xt[...], g_pre[...]).astype(BF)
    dc_ref[...] = mm(gt[...], hidden[...]).T


def finish(place, ex, everyone, base_t, basis, pieces):
    width, tokens = base_t.shape
    hid = pieces[0].shape[1]
    rank = basis.shape[1]
    dp, rows, _ = everyone.shape
    column = lambda rows: pl.BlockSpec((rows, CHUNK), lambda i, p: (0, i))
    return pl.pallas_call(
        finish_kernel,
        out_shape=[jax.ShapeDtypeStruct((width, hid), BF), jax.ShapeDtypeStruct((hid, rank), F32)],
        grid_spec=pltpu.PrefetchScalarGridSpec(
            num_scalar_prefetch=1,
            grid=(hid // CHUNK,),
            in_specs=[
                pl.BlockSpec(ex.shape, lambda i, p: (0, 0, 0)),
                pl.BlockSpec((dp, rows, CHUNK), lambda i, p: (0, 0, i)),
                pl.BlockSpec(base_t.shape, lambda i, p: (0, 0)),
                pl.BlockSpec(basis.shape, lambda i, p: (0, 0)),
            ]
            + [column(p.shape[0]) for p in pieces],
            out_specs=[column(width), pl.BlockSpec((CHUNK, rank), lambda i, p: (i, 0))],
            scratch_shapes=[
                pltpu.VMEM((width, tokens), BF),
                pltpu.VMEM((tokens, rank), BF),
                pltpu.VMEM((rank, tokens), BF),
                pltpu.VMEM((tokens, rank), BF),
                pltpu.VMEM((tokens, CHUNK), BF),
                pltpu.VMEM((tokens, CHUNK), BF),
            ],
        ),
        compiler_params=PARAMS,
    )(place, ex, everyone, base_t, basis, *pieces)


def to_dp(x, dx, dy):
    size = lax.axis_size("dp")
    pairs = [(i, ((i // 2 + dx) % X_SIZE) * 2 + ((i % 2) ^ dy)) for i in range(size)]
    return lax.ppermute(x, "dp", pairs)


def to_tensor(x, k):
    size = lax.axis_size("tensor")
    return lax.ppermute(x, "tensor", [(t, t ^ k) for t in range(size)])


def hop(part, by, before=(), during=lambda *a: ()):
    sections, tensors = lax.axis_size("section"), lax.axis_size("tensor")
    pair_sum, before = tie(part + to_tensor(part, 1), before)
    pairs = [
        (s * tensors + t, (s + by) * tensors + (t ^ (2 * (t % 2))))
        for s in range(sections)
        for t in range(tensors)
        if 0 <= s + by < sections
    ]
    got = lax.ppermute(pair_sum, ("section", "tensor"), pairs)
    got, made = tie(got, during(*before))
    return (got, to_tensor(got, 1)), before, made


def cat(*xs):
    return jnp.concatenate(xs, axis=0)


def plus(x, *ys):
    total = x.astype(F32)
    for start, y in ys:
        pads = ((start, x.shape[0] - start - y.shape[0]), (0, 0))
        total = total + jnp.pad(y.astype(F32), pads)
    return total.astype(x.dtype)


def reduce_2(two, left_1, right_1, steps):
    u0, u1, v = steps
    h, q = two.shape[0] // 2, two.shape[0] // 4
    up = cat(two[:h], plus(right_1, (0, u0)))
    down = cat(plus(two[h:], (0, v)), plus(left_1, (q, u1)))
    return up, down


def reduce_3(left, right, side, up, down, other):
    h = left.shape[0] // 2
    return (
        plus(right, (0, up[:h]), (h, other[:h])),
        plus(left, (h, down[:h]), (h, other[h:])),
        plus(side, (0, up[h:]), (0, down[h:])),
    )


def swap(x):
    return lax.all_to_all(x, "dp", 0, 0, tiled=True)


def tie(*xs):
    return lax.optimization_barrier(xs)


def on_device(base, w_in, w_out, basis, cotangent):
    dp = lax.axis_size("dp")
    sections = lax.axis_size("section")
    last = (lax.axis_index("section") == sections - 1).astype(jnp.int32).reshape(1)
    d = lax.axis_index("dp")
    place = jnp.stack(
        [((d // 2 + dx) % X_SIZE) * 2 + (d % 2 + dy) % 2 for dx, dy in RELATIVE]
    ).astype(jnp.int32)
    micro, tokens, width = base.shape
    rows = tokens // dp
    own = micro * rows
    rank = basis.shape[1]
    w_in, w_out = w_in[0], w_out[0]
    hid = w_in.shape[1]
    tok = jax.ShapeDtypeStruct((own, rank), F32)
    f = lambda a: a.astype(F32)

    h, q = own // 2, own // 4
    cuts = [
        [(0, 0, q)], [(0, q, h)], [(0, h, own)], [(1, 0, own)], [(2, 0, h)], [(3, 0, h)],
        [(3, h, own), (2, h, own)],
    ]
    early = product(place, base, w_in, dp, EARLY, cuts)
    (*far, two, left_1, right_1, other), base_1 = tie(early, base)
    steps = to_dp(far[0], 1, 0), to_dp(far[1], -1, 0), to_dp(far[2], 0, 1)
    base_t = turn(place, base_1, dp)
    steps, base_t = tie(steps, base_t)
    up, down = reduce_2(two, left_1, right_1, steps)
    up, down, other, basis_1 = tie(up, down, other, basis)
    up, down, other = to_dp(up, 1, 0), to_dp(down, -1, 0), to_dp(other, 0, 1)
    proj = project(basis_1, w_in, w_out, dp)
    up, down, other, proj, base_2 = tie(up, down, other, proj, base_1)
    proj = swap(proj)
    late = product(place, base_2, w_in, dp, LATE, [[(j, 0, own)] for j in range(len(LATE))])
    proj, late = tie(proj, late)
    proj = call(functools.partial(fold_kernel, rank), jax.ShapeDtypeStruct(proj.shape, BF), proj)
    everyone = swap(proj)
    left, right, side, mine = late
    sent = reduce_3(left, right, side, up, down, other)
    got = to_dp(sent[0], 1, 0), to_dp(sent[1], -1, 0), to_dp(sent[2], 0, 1)
    own_pre = ((f(mine) + f(got[0])) + (f(got[1]) + f(got[2]))).astype(BF)

    left, right = to_dp(own_pre, 1, 0), to_dp(own_pre, -1, 0)
    part = call(first_kernel, tok, own_pre, everyone)
    got, _, mine = hop(part, 1, (own_pre,), lambda a: (a[:h], a[h:]))
    side_low = to_dp(mine[0], 0, 1)
    part = call(forward_kernel, tok, own_pre, everyone, *got)
    got, _, _ = hop(part, 1)
    got, left, right, side_low, high = tie(got, left, right, side_low, mine[1])
    side_high = to_dp(high, 0, 1)
    far = to_dp(left, 1, 0)
    part = call(forward_kernel, tok, own_pre, everyone, *got)
    got, _, _ = hop(part, 1)
    got, side_low = tie(got, side_low)
    left_low, right_low = to_dp(side_low, 1, 0), to_dp(side_low, -1, 0)
    c_in, coef_part, slope = call(
        middle_kernel,
        (jax.ShapeDtypeStruct((own, rank), BF), tok, jax.ShapeDtypeStruct((own, hid), BF)),
        own_pre, everyone, *got,
    )
    cot = cotangent.reshape(own, rank)

    def back(got):
        return call(backward_kernel, tok, last, slope, everyone, cot, *got)

    got, _, _ = hop(back((cot, cot)), -1)
    got, far, side_high, left_low, right_low = tie(got, far, side_high, left_low, right_low)
    left_high, right_high = to_dp(side_high, 1, 0), to_dp(side_high, -1, 0)
    far_low = to_dp(left_low, 1, 0)
    got, _, _ = hop(back(got), -1)
    got, left_high, right_high = tie(got, left_high, right_high)
    far_high = to_dp(right_high, -1, 0)
    got, _, _ = hop(back(got), -1)
    got, far_low, far_high = tie(got, far_low, far_high)
    g_out = jnp.where(last[0] == 1, cot, got[0] + got[1])
    ex = jnp.concatenate([g_out.astype(BF), c_in], axis=1)
    ex = swap(jnp.broadcast_to(ex[None], (dp,) + ex.shape))
    parts = cat(coef_part, back(got))
    parts = parts + to_tensor(parts, 1)
    ex, parts = tie(ex, parts)
    pieces = [
        own_pre, side_low, side_high, left, left_low, left_high,
        right, right_low, right_high, far, far_low, far_high,
    ]
    grad_up, down_coefs = finish(place, ex, everyone, base_t, basis, pieces)
    parts = (parts + to_tensor(parts, 2)).reshape(2, 1, micro, rows, rank)
    return parts[0], parts[1], grad_up[None], down_coefs[None]


def solution(mesh):
    return jax.shard_map(
        on_device,
        mesh=mesh,
        in_specs=(
            P(None, None, "dp"),
            P("section", "dp", "tensor"),
            P("section", "tensor", "dp"),
            P("dp", None),
            P(None, "dp", None),
        ),
        out_specs=(
            P("section", None, "dp", None),
            P("section", None, "dp", None),
            P("section", "dp", "tensor"),
            P("section", "tensor", None),
        ),
        check_vma=False,
    )
```

time: 311 us -> 252 us (0.81)
  Pallas kernels: 103 us -> 66.2 us
  local copies, waits for them, and re-layouts: 29.2 us -> 10.2 us
  waiting for transfers between devices: 89.6 us -> 99.4 us
  starting transfers between devices: 72.5 us -> 66.1 us
    pallas_call x13 -> x5, Pallas kernels: 92.3 us -> 56.8 us  [the longest x1 21.3 us: finish(): pl.pallas_call(finish_kernel, out_shape=[jax.ShapeDtypeStruct((width, hid...]
    unnamed x84 -> x36, local copies, waits for them, and re-layouts: 21.1 us -> 1.96 us
    all_to_all x3, waiting for transfers between devices: 5.81 us -> 23.9 us  [swap(): return lax.all_to_all(x, 'dp', 0, 0, tiled=True)]
    ppermute x24 -> x20, waiting for transfers between devices: 54.6 us -> 40.9 us  [to_dp(): return lax.ppermute(x, 'dp', pairs)]
    ppermute x24 -> x20, starting transfers between devices: 23.7 us -> 18.9 us  [to_dp(): return lax.ppermute(x, 'dp', pairs)]
    pallas_call x8 -> x9, Pallas kernels: 10.9 us -> 9.38 us  [call(): return pl.pallas_call(kernel, out_shape=outs, compiler_params=SMALL)(*args)]
  transfers between devices with their start and end apart: 47 -> 43, of which waited for: 24 -> 30; matrix products, arithmetic and copies ran while one was open for 7% -> 4% of each run, Pallas kernels for 24% -> 22%
where the time goes in v5:
time: 252 us; the launch traced here: 251 us
  waiting for transfers between devices  99.4 us (39%)
  Pallas kernels  66.2 us (26%)
  starting transfers between devices  66.1 us (26%)
  local copies, waits for them, and re-layouts  10.2 us (4%)
  other arithmetic  8.04 us (3%)
    ppermute x20, waiting for transfers between devices, to_dp(): return lax.ppermute(x, 'dp', pairs)  40.9 us
    all_to_all x3, waiting for transfers between devices, swap(): return lax.all_to_all(x, 'dp', 0, 0, tiled=True)  23.9 us
    ppermute x6, waiting for transfers between devices, hop(): got = lax.ppermute(pair_sum, ('section', 'tensor'), pairs)  22.4 us
    ppermute x6, starting transfers between devices, hop(): got = lax.ppermute(pair_sum, ('section', 'tensor'), pairs)  21.9 us
    pallas_call x1, Pallas kernels, finish(): pl.pallas_call(finish_kernel, out_shape=[jax.ShapeDtypeStruct((width, hid...  21.3 us
    pallas_call x2, Pallas kernels, product(): pl.pallas_call(functools.partial(product_kernel, count, plan), out_shape=...  19.6 us
    ppermute x20, starting transfers between devices, to_dp(): return lax.ppermute(x, 'dp', pairs)  18.9 us
    ppermute x14, starting transfers between devices, to_tensor(): return lax.ppermute(x, 'tensor', [(t, t ^ k) for t in range(size)])  13.6 us
  transfers between devices with their start and end apart: 43, of which 30 were waited for; matrix products, arithmetic and copies ran while one was open for 4% of the time, Pallas kernels for 22%

profile of v5, /device:TPU:1, one launch (start us, length us, event | category | flops | bytes accessed | tf_op | source)
XLA Modules:
  0.0 251.0 jit_solution(1850174898784219106)
XLA Ops:
  1.4 9.8 %shard_map.84 = (bf16[32,3584]{1,0:T(8,128)(2,1)}, bf16[32,3584]{1,0:T(8,128)(2,1)}, bf16[64,3584]{1,0:T(8,128)(2,1)}, bf16[128,3584]{1,0:T(8,128)(2,1)}, bf16[6...) custom-call(s32[8]{0:T(128)} %stack.35.place_ref, bf16[4,256,1024]{2,1,0:T(8,128)(2,1)} %refs_3_.3, ...), custom_call_target="tpu_custom_call" | custom-call | tf_op jit(solution)/shard_map/pallas_call | solution.py:153
  17.1 4.3 %shard_map.85.base_ref = bf16[1024,1024]{1,0:T(8,128)(2,1)} custom-call(s32[8]{0:T(128)} %stack.35.place_ref, bf16[4,256,1024]{2,1,0:T(8,128)(2,1)} %refs_3_.3, bf16[4,256,1024]{2,1,0:T(8,128)(2,1)} %refs_3_.3, bf16[4,256,1024]{2,1,0:T(8,128)(2,1)} %refs_3_.3, bf16[4,256,1024]{2,1,0:T(8,128)(2,1)} %refs_3_.3, bf16[4,256,1024]{2,1,0:T(8,128)(2,1)} %refs_3_.3, ...), custom_call_target="tpu_custom_call" | custom-call | tf_op jit(solution)/shard_map/pallas_call | solution.py:236
  28.1 11.5 %shard_map.86 = bf16[8,32,3712]{2,1,0:T(8,128)(2,1)} custom-call(f32[1024,128]{1,0:T(8,128)} %basis_ref.2, bf16[1024,3584]{1,0:T(8,128)(2,1)} %bitcast.24, bf16[3584,1024]{1,0:T(8,128)(2,1)} %bitcast.26), custom_call_target="tpu_custom_call" | custom-call | tf_op jit(solution)/shard_map/pallas_call | solution.py:195
  39.6 5.8 %collective-permute-done.3 = bf16[128,3584]{1,0:T(8,128)(2,1)S(1)} collective-permute-done((bf16[128,3584]{1,0:T(8,128)(2,1)S(1)}, bf16[128,3584]{1,0:T(8,128)(2,1)S(1)}, u32[]{:S(2)}, u32[]{:S(2)}) %collective-permute-start.3) | collective-permute-done | bytes 917536 | tf_op jit(solution)/shard_map/ppermute | solution.py:318
  46.8 3.9 %all-to-all-start = ((bf16[8,32,3712]{2,1,0:T(8,128)(2,1)}), bf16[8,32,3712]{2,1,0:T(8,128)(2,1)S(1)}, u32[]{:S(2)}, u32[]{:S(2)}) async-start(bf16[8,32,3712]{2,1,0:T(8,128)(2,1)} %shard_map.86), calls=%async_computation | async-start | bytes 3801088 | tf_op jit(solution)/shard_map/all_to_all | solution.py:370
  50.7 9.8 %shard_map.87 = (bf16[128,3584]{1,0:T(8,128)(2,1)}, bf16[128,3584]{1,0:T(8,128)(2,1)}, bf16[128,3584]{1,0:T(8,128)(2,1)}, bf16[128,3584]{1,0:T(8,128)(2,1)}) custom-call(s32[8]{0:T(128)} %stack.35.place_ref, bf16[4,256,1024]{2,1,0:T(8,128)(2,1)} %refs_3_.3, bf16[4,256,1024]{2,1,0:T(8,128)(2,1)} %refs_3_.3, bf16[4,256,1024]{2,1,0:T(8,128)(2,1)} %refs_3_.3, ...), custom_call_target="tpu_custom_call" | custom-call | tf_op jit(solution)/shard_map/pallas_call | solution.py:153
  64.7 11.1 %all-to-all-done.x_ref = bf16[8,32,3712]{2,1,0:T(8,128)(2,1)S(1)} async-done(((bf16[8,32,3712]{2,1,0:T(8,128)(2,1)}), bf16[8,32,3712]{2,1,0:T(8,128)(2,1)S(1)}, u32[]{:S(2)}, u32[]{:S(2)}) %all-to-all-start) | async-done | bytes 1900576 | tf_op jit(solution)/shard_map/all_to_all | solution.py:370
  75.8 2.8 %add_convert_fusion.3 = bf16[128,3584]{1,0:T(8,128)(2,1)} fusion(bf16[128,3584]{1,0:T(8,128)(2,1)} %get-tuple-element.105, bf16[64,3584]{1,0:T(8,128)(2,1)} %get-tuple-element.150, bf16[128,3584]{1,0:T(8,128)(2,1)S(1)} %collective-permute-done.3, pred[128]{0:T(512)(128)(4,1)S(1)} %copy-done.17), kind=kLoop, calls=%fused_computation.3 | loop fusion | flops 3211264 | bytes 3211392 | tf_op jit(solution)/shard_map/convert_element_type | solution.py:349
  85.2 3.6 %all-to-all-start.1 = ((bf16[8,32,3712]{2,1,0:T(8,128)(2,1)}), bf16[8,32,3712]{2,1,0:T(8,128)(2,1)S(1)}, u32[]{:S(2)}, u32[]{:S(2)}) async-start(bf16[8,32,3712]{2,1,0:T(8,128)(2,1)} %copy-done.4), calls=%async_computation.1 | async-start | bytes 3801088 | tf_op jit(solution)/shard_map/all_to_all | solution.py:370
  88.8 10.5 %collective-permute-done.6 = bf16[128,3584]{1,0:T(8,128)(2,1)S(1)} collective-permute-done((bf16[128,3584]{1,0:T(8,128)(2,1)}, bf16[128,3584]{1,0:T(8,128)(2,1)S(1)}, u32[]{:S(2)}, u32[]{:S(2)}) %collective-permute-start.6) | collective-permute-done | bytes 917536 | tf_op jit(solution)/shard_map/ppermute | solution.py:318
  100.2 13.7 %collective-permute-done.8 = bf16[128,3584]{1,0:T(8,128)(2,1)} collective-permute-done((bf16[128,3584]{1,0:T(8,128)(2,1)}, bf16[128,3584]{1,0:T(8,128)(2,1)}, u32[]{:S(2)}, u32[]{:S(2)}) %collective-permute-start.8) | collective-permute-done | bytes 917536 | tf_op jit(solution)/shard_map/ppermute | solution.py:318
  116.4 6.6 %all-to-all-done.1.all_ref = bf16[8,32,3712]{2,1,0:T(8,128)(2,1)S(1)} async-done(((bf16[8,32,3712]{2,1,0:T(8,128)(2,1)}), bf16[8,32,3712]{2,1,0:T(8,128)(2,1)S(1)}, u32[]{:S(2)}, u32[]{:S(2)}) %all-to-all-start.1) | async-done | bytes 1900576 | tf_op jit(solution)/shard_map/all_to_all | solution.py:370
  123.5 4.1 %collective-permute-start.9 = (f32[128,128]{1,0:T(8,128)S(1)}, f32[128,128]{1,0:T(8,128)S(1)}, u32[]{:S(2)}, u32[]{:S(2)}) collective-permute-start(f32[128,128]{1,0:T(8,128)S(1)} %shard_map.89), channel_id=1, source_target_pairs={{0,1},{1,0},{2,3},{3,2},{4,5},{5,4},{6,7},{7,6},{8,9},{9,8},{10,11... | collective-permute-start | bytes 196616 | tf_op jit(solution)/shard_map/ppermute | solution.py:323
  129.1 5.9 %collective-permute-start.10 = (f32[128,128]{1,0:T(8,128)S(1)}, f32[128,128]{1,0:T(8,128)S(1)}, u32[]{:S(2)}, u32[]{:S(2)}) collective-permute-start(f32[128,128]{1,0:T(8,128)S(1)} %add.190), channel_id=1, source_target_pairs={{0,32},{1,35},{2,34},{3,33},{32,64},{33,67},{34,66},{35,65},{64,96... | collective-permute-start | bytes 196616 | tf_op jit(solution)/shard_map/ppermute | solution.py:335
  140.0 6.2 %collective-permute-start.13 = (f32[128,128]{1,0:T(8,128)S(1)}, f32[128,128]{1,0:T(8,128)S(1)}, u32[]{:S(2)}, u32[]{:S(2)}) collective-permute-start(f32[128,128]{1,0:T(8,128)S(1)} %add.191), channel_id=1, source_target_pairs={{0,32},{1,35},{2,34},{3,33},{32,64},{33,67},{34,66},{35,65},{64,96... | collective-permute-start | bytes 196616 | tf_op jit(solution)/shard_map/ppermute | solution.py:335
  154.1 5.9 %collective-permute-start.19 = (f32[128,128]{1,0:T(8,128)S(1)}, f32[128,128]{1,0:T(8,128)S(1)}, u32[]{:S(2)}, u32[]{:S(2)}) collective-permute-start(f32[128,128]{1,0:T(8,128)S(1)} %add.192), channel_id=1, source_target_pairs={{0,32},{1,35},{2,34},{3,33},{32,64},{33,67},{34,66},{35,65},{64,96... | collective-permute-start | bytes 196616 | tf_op jit(solution)/shard_map/ppermute | solution.py:335
  170.4 7.0 %collective-permute-done.22.r0 = f32[128,128]{1,0:T(8,128)S(1)} collective-permute-done((f32[128,128]{1,0:T(8,128)S(1)}, f32[128,128]{1,0:T(8,128)S(1)}, u32[]{:S(2)}, u32[]{:S(2)}) %collective-permute-start.22) | collective-permute-done | bytes 65568 | tf_op jit(solution)/shard_map/ppermute | solution.py:335
  178.6 4.1 %collective-permute-done.26.refs_4_ = bf16[64,3584]{1,0:T(8,128)(2,1)} collective-permute-done((bf16[64,3584]{1,0:T(8,128)(2,1)}, bf16[64,3584]{1,0:T(8,128)(2,1)}, u32[]{:S(2)}, u32[]{:S(2)}) %collective-permute-start.26) | collective-permute-done | bytes 458784 | tf_op jit(solution)/shard_map/ppermute | solution.py:318
  185.6 2.7 %collective-permute-start.28 = (f32[128,128]{1,0:T(8,128)S(1)}, f32[128,128]{1,0:T(8,128)S(1)}, u32[]{:S(2)}, u32[]{:S(2)}) collective-permute-start(f32[128,128]{1,0:T(8,128)S(1)} %shard_map.94), channel_id=1, source_target_pairs={{0,1},{1,0},{2,3},{3,2},{4,5},{5,4},{6,7},{7,6},{8,9},{9,8},{10,11... | collective-permute-start | bytes 196616 | tf_op jit(solution)/shard_map/ppermute | solution.py:323
  190.6 6.3 %collective-permute-done.29.r0 = f32[128,128]{1,0:T(8,128)S(1)} collective-permute-done((f32[128,128]{1,0:T(8,128)S(1)}, f32[128,128]{1,0:T(8,128)S(1)}, u32[]{:S(2)}, u32[]{:S(2)}) %collective-permute-start.29) | collective-permute-done | bytes 65568 | tf_op jit(solution)/shard_map/ppermute | solution.py:335
  204.5 6.1 %collective-permute-done.34.r0 = f32[128,128]{1,0:T(8,128)S(1)} collective-permute-done((f32[128,128]{1,0:T(8,128)S(1)}, f32[128,128]{1,0:T(8,128)S(1)}, u32[]{:S(2)}, u32[]{:S(2)}) %collective-permute-start.34) | collective-permute-done | bytes 65568 | tf_op jit(solution)/shard_map/ppermute | solution.py:335
  212.7 4.2 %all-to-all-start.2 = ((bf16[8,128,256]{2,1,0:T(8,128)(2,1)}), bf16[8,128,256]{2,1,0:T(8,128)(2,1)}, u32[]{:S(2)}, u32[]{:S(2)}) async-start(bf16[8,128,256]{2,1,0:T(8,128)(2,1)} %broadcast_in_dim.12), calls=%async_computation.2 | async-start | bytes 1048576 | tf_op jit(solution)/shard_map/all_to_all | solution.py:370
  220.1 6.3 %all-to-all-done.2.ex_ref = bf16[8,128,256]{2,1,0:T(8,128)(2,1)} async-done(((bf16[8,128,256]{2,1,0:T(8,128)(2,1)}), bf16[8,128,256]{2,1,0:T(8,128)(2,1)}, u32[]{:S(2)}, u32[]{:S(2)}) %all-to-all-start.2) | async-done | bytes 524320 | tf_op jit(solution)/shard_map/all_to_all | solution.py:370
  229.0 21.3 %shard_map.97 = (bf16[1024,3584]{1,0:T(8,128)(2,1)}, f32[3584,128]{1,0:T(8,128)}) custom-call(s32[8]{0:T(128)} %stack.35.place_ref, bf16[8,128,256]{2,1,0:T(8,128)(2,1)} %all-to-all-done.2.ex_ref, bf16[8,32,3712]{2,1,0:T(8,128)(2,1)} %copy-done, bf16[1024,1024]{1,0:T(8,128)(2,1)} %shard_map.85.base_ref, f32[1024,128]{1,0:T(8,128)} %basis_ref.2, ...), custom_call_target="tpu_custom_call" | custom-call | tf_op jit(solution)/shard_map/pallas_call | solution.py:288
  (140 shorter events, 76.4 us)
Async XLA Ops:
  11.2 12.2 %collective-permute-start.2 = (bf16[64,3584]{1,0:T(8,128)(2,1)}, bf16[64,3584]{1,0:T(8,128)(2,1)S(1)}, u32[]{:S(2)}, u32[]{:S(2)}) collective-permute-start(bf16[64,3584]{1,0:T(8,128)(2,1)} %get-tuple-element.87), channel_id=1, source_target_pairs={{0,4},{4,0},{8,12},{12,8},{16,20},{20,16},{24,28},{28,24},{1,5},{5... | collective-permute-start | bytes 1376264 | tf_op jit(solution)/shard_map/ppermute | solution.py:318
  13.4 8.1 %collective-permute-start = (bf16[32,3584]{1,0:T(8,128)(2,1)}, bf16[32,3584]{1,0:T(8,128)(2,1)S(1)}, u32[]{:S(2)}, u32[]{:S(2)}) collective-permute-start(bf16[32,3584]{1,0:T(8,128)(2,1)} %get-tuple-element.85), channel_id=1, source_target_pairs={{0,8},{4,12},{8,16},{12,20},{16,24},{20,28},{24,0},{28,4},{1,9},{5... | collective-permute-start | bytes 688136 | tf_op jit(solution)/shard_map/ppermute | solution.py:318
  23.8 21.6 %collective-permute-start.3 = (bf16[128,3584]{1,0:T(8,128)(2,1)S(1)}, bf16[128,3584]{1,0:T(8,128)(2,1)S(1)}, u32[]{:S(2)}, u32[]{:S(2)}) collective-permute-start(bf16[128,3584]{1,0:T(8,128)(2,1)S(1)} %pad_maximum_fusion), channel_id=1, source_target_pairs={{0,8},{4,12},{8,16},{12,20},{16,24},{20,28},{24,0},{28,4},{1,9},{5... | collective-permute-start | bytes 2752520 | tf_op jit(solution)/shard_map/ppermute | solution.py:318
  25.4 20.1 %collective-permute-start.4 = (bf16[128,3584]{1,0:T(8,128)(2,1)S(1)}, bf16[128,3584]{1,0:T(8,128)(2,1)}, u32[]{:S(2)}, u32[]{:S(2)}) collective-permute-start(bf16[128,3584]{1,0:T(8,128)(2,1)S(1)} %pad_maximum_fusion.1), channel_id=1, source_target_pairs={{0,24},{4,28},{8,0},{12,4},{16,8},{20,12},{24,16},{28,20},{1,25},{... | collective-permute-start | bytes 2752520 | tf_op jit(solution)/shard_map/ppermute | solution.py:318
  26.7 20.1 %collective-permute-start.5 = (bf16[128,3584]{1,0:T(8,128)(2,1)}, bf16[128,3584]{1,0:T(8,128)(2,1)}, u32[]{:S(2)}, u32[]{:S(2)}) collective-permute-start(bf16[128,3584]{1,0:T(8,128)(2,1)} %get-tuple-element.96), channel_id=1, source_target_pairs={{0,4},{4,0},{8,12},{12,8},{16,20},{20,16},{24,28},{28,24},{1,5},{5... | collective-permute-start | bytes 2752520 | tf_op jit(solution)/shard_map/ppermute | solution.py:318
  46.8 29.0 %all-to-all-start = ((bf16[8,32,3712]{2,1,0:T(8,128)(2,1)}), bf16[8,32,3712]{2,1,0:T(8,128)(2,1)S(1)}, u32[]{:S(2)}, u32[]{:S(2)}) async-start(bf16[8,32,3712]{2,1,0:T(8,128)(2,1)} %shard_map.86), calls=%async_computation | async-start | bytes 3801088 | tf_op jit(solution)/shard_map/all_to_all | solution.py:370
  78.7 20.6 %collective-permute-start.6 = (bf16[128,3584]{1,0:T(8,128)(2,1)}, bf16[128,3584]{1,0:T(8,128)(2,1)S(1)}, u32[]{:S(2)}, u32[]{:S(2)}) collective-permute-start(bf16[128,3584]{1,0:T(8,128)(2,1)} %add_convert_fusion.3), channel_id=1, source_target_pairs={{0,8},{4,12},{8,16},{12,20},{16,24},{20,28},{24,0},{28,4},{1,9},{5... | collective-permute-start | bytes 2752520 | tf_op jit(solution)/shard_map/ppermute | solution.py:318
  79.9 19.7 %collective-permute-start.7 = (bf16[128,3584]{1,0:T(8,128)(2,1)}, bf16[128,3584]{1,0:T(8,128)(2,1)}, u32[]{:S(2)}, u32[]{:S(2)}) collective-permute-start(bf16[128,3584]{1,0:T(8,128)(2,1)} %add_convert_fusion.2), channel_id=1, source_target_pairs={{0,24},{4,28},{8,0},{12,4},{16,8},{20,12},{24,16},{28,20},{1,25},{... | collective-permute-start | bytes 2752520 | tf_op jit(solution)/shard_map/ppermute | solution.py:318
  83.6 30.3 %collective-permute-start.8 = (bf16[128,3584]{1,0:T(8,128)(2,1)}, bf16[128,3584]{1,0:T(8,128)(2,1)}, u32[]{:S(2)}, u32[]{:S(2)}) collective-permute-start(bf16[128,3584]{1,0:T(8,128)(2,1)} %add_convert_fusion.1), channel_id=1, source_target_pairs={{0,4},{4,0},{8,12},{12,8},{16,20},{20,16},{24,28},{28,24},{1,5},{5... | collective-permute-start | bytes 2752520 | tf_op jit(solution)/shard_map/ppermute | solution.py:318
  85.2 37.8 %all-to-all-start.1 = ((bf16[8,32,3712]{2,1,0:T(8,128)(2,1)}), bf16[8,32,3712]{2,1,0:T(8,128)(2,1)S(1)}, u32[]{:S(2)}, u32[]{:S(2)}) async-start(bf16[8,32,3712]{2,1,0:T(8,128)(2,1)} %copy-done.4), calls=%async_computation.1 | async-start | bytes 3801088 | tf_op jit(solution)/shard_map/all_to_all | solution.py:370
  127.6 22.0 %collective-permute-start.16 = (bf16[128,3584]{1,0:T(8,128)(2,1)S(1)}, bf16[128,3584]{1,0:T(8,128)(2,1)S(1)}, u32[]{:S(2)}, u32[]{:S(2)}) collective-permute-start(bf16[128,3584]{1,0:T(8,128)(2,1)S(1)} %add_convert_fusion.base_ref.refs_0_), channel_id=1, source_target_pairs={{0,24},{4,28},{8,0},{12,4},{16,8},{20,12},{24,16},{28,20},{1,25},{... | collective-permute-start | bytes 2752520 | tf_op jit(solution)/shard_map/ppermute | solution.py:318
  127.7 22.9 %collective-permute-start.15 = (bf16[128,3584]{1,0:T(8,128)(2,1)S(1)}, bf16[128,3584]{1,0:T(8,128)(2,1)}, u32[]{:S(2)}, u32[]{:S(2)}) collective-permute-start(bf16[128,3584]{1,0:T(8,128)(2,1)S(1)} %add_convert_fusion.base_ref.refs_0_), channel_id=1, source_target_pairs={{0,8},{4,12},{8,16},{12,20},{16,24},{20,28},{24,0},{28,4},{1,9},{5... | collective-permute-start | bytes 2752520 | tf_op jit(solution)/shard_map/ppermute | solution.py:318
  136.4 14.3 %collective-permute-start.17 = (bf16[64,3584]{1,0:T(8,128)(2,1)S(1)}, bf16[64,3584]{1,0:T(8,128)(2,1)}, u32[]{:S(2)}, u32[]{:S(2)}) collective-permute-start(bf16[64,3584]{1,0:T(8,128)(2,1)S(1)} %get-tuple-element.115), channel_id=1, source_target_pairs={{0,4},{4,0},{8,12},{12,8},{16,20},{20,16},{24,28},{28,24},{1,5},{5... | collective-permute-start | bytes 1376264 | tf_op jit(solution)/shard_map/ppermute | solution.py:318
  150.6 32.0 %collective-permute-start.24 = (bf16[128,3584]{1,0:T(8,128)(2,1)}, bf16[128,3584]{1,0:T(8,128)(2,1)}, u32[]{:S(2)}, u32[]{:S(2)}) collective-permute-start(bf16[128,3584]{1,0:T(8,128)(2,1)} %collective-permute-done.15.refs_3_), channel_id=1, source_target_pairs={{0,8},{4,12},{8,16},{12,20},{16,24},{20,28},{24,0},{28,4},{1,9},{5... | collective-permute-start | bytes 2752520 | tf_op jit(solution)/shard_map/ppermute | solution.py:318
  161.3 17.2 %collective-permute-start.25 = (bf16[64,3584]{1,0:T(8,128)(2,1)}, bf16[64,3584]{1,0:T(8,128)(2,1)}, u32[]{:S(2)}, u32[]{:S(2)}) collective-permute-start(bf16[64,3584]{1,0:T(8,128)(2,1)} %get-tuple-element.124), channel_id=1, source_target_pairs={{0,4},{4,0},{8,12},{12,8},{16,20},{20,16},{24,28},{28,24},{1,5},{5... | collective-permute-start | bytes 1376264 | tf_op jit(solution)/shard_map/ppermute | solution.py:318
  162.6 16.0 %collective-permute-start.27 = (bf16[64,3584]{1,0:T(8,128)(2,1)}, bf16[64,3584]{1,0:T(8,128)(2,1)}, u32[]{:S(2)}, u32[]{:S(2)}) collective-permute-start(bf16[64,3584]{1,0:T(8,128)(2,1)} %collective-permute-done.17.refs_1_), channel_id=1, source_target_pairs={{0,24},{4,28},{8,0},{12,4},{16,8},{20,12},{24,16},{28,20},{1,25},{... | collective-permute-start | bytes 1376264 | tf_op jit(solution)/shard_map/ppermute | solution.py:318
  165.1 17.6 %collective-permute-start.26 = (bf16[64,3584]{1,0:T(8,128)(2,1)}, bf16[64,3584]{1,0:T(8,128)(2,1)}, u32[]{:S(2)}, u32[]{:S(2)}) collective-permute-start(bf16[64,3584]{1,0:T(8,128)(2,1)} %collective-permute-done.17.refs_1_), channel_id=1, source_target_pairs={{0,8},{4,12},{8,16},{12,20},{16,24},{20,28},{24,0},{28,4},{1,9},{5... | collective-permute-start | bytes 1376264 | tf_op jit(solution)/shard_map/ppermute | solution.py:318
  169.1 8.3 %collective-permute-start.22 = (f32[128,128]{1,0:T(8,128)S(1)}, f32[128,128]{1,0:T(8,128)S(1)}, u32[]{:S(2)}, u32[]{:S(2)}) collective-permute-start(f32[128,128]{1,0:T(8,128)S(1)} %add.193), channel_id=1, source_target_pairs={{32,0},{33,3},{34,2},{35,1},{64,32},{65,35},{66,34},{67,33},{96,64... | collective-permute-start | bytes 196616 | tf_op jit(solution)/shard_map/ppermute | solution.py:335
  182.7 15.4 %collective-permute-start.32 = (bf16[64,3584]{1,0:T(8,128)(2,1)}, bf16[64,3584]{1,0:T(8,128)(2,1)}, u32[]{:S(2)}, u32[]{:S(2)}) collective-permute-start(bf16[64,3584]{1,0:T(8,128)(2,1)} %collective-permute-done.25.refs_2_), channel_id=1, source_target_pairs={{0,24},{4,28},{8,0},{12,4},{16,8},{20,12},{24,16},{28,20},{1,25},{... | collective-permute-start | bytes 1376264 | tf_op jit(solution)/shard_map/ppermute | solution.py:318
  182.7 15.4 %collective-permute-start.31 = (bf16[64,3584]{1,0:T(8,128)(2,1)}, bf16[64,3584]{1,0:T(8,128)(2,1)S(1)}, u32[]{:S(2)}, u32[]{:S(2)}) collective-permute-start(bf16[64,3584]{1,0:T(8,128)(2,1)} %collective-permute-done.25.refs_2_), channel_id=1, source_target_pairs={{0,8},{4,12},{8,16},{12,20},{16,24},{20,28},{24,0},{28,4},{1,9},{5... | collective-permute-start | bytes 1376264 | tf_op jit(solution)/shard_map/ppermute | solution.py:318
  196.8 13.8 %collective-permute-start.36 = (bf16[64,3584]{1,0:T(8,128)(2,1)}, bf16[64,3584]{1,0:T(8,128)(2,1)}, u32[]{:S(2)}, u32[]{:S(2)}) collective-permute-start(bf16[64,3584]{1,0:T(8,128)(2,1)} %collective-permute-done.26.refs_4_), channel_id=1, source_target_pairs={{0,8},{4,12},{8,16},{12,20},{16,24},{20,28},{24,0},{28,4},{1,9},{5... | collective-permute-start | bytes 1376264 | tf_op jit(solution)/shard_map/ppermute | solution.py:318
  198.1 13.8 %collective-permute-start.37 = (bf16[64,3584]{1,0:T(8,128)(2,1)}, bf16[64,3584]{1,0:T(8,128)(2,1)}, u32[]{:S(2)}, u32[]{:S(2)}) collective-permute-start(bf16[64,3584]{1,0:T(8,128)(2,1)} %collective-permute-done.32.refs_8_), channel_id=1, source_target_pairs={{0,24},{4,28},{8,0},{12,4},{16,8},{20,12},{24,16},{28,20},{1,25},{... | collective-permute-start | bytes 1376264 | tf_op jit(solution)/shard_map/ppermute | solution.py:318
  212.7 13.6 %all-to-all-start.2 = ((bf16[8,128,256]{2,1,0:T(8,128)(2,1)}), bf16[8,128,256]{2,1,0:T(8,128)(2,1)}, u32[]{:S(2)}, u32[]{:S(2)}) async-start(bf16[8,128,256]{2,1,0:T(8,128)(2,1)} %broadcast_in_dim.12), calls=%async_computation.2 | async-start | bytes 1048576 | tf_op jit(solution)/shard_map/all_to_all | solution.py:370
  226.4 24.0 %collective-permute-start.39 = (f32[256,128]{1,0:T(8,128)S(1)}, f32[256,128]{1,0:T(8,128)S(1)}, u32[]{:S(2)}, u32[]{:S(2)}) collective-permute-start(f32[256,128]{1,0:T(8,128)S(1)} %fusion), channel_id=1, source_target_pairs={{0,2},{1,3},{2,0},{3,1},{4,6},{5,7},{6,4},{7,5},{8,10},{9,11},{10,... | collective-permute-start | bytes 393224 | tf_op jit(solution)/shard_map/ppermute | solution.py:323
  (38 other events, 367.3 us)

commit v6 on v5

--- a/solution.py
+++ b/solution.py
@@ -405,10 +405,9 @@
     up, down, other, basis_1 = tie(up, down, other, basis)
     up, down, other = to_dp(up, 1, 0), to_dp(down, -1, 0), to_dp(other, 0, 1)
     proj = project(basis_1, w_in, w_out, dp)
-    up, down, other, proj, base_2 = tie(up, down, other, proj, base_1)
+    up, down, base_2 = tie(up, down, base_1)
     proj = swap(proj)
     late = product(place, base_2, w_in, dp, LATE, [[(j, 0, own)] for j in range(len(LATE))])
-    proj, late = tie(proj, late)
     proj = call(functools.partial(fold_kernel, rank), jax.ShapeDtypeStruct(proj.shape, BF), proj)
     everyone = swap(proj)
     left, right, side, mine = late
@@ -424,10 +423,10 @@
     got, _, _ = hop(part, 1)
     got, left, right, side_low, high = tie(got, left, right, side_low, mine[1])
     side_high = to_dp(high, 0, 1)
-    far = to_dp(left, 1, 0)
+    far_0, far_1 = to_dp(left[:h], 1, 0), to_dp(right[h:], -1, 0)
     part = call(forward_kernel, tok, own_pre, everyone, *got)
     got, _, _ = hop(part, 1)
-    got, side_low = tie(got, side_low)
+    got, far_0, far_1 = tie(got, far_0, far_1)
     left_low, right_low = to_dp(side_low, 1, 0), to_dp(side_low, -1, 0)
     c_in, coef_part, slope = call(
         middle_kernel,
@@ -440,7 +439,7 @@
         return call(backward_kernel, tok, last, slope, everyone, cot, *got)
 
     got, _, _ = hop(back((cot, cot)), -1)
-    got, far, side_high, left_low, right_low = tie(got, far, side_high, left_low, right_low)
+    got, side_high, left_low, right_low = tie(got, side_high, left_low, right_low)
     left_high, right_high = to_dp(side_high, 1, 0), to_dp(side_high, -1, 0)
     far_low = to_dp(left_low, 1, 0)
     got, _, _ = hop(back(got), -1)
@@ -456,7 +455,7 @@
     ex, parts = tie(ex, parts)
     pieces = [
         own_pre, side_low, side_high, left, left_low, left_high,
-        right, right_low, right_high, far, far_low, far_high,
+        right, right_low, right_high, far_0, far_1, far_low, far_high,
     ]
     grad_up, down_coefs = finish(place, ex, everyone, base_t, basis, pieces)
     parts = (parts + to_tensor(parts, 2)).reshape(2, 1, micro, rows, rank)

time: 252 us -> 239 us (0.948)
  waiting for transfers between devices: 99.4 us -> 81.1 us
  starting transfers between devices: 66.1 us -> 69.3 us
    ppermute x20 -> x21, waiting for transfers between devices: 40.9 us -> 19.6 us  [to_dp(): return lax.ppermute(x, 'dp', pairs)]
    ppermute x20 -> x21, starting transfers between devices: 18.9 us -> 25.4 us  [to_dp(): return lax.ppermute(x, 'dp', pairs)]
    ppermute x14, starting transfers between devices: 13.6 us -> 9.64 us  [to_tensor(): return lax.ppermute(x, 'tensor', [(t, t ^ k) for t in range(size)])]
    all_to_all x3, waiting for transfers between devices: 23.9 us -> 26.7 us  [swap(): return lax.all_to_all(x, 'dp', 0, 0, tiled=True)]
  transfers between devices with their start and end apart: 43 -> 44, of which waited for: 30 -> 26; matrix products, arithmetic and copies ran while one was open for 4% -> 4% of each run, Pallas kernels for 22% -> 24%
where the time goes in v6:
time: 239 us; the launch traced here: 236 us
  waiting for transfers between devices  81.1 us (34%)
  starting transfers between devices  69.3 us (29%)
  Pallas kernels  66.2 us (28%)
  local copies, waits for them, and re-layouts  10.3 us (4%)
  other arithmetic  8.41 us (4%)
    all_to_all x3, waiting for transfers between devices, swap(): return lax.all_to_all(x, 'dp', 0, 0, tiled=True)  26.7 us
    ppermute x21, starting transfers between devices, to_dp(): return lax.ppermute(x, 'dp', pairs)  25.4 us
    ppermute x6, waiting for transfers between devices, hop(): got = lax.ppermute(pair_sum, ('section', 'tensor'), pairs)  23.9 us
    ppermute x6, starting transfers between devices, hop(): got = lax.ppermute(pair_sum, ('section', 'tensor'), pairs)  22.1 us
    pallas_call x1, Pallas kernels, finish(): pl.pallas_call(finish_kernel, out_shape=[jax.ShapeDtypeStruct((width, hid...  21.4 us
    ppermute x21, waiting for transfers between devices, to_dp(): return lax.ppermute(x, 'dp', pairs)  19.6 us
    pallas_call x2, Pallas kernels, product(): pl.pallas_call(functools.partial(product_kernel, count, plan), out_shape=...  19.6 us
    all_to_all x3, starting transfers between devices, swap(): return lax.all_to_all(x, 'dp', 0, 0, tiled=True)  12.2 us
  transfers between devices with their start and end apart: 44, of which 26 were waited for; matrix products, arithmetic and copies ran while one was open for 4% of the time, Pallas kernels for 24%

profile of v6, /device:TPU:1, one launch (start us, length us, event | category | flops | bytes accessed | tf_op | source)
XLA Modules:
  0.0 236.5 jit_solution(12178273141139024105)
XLA Ops:
  1.4 9.8 %shard_map.84 = (bf16[32,3584]{1,0:T(8,128)(2,1)}, bf16[32,3584]{1,0:T(8,128)(2,1)}, bf16[64,3584]{1,0:T(8,128)(2,1)}, bf16[128,3584]{1,0:T(8,128)(2,1)}, bf16[6...) custom-call(s32[8]{0:T(128)} %stack.35.place_ref, bf16[4,256,1024]{2,1,0:T(8,128)(2,1)} %refs_3_.3, ...), custom_call_target="tpu_custom_call" | custom-call | tf_op jit(solution)/shard_map/pallas_call | solution.py:153
  11.2 2.2 collective-permute-start.2
  17.1 4.3 %shard_map.85.base_ref = bf16[1024,1024]{1,0:T(8,128)(2,1)} custom-call(s32[8]{0:T(128)} %stack.35.place_ref, bf16[4,256,1024]{2,1,0:T(8,128)(2,1)} %refs_3_.3, bf16[4,256,1024]{2,1,0:T(8,128)(2,1)} %refs_3_.3, bf16[4,256,1024]{2,1,0:T(8,128)(2,1)} %refs_3_.3, bf16[4,256,1024]{2,1,0:T(8,128)(2,1)} %refs_3_.3, bf16[4,256,1024]{2,1,0:T(8,128)(2,1)} %refs_3_.3, ...), custom_call_target="tpu_custom_call" | custom-call | tf_op jit(solution)/shard_map/pallas_call | solution.py:236
  29.8 11.5 %shard_map.87 = bf16[8,32,3712]{2,1,0:T(8,128)(2,1)} custom-call(f32[1024,128]{1,0:T(8,128)} %basis_ref.2, bf16[1024,3584]{1,0:T(8,128)(2,1)} %bitcast.24, bf16[3584,1024]{1,0:T(8,128)(2,1)} %bitcast.26), custom_call_target="tpu_custom_call" | custom-call | tf_op jit(solution)/shard_map/pallas_call | solution.py:195
  41.3 3.6 %all-to-all-start = ((bf16[8,32,3712]{2,1,0:T(8,128)(2,1)}), bf16[8,32,3712]{2,1,0:T(8,128)(2,1)S(1)}, u32[]{:S(2)}, u32[]{:S(2)}) async-start(bf16[8,32,3712]{2,1,0:T(8,128)(2,1)} %shard_map.87), calls=%async_computation | async-start | bytes 3801088 | tf_op jit(solution)/shard_map/all_to_all | solution.py:370
  44.9 2.4 %collective-permute-done.3 = bf16[128,3584]{1,0:T(8,128)(2,1)S(1)} collective-permute-done((bf16[128,3584]{1,0:T(8,128)(2,1)}, bf16[128,3584]{1,0:T(8,128)(2,1)S(1)}, u32[]{:S(2)}, u32[]{:S(2)}) %collective-permute-start.3) | collective-permute-done | bytes 917536 | tf_op jit(solution)/shard_map/ppermute | solution.py:318
  47.4 9.8 %shard_map.86 = (bf16[128,3584]{1,0:T(8,128)(2,1)}, bf16[128,3584]{1,0:T(8,128)(2,1)}, bf16[128,3584]{1,0:T(8,128)(2,1)}, bf16[128,3584]{1,0:T(8,128)(2,1)}) custom-call(s32[8]{0:T(128)} %stack.35.place_ref, bf16[4,256,1024]{2,1,0:T(8,128)(2,1)} %refs_3_.3, bf16[4,256,1024]{2,1,0:T(8,128)(2,1)} %refs_3_.3, bf16[4,256,1024]{2,1,0:T(8,128)(2,1)} %refs_3_.3, ...), custom_call_target="tpu_custom_call" | custom-call | tf_op jit(solution)/shard_map/pallas_call | solution.py:153
  67.7 2.6 %all-to-all-done.x_ref = bf16[8,32,3712]{2,1,0:T(8,128)(2,1)S(1)} async-done(((bf16[8,32,3712]{2,1,0:T(8,128)(2,1)}), bf16[8,32,3712]{2,1,0:T(8,128)(2,1)S(1)}, u32[]{:S(2)}, u32[]{:S(2)}) %all-to-all-start) | async-done | bytes 1900576 | tf_op jit(solution)/shard_map/all_to_all | solution.py:370
  71.7 4.3 %all-to-all-start.1 = ((bf16[8,32,3712]{2,1,0:T(8,128)(2,1)}), bf16[8,32,3712]{2,1,0:T(8,128)(2,1)S(1)}, u32[]{:S(2)}, u32[]{:S(2)}) async-start(bf16[8,32,3712]{2,1,0:T(8,128)(2,1)} %copy-done.4), calls=%async_computation.1 | async-start | bytes 3801088 | tf_op jit(solution)/shard_map/all_to_all | solution.py:370
  76.0 11.4 %collective-permute-done.6 = bf16[128,3584]{1,0:T(8,128)(2,1)S(1)} collective-permute-done((bf16[128,3584]{1,0:T(8,128)(2,1)}, bf16[128,3584]{1,0:T(8,128)(2,1)S(1)}, u32[]{:S(2)}, u32[]{:S(2)}) %collective-permute-start.6) | collective-permute-done | bytes 917536 | tf_op jit(solution)/shard_map/ppermute | solution.py:318
  88.3 2.5 %add_convert_fusion.base_ref.refs_0_ = bf16[128,3584]{1,0:T(8,128)(2,1)S(1)} fusion(bf16[128,3584]{1,0:T(8,128)(2,1)} %collective-permute-done.8, bf16[128,3584]{1,0:T(8,128)(2,1)} %collective-permute-done.7, bf16[128,3584]{1,0:T(8,128)(2,1)} %copy-done.10, bf16[128,3584]{1,0:T(8,128)(2,1)} %get-tuple-element.90), kind=kLoop, calls=%fused_computation | loop fusion | flops 3670016 | bytes 4587520 | tf_op jit(solution)/shard_map/convert_element_type | solution.py:416
  90.8 18.0 %all-to-all-done.1.all_ref = bf16[8,32,3712]{2,1,0:T(8,128)(2,1)S(1)} async-done(((bf16[8,32,3712]{2,1,0:T(8,128)(2,1)}), bf16[8,32,3712]{2,1,0:T(8,128)(2,1)S(1)}, u32[]{:S(2)}, u32[]{:S(2)}) %all-to-all-start.1) | async-done | bytes 1900576 | tf_op jit(solution)/shard_map/all_to_all | solution.py:370
  109.3 3.5 %collective-permute-start.9 = (f32[128,128]{1,0:T(8,128)S(1)}, f32[128,128]{1,0:T(8,128)S(1)}, u32[]{:S(2)}, u32[]{:S(2)}) collective-permute-start(f32[128,128]{1,0:T(8,128)S(1)} %shard_map.89), channel_id=1, source_target_pairs={{0,1},{1,0},{2,3},{3,2},{4,5},{5,4},{6,7},{7,6},{8,9},{9,8},{10,11... | collective-permute-start | bytes 196616 | tf_op jit(solution)/shard_map/ppermute | solution.py:323
  112.9 2.8 %collective-permute-start.16 = (bf16[128,3584]{1,0:T(8,128)(2,1)S(1)}, bf16[128,3584]{1,0:T(8,128)(2,1)S(1)}, u32[]{:S(2)}, u32[]{:S(2)}) collective-permute-start(bf16[128,3584]{1,0:T(8,128)(2,1)S(1)} %add_convert_fusion.base_ref.refs_0_), channel_id=1, source_target_pairs={{0,24},{4,28},{8,0},{12,4},{16,8},{20,12},{24,16},{28,20},{1,25},{... | collective-permute-start | bytes 2752520 | tf_op jit(solution)/shard_map/ppermute | solution.py:318
  115.7 5.7 %collective-permute-start.10 = (f32[128,128]{1,0:T(8,128)S(1)}, f32[128,128]{1,0:T(8,128)S(1)}, u32[]{:S(2)}, u32[]{:S(2)}) collective-permute-start(f32[128,128]{1,0:T(8,128)S(1)} %add.190), channel_id=1, source_target_pairs={{0,32},{1,35},{2,34},{3,33},{32,64},{33,67},{34,66},{35,65},{64,96... | collective-permute-start | bytes 196616 | tf_op jit(solution)/shard_map/ppermute | solution.py:335
  128.0 6.7 %collective-permute-start.13 = (f32[128,128]{1,0:T(8,128)S(1)}, f32[128,128]{1,0:T(8,128)S(1)}, u32[]{:S(2)}, u32[]{:S(2)}) collective-permute-start(f32[128,128]{1,0:T(8,128)S(1)} %add.191), channel_id=1, source_target_pairs={{0,32},{1,35},{2,34},{3,33},{32,64},{33,67},{34,66},{35,65},{64,96... | collective-permute-start | bytes 196616 | tf_op jit(solution)/shard_map/ppermute | solution.py:335
  136.0 2.5 %collective-permute-done.15.refs_3_ = bf16[128,3584]{1,0:T(8,128)(2,1)S(1)} collective-permute-done((bf16[128,3584]{1,0:T(8,128)(2,1)S(1)}, bf16[128,3584]{1,0:T(8,128)(2,1)S(1)}, u32[]{:S(2)}, u32[]{:S(2)}) %collective-permute-start.15) | collective-permute-done | bytes 917536 | tf_op jit(solution)/shard_map/ppermute | solution.py:318
  145.3 5.7 %collective-permute-start.19 = (f32[128,128]{1,0:T(8,128)S(1)}, f32[128,128]{1,0:T(8,128)S(1)}, u32[]{:S(2)}, u32[]{:S(2)}) collective-permute-start(f32[128,128]{1,0:T(8,128)S(1)} %add.192), channel_id=1, source_target_pairs={{0,32},{1,35},{2,34},{3,33},{32,64},{33,67},{34,66},{35,65},{64,96... | collective-permute-start | bytes 196616 | tf_op jit(solution)/shard_map/ppermute | solution.py:335
  161.6 8.5 %collective-permute-done.24.r0 = f32[128,128]{1,0:T(8,128)S(1)} collective-permute-done((f32[128,128]{1,0:T(8,128)S(1)}, f32[128,128]{1,0:T(8,128)S(1)}, u32[]{:S(2)}, u32[]{:S(2)}) %collective-permute-start.24) | collective-permute-done | bytes 65568 | tf_op jit(solution)/shard_map/ppermute | solution.py:335
  177.4 6.1 %collective-permute-done.30.r0 = f32[128,128]{1,0:T(8,128)S(1)} collective-permute-done((f32[128,128]{1,0:T(8,128)S(1)}, f32[128,128]{1,0:T(8,128)S(1)}, u32[]{:S(2)}, u32[]{:S(2)}) %collective-permute-start.30) | collective-permute-done | bytes 65568 | tf_op jit(solution)/shard_map/ppermute | solution.py:335
  191.8 6.1 %collective-permute-done.35.r0 = f32[128,128]{1,0:T(8,128)S(1)} collective-permute-done((f32[128,128]{1,0:T(8,128)S(1)}, f32[128,128]{1,0:T(8,128)S(1)}, u32[]{:S(2)}, u32[]{:S(2)}) %collective-permute-start.35) | collective-permute-done | bytes 65568 | tf_op jit(solution)/shard_map/ppermute | solution.py:335
  200.1 4.4 %all-to-all-start.2 = ((bf16[8,128,256]{2,1,0:T(8,128)(2,1)}), bf16[8,128,256]{2,1,0:T(8,128)(2,1)}, u32[]{:S(2)}, u32[]{:S(2)}) async-start(bf16[8,128,256]{2,1,0:T(8,128)(2,1)} %broadcast_in_dim.12), calls=%async_computation.2 | async-start | bytes 1048576 | tf_op jit(solution)/shard_map/all_to_all | solution.py:370
  207.4 6.1 %all-to-all-done.2.ex_ref = bf16[8,128,256]{2,1,0:T(8,128)(2,1)} async-done(((bf16[8,128,256]{2,1,0:T(8,128)(2,1)}), bf16[8,128,256]{2,1,0:T(8,128)(2,1)}, u32[]{:S(2)}, u32[]{:S(2)}) %all-to-all-start.2) | async-done | bytes 524320 | tf_op jit(solution)/shard_map/all_to_all | solution.py:370
  214.4 21.4 %shard_map.97 = (bf16[1024,3584]{1,0:T(8,128)(2,1)}, f32[3584,128]{1,0:T(8,128)}) custom-call(s32[8]{0:T(128)} %stack.35.place_ref, bf16[8,128,256]{2,1,0:T(8,128)(2,1)} %all-to-all-done.2.ex_ref, bf16[8,32,3712]{2,1,0:T(8,128)(2,1)} %copy-done, bf16[1024,1024]{1,0:T(8,128)(2,1)} %shard_map.85.base_ref, f32[1024,128]{1,0:T(8,128)} %basis_ref.2, ...), custom_call_target="tpu_custom_call" | custom-call | tf_op jit(solution)/shard_map/pallas_call | solution.py:288
  (144 shorter events, 73.5 us)
Async XLA Ops:
  11.2 12.2 %collective-permute-start.2 = (bf16[64,3584]{1,0:T(8,128)(2,1)}, bf16[64,3584]{1,0:T(8,128)(2,1)S(1)}, u32[]{:S(2)}, u32[]{:S(2)}) collective-permute-start(bf16[64,3584]{1,0:T(8,128)(2,1)} %get-tuple-element.80), channel_id=1, source_target_pairs={{0,4},{4,0},{8,12},{12,8},{16,20},{20,16},{24,28},{28,24},{1,5},{5... | collective-permute-start | bytes 1376264 | tf_op jit(solution)/shard_map/ppermute | solution.py:318
  25.6 21.7 %collective-permute-start.3 = (bf16[128,3584]{1,0:T(8,128)(2,1)}, bf16[128,3584]{1,0:T(8,128)(2,1)S(1)}, u32[]{:S(2)}, u32[]{:S(2)}) collective-permute-start(bf16[128,3584]{1,0:T(8,128)(2,1)} %pad_maximum_fusion), channel_id=1, source_target_pairs={{0,8},{4,12},{8,16},{12,20},{16,24},{20,28},{24,0},{28,4},{1,9},{5... | collective-permute-start | bytes 2752520 | tf_op jit(solution)/shard_map/ppermute | solution.py:318
  27.1 20.3 %collective-permute-start.4 = (bf16[128,3584]{1,0:T(8,128)(2,1)}, bf16[128,3584]{1,0:T(8,128)(2,1)}, u32[]{:S(2)}, u32[]{:S(2)}) collective-permute-start(bf16[128,3584]{1,0:T(8,128)(2,1)} %pad_maximum_fusion.1), channel_id=1, source_target_pairs={{0,24},{4,28},{8,0},{12,4},{16,8},{20,12},{24,16},{28,20},{1,25},{... | collective-permute-start | bytes 2752520 | tf_op jit(solution)/shard_map/ppermute | solution.py:318
  28.3 30.2 %collective-permute-start.5 = (bf16[128,3584]{1,0:T(8,128)(2,1)}, bf16[128,3584]{1,0:T(8,128)(2,1)}, u32[]{:S(2)}, u32[]{:S(2)}) collective-permute-start(bf16[128,3584]{1,0:T(8,128)(2,1)} %get-tuple-element.93), channel_id=1, source_target_pairs={{0,4},{4,0},{8,12},{12,8},{16,20},{20,16},{24,28},{28,24},{1,5},{5... | collective-permute-start | bytes 2752520 | tf_op jit(solution)/shard_map/ppermute | solution.py:318
  41.3 28.9 %all-to-all-start = ((bf16[8,32,3712]{2,1,0:T(8,128)(2,1)}), bf16[8,32,3712]{2,1,0:T(8,128)(2,1)S(1)}, u32[]{:S(2)}, u32[]{:S(2)}) async-start(bf16[8,32,3712]{2,1,0:T(8,128)(2,1)} %shard_map.87), calls=%async_computation | async-start | bytes 3801088 | tf_op jit(solution)/shard_map/all_to_all | solution.py:370
  61.2 26.1 %collective-permute-start.6 = (bf16[128,3584]{1,0:T(8,128)(2,1)}, bf16[128,3584]{1,0:T(8,128)(2,1)S(1)}, u32[]{:S(2)}, u32[]{:S(2)}) collective-permute-start(bf16[128,3584]{1,0:T(8,128)(2,1)} %add_convert_fusion.3), channel_id=1, source_target_pairs={{0,8},{4,12},{8,16},{12,20},{16,24},{20,28},{24,0},{28,4},{1,9},{5... | collective-permute-start | bytes 2752520 | tf_op jit(solution)/shard_map/ppermute | solution.py:318
  63.6 23.9 %collective-permute-start.7 = (bf16[128,3584]{1,0:T(8,128)(2,1)}, bf16[128,3584]{1,0:T(8,128)(2,1)}, u32[]{:S(2)}, u32[]{:S(2)}) collective-permute-start(bf16[128,3584]{1,0:T(8,128)(2,1)} %add_convert_fusion.2), channel_id=1, source_target_pairs={{0,24},{4,28},{8,0},{12,4},{16,8},{20,12},{24,16},{28,20},{1,25},{... | collective-permute-start | bytes 2752520 | tf_op jit(solution)/shard_map/ppermute | solution.py:318
  66.1 21.4 %collective-permute-start.8 = (bf16[128,3584]{1,0:T(8,128)(2,1)}, bf16[128,3584]{1,0:T(8,128)(2,1)}, u32[]{:S(2)}, u32[]{:S(2)}) collective-permute-start(bf16[128,3584]{1,0:T(8,128)(2,1)} %add_convert_fusion.1), channel_id=1, source_target_pairs={{0,4},{4,0},{8,12},{12,8},{16,20},{20,16},{24,28},{28,24},{1,5},{5... | collective-permute-start | bytes 2752520 | tf_op jit(solution)/shard_map/ppermute | solution.py:318
  71.7 37.1 %all-to-all-start.1 = ((bf16[8,32,3712]{2,1,0:T(8,128)(2,1)}), bf16[8,32,3712]{2,1,0:T(8,128)(2,1)S(1)}, u32[]{:S(2)}, u32[]{:S(2)}) async-start(bf16[8,32,3712]{2,1,0:T(8,128)(2,1)} %copy-done.4), calls=%async_computation.1 | async-start | bytes 3801088 | tf_op jit(solution)/shard_map/all_to_all | solution.py:370
  112.9 23.2 %collective-permute-start.16 = (bf16[128,3584]{1,0:T(8,128)(2,1)S(1)}, bf16[128,3584]{1,0:T(8,128)(2,1)S(1)}, u32[]{:S(2)}, u32[]{:S(2)}) collective-permute-start(bf16[128,3584]{1,0:T(8,128)(2,1)S(1)} %add_convert_fusion.base_ref.refs_0_), channel_id=1, source_target_pairs={{0,24},{4,28},{8,0},{12,4},{16,8},{20,12},{24,16},{28,20},{1,25},{... | collective-permute-start | bytes 2752520 | tf_op jit(solution)/shard_map/ppermute | solution.py:318
  115.7 22.8 %collective-permute-start.15 = (bf16[128,3584]{1,0:T(8,128)(2,1)S(1)}, bf16[128,3584]{1,0:T(8,128)(2,1)S(1)}, u32[]{:S(2)}, u32[]{:S(2)}) collective-permute-start(bf16[128,3584]{1,0:T(8,128)(2,1)S(1)} %add_convert_fusion.base_ref.refs_0_), channel_id=1, source_target_pairs={{0,8},{4,12},{8,16},{12,20},{16,24},{20,28},{24,0},{28,4},{1,9},{5... | collective-permute-start | bytes 2752520 | tf_op jit(solution)/shard_map/ppermute | solution.py:318
  122.8 15.7 %collective-permute-start.17 = (bf16[64,3584]{1,0:T(8,128)(2,1)S(1)}, bf16[64,3584]{1,0:T(8,128)(2,1)}, u32[]{:S(2)}, u32[]{:S(2)}) collective-permute-start(bf16[64,3584]{1,0:T(8,128)(2,1)S(1)} %get-tuple-element.101), channel_id=1, source_target_pairs={{0,4},{4,0},{8,12},{12,8},{16,20},{20,16},{24,28},{28,24},{1,5},{5... | collective-permute-start | bytes 1376264 | tf_op jit(solution)/shard_map/ppermute | solution.py:318
  140.2 15.2 %collective-permute-start.22 = (bf16[64,3584]{1,0:T(8,128)(2,1)}, bf16[64,3584]{1,0:T(8,128)(2,1)}, u32[]{:S(2)}, u32[]{:S(2)}) collective-permute-start(bf16[64,3584]{1,0:T(8,128)(2,1)} %slice.53), channel_id=1, source_target_pairs={{0,24},{4,28},{8,0},{12,4},{16,8},{20,12},{24,16},{28,20},{1,25},{... | collective-permute-start | bytes 1376264 | tf_op jit(solution)/shard_map/ppermute | solution.py:318
  141.6 13.8 %collective-permute-start.21 = (bf16[64,3584]{1,0:T(8,128)(2,1)}, bf16[64,3584]{1,0:T(8,128)(2,1)}, u32[]{:S(2)}, u32[]{:S(2)}) collective-permute-start(bf16[64,3584]{1,0:T(8,128)(2,1)} %slice.52), channel_id=1, source_target_pairs={{0,8},{4,12},{8,16},{12,20},{16,24},{20,28},{24,0},{28,4},{1,9},{5... | collective-permute-start | bytes 1376264 | tf_op jit(solution)/shard_map/ppermute | solution.py:318
  152.3 17.9 %collective-permute-start.26 = (bf16[64,3584]{1,0:T(8,128)(2,1)}, bf16[64,3584]{1,0:T(8,128)(2,1)}, u32[]{:S(2)}, u32[]{:S(2)}) collective-permute-start(bf16[64,3584]{1,0:T(8,128)(2,1)} %get-tuple-element.110), channel_id=1, source_target_pairs={{0,4},{4,0},{8,12},{12,8},{16,20},{20,16},{24,28},{28,24},{1,5},{5... | collective-permute-start | bytes 1376264 | tf_op jit(solution)/shard_map/ppermute | solution.py:318
  154.0 16.2 %collective-permute-start.28 = (bf16[64,3584]{1,0:T(8,128)(2,1)}, bf16[64,3584]{1,0:T(8,128)(2,1)}, u32[]{:S(2)}, u32[]{:S(2)}) collective-permute-start(bf16[64,3584]{1,0:T(8,128)(2,1)} %collective-permute-done.17.refs_1_), channel_id=1, source_target_pairs={{0,24},{4,28},{8,0},{12,4},{16,8},{20,12},{24,16},{28,20},{1,25},{... | collective-permute-start | bytes 1376264 | tf_op jit(solution)/shard_map/ppermute | solution.py:318
  155.2 15.0 %collective-permute-start.27 = (bf16[64,3584]{1,0:T(8,128)(2,1)}, bf16[64,3584]{1,0:T(8,128)(2,1)}, u32[]{:S(2)}, u32[]{:S(2)}) collective-permute-start(bf16[64,3584]{1,0:T(8,128)(2,1)} %collective-permute-done.17.refs_1_), channel_id=1, source_target_pairs={{0,8},{4,12},{8,16},{12,20},{16,24},{20,28},{24,0},{28,4},{1,9},{5... | collective-permute-start | bytes 1376264 | tf_op jit(solution)/shard_map/ppermute | solution.py:318
  160.3 9.8 %collective-permute-start.24 = (f32[128,128]{1,0:T(8,128)S(1)}, f32[128,128]{1,0:T(8,128)S(1)}, u32[]{:S(2)}, u32[]{:S(2)}) collective-permute-start(f32[128,128]{1,0:T(8,128)S(1)} %add.193), channel_id=1, source_target_pairs={{32,0},{33,3},{34,2},{35,1},{64,32},{65,35},{66,34},{67,33},{96,64... | collective-permute-start | bytes 196616 | tf_op jit(solution)/shard_map/ppermute | solution.py:335
  171.4 13.4 %collective-permute-start.33 = (bf16[64,3584]{1,0:T(8,128)(2,1)}, bf16[64,3584]{1,0:T(8,128)(2,1)}, u32[]{:S(2)}, u32[]{:S(2)}) collective-permute-start(bf16[64,3584]{1,0:T(8,128)(2,1)} %collective-permute-done.26.refs_2_), channel_id=1, source_target_pairs={{0,24},{4,28},{8,0},{12,4},{16,8},{20,12},{24,16},{28,20},{1,25},{... | collective-permute-start | bytes 1376264 | tf_op jit(solution)/shard_map/ppermute | solution.py:318
  172.9 13.1 %collective-permute-start.32 = (bf16[64,3584]{1,0:T(8,128)(2,1)}, bf16[64,3584]{1,0:T(8,128)(2,1)S(1)}, u32[]{:S(2)}, u32[]{:S(2)}) collective-permute-start(bf16[64,3584]{1,0:T(8,128)(2,1)} %collective-permute-done.26.refs_2_), channel_id=1, source_target_pairs={{0,8},{4,12},{8,16},{12,20},{16,24},{20,28},{24,0},{28,4},{1,9},{5... | collective-permute-start | bytes 1376264 | tf_op jit(solution)/shard_map/ppermute | solution.py:318
  183.5 14.4 %collective-permute-start.37 = (bf16[64,3584]{1,0:T(8,128)(2,1)}, bf16[64,3584]{1,0:T(8,128)(2,1)}, u32[]{:S(2)}, u32[]{:S(2)}) collective-permute-start(bf16[64,3584]{1,0:T(8,128)(2,1)} %collective-permute-done.27.refs_4_), channel_id=1, source_target_pairs={{0,8},{4,12},{8,16},{12,20},{16,24},{20,28},{24,0},{28,4},{1,9},{5... | collective-permute-start | bytes 1376264 | tf_op jit(solution)/shard_map/ppermute | solution.py:318
  186.0 13.2 %collective-permute-start.38 = (bf16[64,3584]{1,0:T(8,128)(2,1)}, bf16[64,3584]{1,0:T(8,128)(2,1)}, u32[]{:S(2)}, u32[]{:S(2)}) collective-permute-start(bf16[64,3584]{1,0:T(8,128)(2,1)} %collective-permute-done.33.refs_8_), channel_id=1, source_target_pairs={{0,24},{4,28},{8,0},{12,4},{16,8},{20,12},{24,16},{28,20},{1,25},{... | collective-permute-start | bytes 1376264 | tf_op jit(solution)/shard_map/ppermute | solution.py:318
  200.1 13.4 %all-to-all-start.2 = ((bf16[8,128,256]{2,1,0:T(8,128)(2,1)}), bf16[8,128,256]{2,1,0:T(8,128)(2,1)}, u32[]{:S(2)}, u32[]{:S(2)}) async-start(bf16[8,128,256]{2,1,0:T(8,128)(2,1)} %broadcast_in_dim.12), calls=%async_computation.2 | async-start | bytes 1048576 | tf_op jit(solution)/shard_map/all_to_all | solution.py:370
  213.5 22.3 %collective-permute-start.40 = (f32[256,128]{1,0:T(8,128)S(1)}, f32[256,128]{1,0:T(8,128)S(1)}, u32[]{:S(2)}, u32[]{:S(2)}) collective-permute-start(f32[256,128]{1,0:T(8,128)S(1)} %fusion), channel_id=1, source_target_pairs={{0,2},{1,3},{2,0},{3,1},{4,6},{5,7},{6,4},{7,5},{8,10},{9,11},{10,... | collective-permute-start | bytes 393224 | tf_op jit(solution)/shard_map/ppermute | solution.py:323
  (39 other events, 355.0 us)

commit v7 on v6

--- a/solution.py
+++ b/solution.py
@@ -109,9 +109,7 @@
     acc = gram_share(g, all_ref)
     for cols in chunks_of(slope_ref.shape[1]):
         g_pre = mm(gw, twice(down_of(all_ref, cols))) * slope_ref[:, cols].astype(F32)
-        hi, lo = split2(g_pre)
-        up = up_of(all_ref, cols)
-        acc += mm_nt(hi, up) + mm_nt(lo, up)
+        acc += mm_nt(g_pre.astype(BF), up_of(all_ref, cols))
     part_ref[...] = acc
 
 
@@ -402,7 +400,7 @@
     base_t = turn(place, base_1, dp)
     steps, base_t = tie(steps, base_t)
     up, down = reduce_2(two, left_1, right_1, steps)
-    up, down, other, basis_1 = tie(up, down, other, basis)
+    up, down, basis_1 = tie(up, down, basis)
     up, down, other = to_dp(up, 1, 0), to_dp(down, -1, 0), to_dp(other, 0, 1)
     proj = project(basis_1, w_in, w_out, dp)
     up, down, base_2 = tie(up, down, base_1)

time: 239 us -> 237 us (level)
  Pallas kernels: 66.2 us -> 63.7 us
    all_to_all x3, waiting for transfers between devices: 26.7 us -> 23.3 us  [swap(): return lax.all_to_all(x, 'dp', 0, 0, tiled=True)]
    pallas_call x9, Pallas kernels: 9.39 us -> 6.75 us  [call(): return pl.pallas_call(kernel, out_shape=outs, compiler_params=SMALL)(*args)]
  transfers between devices with their start and end apart: 44 -> 44, of which waited for: 26 -> 25; matrix products, arithmetic and copies ran while one was open for 4% -> 7% of each run, Pallas kernels for 24% -> 23%
where the time goes in v7:
time: 237 us; the launch traced here: 234 us
  waiting for transfers between devices  79.1 us (33%)
  starting transfers between devices  67.7 us (29%)
  Pallas kernels  63.7 us (27%)
  local copies, waits for them, and re-layouts  12.2 us (5%)
  other arithmetic  9.87 us (4%)
    ppermute x6, waiting for transfers between devices, hop(): got = lax.ppermute(pair_sum, ('section', 'tensor'), pairs)  24.5 us
    all_to_all x3, waiting for transfers between devices, swap(): return lax.all_to_all(x, 'dp', 0, 0, tiled=True)  23.3 us
    ppermute x21, starting transfers between devices, to_dp(): return lax.ppermute(x, 'dp', pairs)  23.2 us
    ppermute x6, starting transfers between devices, hop(): got = lax.ppermute(pair_sum, ('section', 'tensor'), pairs)  23.1 us
    pallas_call x1, Pallas kernels, finish(): pl.pallas_call(finish_kernel, out_shape=[jax.ShapeDtypeStruct((width, hid...  21.4 us
    ppermute x21, waiting for transfers between devices, to_dp(): return lax.ppermute(x, 'dp', pairs)  20.5 us
    pallas_call x2, Pallas kernels, product(): pl.pallas_call(functools.partial(product_kernel, count, plan), out_shape=...  19.7 us
    all_to_all x3, starting transfers between devices, swap(): return lax.all_to_all(x, 'dp', 0, 0, tiled=True)  11.8 us
  transfers between devices with their start and end apart: 44, of which 25 were waited for; matrix products, arithmetic and copies ran while one was open for 7% of the time, Pallas kernels for 23%

profile of v7, /device:TPU:1, one launch (start us, length us, event | category | flops | bytes accessed | tf_op | source)
XLA Modules:
  0.0 233.7 jit_solution(8111973552283229646)
XLA Ops:
  1.4 9.8 %shard_map.84 = (bf16[32,3584]{1,0:T(8,128)(2,1)}, bf16[32,3584]{1,0:T(8,128)(2,1)}, bf16[64,3584]{1,0:T(8,128)(2,1)}, bf16[128,3584]{1,0:T(8,128)(2,1)}, bf16[6...) custom-call(s32[8]{0:T(128)} %stack.35.place_ref, bf16[4,256,1024]{2,1,0:T(8,128)(2,1)} %refs_3_.3, ...), custom_call_target="tpu_custom_call" | custom-call | tf_op jit(solution)/shard_map/pallas_call | solution.py:151
  11.2 2.1 collective-permute-start.2
  17.2 4.3 %shard_map.85.base_ref = bf16[1024,1024]{1,0:T(8,128)(2,1)} custom-call(s32[8]{0:T(128)} %stack.35.place_ref, bf16[4,256,1024]{2,1,0:T(8,128)(2,1)} %refs_3_.3, bf16[4,256,1024]{2,1,0:T(8,128)(2,1)} %refs_3_.3, bf16[4,256,1024]{2,1,0:T(8,128)(2,1)} %refs_3_.3, bf16[4,256,1024]{2,1,0:T(8,128)(2,1)} %refs_3_.3, bf16[4,256,1024]{2,1,0:T(8,128)(2,1)} %refs_3_.3, ...), custom_call_target="tpu_custom_call" | custom-call | tf_op jit(solution)/shard_map/pallas_call | solution.py:234
  28.4 11.5 %shard_map.87 = bf16[8,32,3712]{2,1,0:T(8,128)(2,1)} custom-call(f32[1024,128]{1,0:T(8,128)} %basis_ref.2, bf16[1024,3584]{1,0:T(8,128)(2,1)} %bitcast.24, bf16[3584,1024]{1,0:T(8,128)(2,1)} %bitcast.26), custom_call_target="tpu_custom_call" | custom-call | tf_op jit(solution)/shard_map/pallas_call | solution.py:193
  39.9 4.0 %all-to-all-start = ((bf16[8,32,3712]{2,1,0:T(8,128)(2,1)}), bf16[8,32,3712]{2,1,0:T(8,128)(2,1)S(1)}, u32[]{:S(2)}, u32[]{:S(2)}) async-start(bf16[8,32,3712]{2,1,0:T(8,128)(2,1)} %shard_map.87), calls=%async_computation | async-start | bytes 3801088 | tf_op jit(solution)/shard_map/all_to_all | solution.py:368
  43.9 2.0 fusion.2
  46.3 2.2 fusion.3
  48.5 9.9 %shard_map.86 = (bf16[128,3584]{1,0:T(8,128)(2,1)}, bf16[128,3584]{1,0:T(8,128)(2,1)}, bf16[128,3584]{1,0:T(8,128)(2,1)}, bf16[128,3584]{1,0:T(8,128)(2,1)}) custom-call(s32[8]{0:T(128)} %stack.35.place_ref, bf16[4,256,1024]{2,1,0:T(8,128)(2,1)} %refs_3_.3, bf16[4,256,1024]{2,1,0:T(8,128)(2,1)} %refs_3_.3, bf16[4,256,1024]{2,1,0:T(8,128)(2,1)} %refs_3_.3, ...), custom_call_target="tpu_custom_call" | custom-call | tf_op jit(solution)/shard_map/pallas_call | solution.py:151
  58.5 2.8 %add_convert_fusion.3 = bf16[128,3584]{1,0:T(8,128)(2,1)} fusion(bf16[128,3584]{1,0:T(8,128)(2,1)} %get-tuple-element.89, bf16[64,3584]{1,0:T(8,128)(2,1)} %get-tuple-element.134, bf16[128,3584]{1,0:T(8,128)(2,1)S(1)} %collective-permute-done.3, pred[128]{0:T(512)(128)(4,1)S(1)} %copy-done.17), kind=kLoop, calls=%fused_computation.3 | loop fusion | flops 3211264 | bytes 3211392 | tf_op jit(solution)/shard_map/convert_element_type | solution.py:347
  70.3 3.6 %all-to-all-start.1 = ((bf16[8,32,3712]{2,1,0:T(8,128)(2,1)}), bf16[8,32,3712]{2,1,0:T(8,128)(2,1)S(1)}, u32[]{:S(2)}, u32[]{:S(2)}) async-start(bf16[8,32,3712]{2,1,0:T(8,128)(2,1)} %copy-done.4), calls=%async_computation.1 | async-start | bytes 3801088 | tf_op jit(solution)/shard_map/all_to_all | solution.py:368
  73.9 14.7 %collective-permute-done.6 = bf16[128,3584]{1,0:T(8,128)(2,1)S(1)} collective-permute-done((bf16[128,3584]{1,0:T(8,128)(2,1)}, bf16[128,3584]{1,0:T(8,128)(2,1)S(1)}, u32[]{:S(2)}, u32[]{:S(2)}) %collective-permute-start.6) | collective-permute-done | bytes 917536 | tf_op jit(solution)/shard_map/ppermute | solution.py:316
  89.6 2.5 %add_convert_fusion.base_ref.refs_0_ = bf16[128,3584]{1,0:T(8,128)(2,1)S(1)} fusion(bf16[128,3584]{1,0:T(8,128)(2,1)} %collective-permute-done.8, bf16[128,3584]{1,0:T(8,128)(2,1)} %collective-permute-done.7, bf16[128,3584]{1,0:T(8,128)(2,1)} %copy-done.11, bf16[128,3584]{1,0:T(8,128)(2,1)} %get-tuple-element.88), kind=kLoop, calls=%fused_computation | loop fusion | flops 3670016 | bytes 4587520 | tf_op jit(solution)/shard_map/convert_element_type | solution.py:414
  92.1 15.9 %all-to-all-done.1.all_ref = bf16[8,32,3712]{2,1,0:T(8,128)(2,1)S(1)} async-done(((bf16[8,32,3712]{2,1,0:T(8,128)(2,1)}), bf16[8,32,3712]{2,1,0:T(8,128)(2,1)S(1)}, u32[]{:S(2)}, u32[]{:S(2)}) %all-to-all-start.1) | async-done | bytes 1900576 | tf_op jit(solution)/shard_map/all_to_all | solution.py:368
  108.5 3.6 %collective-permute-start.9 = (f32[128,128]{1,0:T(8,128)S(1)}, f32[128,128]{1,0:T(8,128)S(1)}, u32[]{:S(2)}, u32[]{:S(2)}) collective-permute-start(f32[128,128]{1,0:T(8,128)S(1)} %shard_map.89), channel_id=1, source_target_pairs={{0,1},{1,0},{2,3},{3,2},{4,5},{5,4},{6,7},{7,6},{8,9},{9,8},{10,11... | collective-permute-start | bytes 196616 | tf_op jit(solution)/shard_map/ppermute | solution.py:321
  112.1 2.2 collective-permute-start.16
  114.3 6.2 %collective-permute-start.10 = (f32[128,128]{1,0:T(8,128)S(1)}, f32[128,128]{1,0:T(8,128)S(1)}, u32[]{:S(2)}, u32[]{:S(2)}) collective-permute-start(f32[128,128]{1,0:T(8,128)S(1)} %add.190), channel_id=1, source_target_pairs={{0,32},{1,35},{2,34},{3,33},{32,64},{33,67},{34,66},{35,65},{64,96... | collective-permute-start | bytes 196616 | tf_op jit(solution)/shard_map/ppermute | solution.py:333
  127.1 6.7 %collective-permute-start.13 = (f32[128,128]{1,0:T(8,128)S(1)}, f32[128,128]{1,0:T(8,128)S(1)}, u32[]{:S(2)}, u32[]{:S(2)}) collective-permute-start(f32[128,128]{1,0:T(8,128)S(1)} %add.191), channel_id=1, source_target_pairs={{0,32},{1,35},{2,34},{3,33},{32,64},{33,67},{34,66},{35,65},{64,96... | collective-permute-start | bytes 196616 | tf_op jit(solution)/shard_map/ppermute | solution.py:333
  143.9 6.2 %collective-permute-start.19 = (f32[128,128]{1,0:T(8,128)S(1)}, f32[128,128]{1,0:T(8,128)S(1)}, u32[]{:S(2)}, u32[]{:S(2)}) collective-permute-start(f32[128,128]{1,0:T(8,128)S(1)} %add.192), channel_id=1, source_target_pairs={{0,32},{1,35},{2,34},{3,33},{32,64},{33,67},{34,66},{35,65},{64,96... | collective-permute-start | bytes 196616 | tf_op jit(solution)/shard_map/ppermute | solution.py:333
  160.1 9.2 %collective-permute-done.24.r0 = f32[128,128]{1,0:T(8,128)S(1)} collective-permute-done((f32[128,128]{1,0:T(8,128)S(1)}, f32[128,128]{1,0:T(8,128)S(1)}, u32[]{:S(2)}, u32[]{:S(2)}) %collective-permute-start.24) | collective-permute-done | bytes 65568 | tf_op jit(solution)/shard_map/ppermute | solution.py:333
  175.9 6.1 %collective-permute-done.30.r0 = f32[128,128]{1,0:T(8,128)S(1)} collective-permute-done((f32[128,128]{1,0:T(8,128)S(1)}, f32[128,128]{1,0:T(8,128)S(1)}, u32[]{:S(2)}, u32[]{:S(2)}) %collective-permute-start.30) | collective-permute-done | bytes 65568 | tf_op jit(solution)/shard_map/ppermute | solution.py:333
  190.0 6.1 %collective-permute-done.35.r0 = f32[128,128]{1,0:T(8,128)S(1)} collective-permute-done((f32[128,128]{1,0:T(8,128)S(1)}, f32[128,128]{1,0:T(8,128)S(1)}, u32[]{:S(2)}, u32[]{:S(2)}) %collective-permute-start.35) | collective-permute-done | bytes 65568 | tf_op jit(solution)/shard_map/ppermute | solution.py:333
  198.3 4.1 %all-to-all-start.2 = ((bf16[8,128,256]{2,1,0:T(8,128)(2,1)}), bf16[8,128,256]{2,1,0:T(8,128)(2,1)}, u32[]{:S(2)}, u32[]{:S(2)}) async-start(bf16[8,128,256]{2,1,0:T(8,128)(2,1)} %broadcast_in_dim.12), calls=%async_computation.2 | async-start | bytes 1048576 | tf_op jit(solution)/shard_map/all_to_all | solution.py:368
  205.1 6.5 %all-to-all-done.2.ex_ref = bf16[8,128,256]{2,1,0:T(8,128)(2,1)} async-done(((bf16[8,128,256]{2,1,0:T(8,128)(2,1)}), bf16[8,128,256]{2,1,0:T(8,128)(2,1)}, u32[]{:S(2)}, u32[]{:S(2)}) %all-to-all-start.2) | async-done | bytes 524320 | tf_op jit(solution)/shard_map/all_to_all | solution.py:368
  211.6 21.4 %shard_map.97 = (bf16[1024,3584]{1,0:T(8,128)(2,1)}, f32[3584,128]{1,0:T(8,128)}) custom-call(s32[8]{0:T(128)} %stack.35.place_ref, bf16[8,128,256]{2,1,0:T(8,128)(2,1)} %all-to-all-done.2.ex_ref, bf16[8,32,3712]{2,1,0:T(8,128)(2,1)} %copy-done, bf16[1024,1024]{1,0:T(8,128)(2,1)} %shard_map.85.base_ref, f32[1024,128]{1,0:T(8,128)} %basis_ref.2, ...), custom_call_target="tpu_custom_call" | custom-call | tf_op jit(solution)/shard_map/pallas_call | solution.py:286
  (144 shorter events, 68.7 us)
Async XLA Ops:
  11.2 12.2 %collective-permute-start.2 = (bf16[64,3584]{1,0:T(8,128)(2,1)}, bf16[64,3584]{1,0:T(8,128)(2,1)S(1)}, u32[]{:S(2)}, u32[]{:S(2)}) collective-permute-start(bf16[64,3584]{1,0:T(8,128)(2,1)} %get-tuple-element.79), channel_id=1, source_target_pairs={{0,4},{4,0},{8,12},{12,8},{16,20},{20,16},{24,28},{28,24},{1,5},{5... | collective-permute-start | bytes 1376264 | tf_op jit(solution)/shard_map/ppermute | solution.py:316
  16.0 27.9 %collective-permute-start.5 = (bf16[128,3584]{1,0:T(8,128)(2,1)}, bf16[128,3584]{1,0:T(8,128)(2,1)}, u32[]{:S(2)}, u32[]{:S(2)}) collective-permute-start(bf16[128,3584]{1,0:T(8,128)(2,1)} %get-tuple-element.91), channel_id=1, source_target_pairs={{0,4},{4,0},{8,12},{12,8},{16,20},{20,16},{24,28},{28,24},{1,5},{5... | collective-permute-start | bytes 2752520 | tf_op jit(solution)/shard_map/ppermute | solution.py:316
  25.6 20.5 %collective-permute-start.3 = (bf16[128,3584]{1,0:T(8,128)(2,1)}, bf16[128,3584]{1,0:T(8,128)(2,1)S(1)}, u32[]{:S(2)}, u32[]{:S(2)}) collective-permute-start(bf16[128,3584]{1,0:T(8,128)(2,1)} %pad_maximum_fusion), channel_id=1, source_target_pairs={{0,8},{4,12},{8,16},{12,20},{16,24},{20,28},{24,0},{28,4},{1,9},{5... | collective-permute-start | bytes 2752520 | tf_op jit(solution)/shard_map/ppermute | solution.py:316
  27.1 19.2 %collective-permute-start.4 = (bf16[128,3584]{1,0:T(8,128)(2,1)}, bf16[128,3584]{1,0:T(8,128)(2,1)}, u32[]{:S(2)}, u32[]{:S(2)}) collective-permute-start(bf16[128,3584]{1,0:T(8,128)(2,1)} %pad_maximum_fusion.1), channel_id=1, source_target_pairs={{0,24},{4,28},{8,0},{12,4},{16,8},{20,12},{24,16},{28,20},{1,25},{... | collective-permute-start | bytes 2752520 | tf_op jit(solution)/shard_map/ppermute | solution.py:316
  39.9 28.9 %all-to-all-start = ((bf16[8,32,3712]{2,1,0:T(8,128)(2,1)}), bf16[8,32,3712]{2,1,0:T(8,128)(2,1)S(1)}, u32[]{:S(2)}, u32[]{:S(2)}) async-start(bf16[8,32,3712]{2,1,0:T(8,128)(2,1)} %shard_map.87), calls=%async_computation | async-start | bytes 3801088 | tf_op jit(solution)/shard_map/all_to_all | solution.py:368
  61.3 27.4 %collective-permute-start.6 = (bf16[128,3584]{1,0:T(8,128)(2,1)}, bf16[128,3584]{1,0:T(8,128)(2,1)S(1)}, u32[]{:S(2)}, u32[]{:S(2)}) collective-permute-start(bf16[128,3584]{1,0:T(8,128)(2,1)} %add_convert_fusion.3), channel_id=1, source_target_pairs={{0,8},{4,12},{8,16},{12,20},{16,24},{20,28},{24,0},{28,4},{1,9},{5... | collective-permute-start | bytes 2752520 | tf_op jit(solution)/shard_map/ppermute | solution.py:316
  63.7 24.9 %collective-permute-start.7 = (bf16[128,3584]{1,0:T(8,128)(2,1)}, bf16[128,3584]{1,0:T(8,128)(2,1)}, u32[]{:S(2)}, u32[]{:S(2)}) collective-permute-start(bf16[128,3584]{1,0:T(8,128)(2,1)} %add_convert_fusion.2), channel_id=1, source_target_pairs={{0,24},{4,28},{8,0},{12,4},{16,8},{20,12},{24,16},{28,20},{1,25},{... | collective-permute-start | bytes 2752520 | tf_op jit(solution)/shard_map/ppermute | solution.py:316
  66.3 22.4 %collective-permute-start.8 = (bf16[128,3584]{1,0:T(8,128)(2,1)}, bf16[128,3584]{1,0:T(8,128)(2,1)}, u32[]{:S(2)}, u32[]{:S(2)}) collective-permute-start(bf16[128,3584]{1,0:T(8,128)(2,1)} %add_convert_fusion.1), channel_id=1, source_target_pairs={{0,4},{4,0},{8,12},{12,8},{16,20},{20,16},{24,28},{28,24},{1,5},{5... | collective-permute-start | bytes 2752520 | tf_op jit(solution)/shard_map/ppermute | solution.py:316
  70.3 37.6 %all-to-all-start.1 = ((bf16[8,32,3712]{2,1,0:T(8,128)(2,1)}), bf16[8,32,3712]{2,1,0:T(8,128)(2,1)S(1)}, u32[]{:S(2)}, u32[]{:S(2)}) async-start(bf16[8,32,3712]{2,1,0:T(8,128)(2,1)} %copy-done.4), calls=%async_computation.1 | async-start | bytes 3801088 | tf_op jit(solution)/shard_map/all_to_all | solution.py:368
  112.1 23.1 %collective-permute-start.16 = (bf16[128,3584]{1,0:T(8,128)(2,1)S(1)}, bf16[128,3584]{1,0:T(8,128)(2,1)S(1)}, u32[]{:S(2)}, u32[]{:S(2)}) collective-permute-start(bf16[128,3584]{1,0:T(8,128)(2,1)S(1)} %add_convert_fusion.base_ref.refs_0_), channel_id=1, source_target_pairs={{0,24},{4,28},{8,0},{12,4},{16,8},{20,12},{24,16},{28,20},{1,25},{... | collective-permute-start | bytes 2752520 | tf_op jit(solution)/shard_map/ppermute | solution.py:316
  114.3 22.8 %collective-permute-start.15 = (bf16[128,3584]{1,0:T(8,128)(2,1)S(1)}, bf16[128,3584]{1,0:T(8,128)(2,1)S(1)}, u32[]{:S(2)}, u32[]{:S(2)}) collective-permute-start(bf16[128,3584]{1,0:T(8,128)(2,1)S(1)} %add_convert_fusion.base_ref.refs_0_), channel_id=1, source_target_pairs={{0,8},{4,12},{8,16},{12,20},{16,24},{20,28},{24,0},{28,4},{1,9},{5... | collective-permute-start | bytes 2752520 | tf_op jit(solution)/shard_map/ppermute | solution.py:316
  121.9 15.2 %collective-permute-start.17 = (bf16[64,3584]{1,0:T(8,128)(2,1)S(1)}, bf16[64,3584]{1,0:T(8,128)(2,1)}, u32[]{:S(2)}, u32[]{:S(2)}) collective-permute-start(bf16[64,3584]{1,0:T(8,128)(2,1)S(1)} %get-tuple-element.99), channel_id=1, source_target_pairs={{0,4},{4,0},{8,12},{12,8},{16,20},{20,16},{24,28},{28,24},{1,5},{5... | collective-permute-start | bytes 1376264 | tf_op jit(solution)/shard_map/ppermute | solution.py:316
  138.8 15.8 %collective-permute-start.22 = (bf16[64,3584]{1,0:T(8,128)(2,1)}, bf16[64,3584]{1,0:T(8,128)(2,1)}, u32[]{:S(2)}, u32[]{:S(2)}) collective-permute-start(bf16[64,3584]{1,0:T(8,128)(2,1)} %slice.53), channel_id=1, source_target_pairs={{0,24},{4,28},{8,0},{12,4},{16,8},{20,12},{24,16},{28,20},{1,25},{... | collective-permute-start | bytes 1376264 | tf_op jit(solution)/shard_map/ppermute | solution.py:316
  140.7 13.8 %collective-permute-start.21 = (bf16[64,3584]{1,0:T(8,128)(2,1)}, bf16[64,3584]{1,0:T(8,128)(2,1)}, u32[]{:S(2)}, u32[]{:S(2)}) collective-permute-start(bf16[64,3584]{1,0:T(8,128)(2,1)} %slice.52), channel_id=1, source_target_pairs={{0,8},{4,12},{8,16},{12,20},{16,24},{20,28},{24,0},{28,4},{1,9},{5... | collective-permute-start | bytes 1376264 | tf_op jit(solution)/shard_map/ppermute | solution.py:316
  151.4 17.9 %collective-permute-start.26 = (bf16[64,3584]{1,0:T(8,128)(2,1)}, bf16[64,3584]{1,0:T(8,128)(2,1)}, u32[]{:S(2)}, u32[]{:S(2)}) collective-permute-start(bf16[64,3584]{1,0:T(8,128)(2,1)} %get-tuple-element.108), channel_id=1, source_target_pairs={{0,4},{4,0},{8,12},{12,8},{16,20},{20,16},{24,28},{28,24},{1,5},{5... | collective-permute-start | bytes 1376264 | tf_op jit(solution)/shard_map/ppermute | solution.py:316
  153.1 16.2 %collective-permute-start.28 = (bf16[64,3584]{1,0:T(8,128)(2,1)}, bf16[64,3584]{1,0:T(8,128)(2,1)}, u32[]{:S(2)}, u32[]{:S(2)}) collective-permute-start(bf16[64,3584]{1,0:T(8,128)(2,1)} %collective-permute-done.17.refs_1_), channel_id=1, source_target_pairs={{0,24},{4,28},{8,0},{12,4},{16,8},{20,12},{24,16},{28,20},{1,25},{... | collective-permute-start | bytes 1376264 | tf_op jit(solution)/shard_map/ppermute | solution.py:316
  154.3 15.0 %collective-permute-start.27 = (bf16[64,3584]{1,0:T(8,128)(2,1)}, bf16[64,3584]{1,0:T(8,128)(2,1)}, u32[]{:S(2)}, u32[]{:S(2)}) collective-permute-start(bf16[64,3584]{1,0:T(8,128)(2,1)} %collective-permute-done.17.refs_1_), channel_id=1, source_target_pairs={{0,8},{4,12},{8,16},{12,20},{16,24},{20,28},{24,0},{28,4},{1,9},{5... | collective-permute-start | bytes 1376264 | tf_op jit(solution)/shard_map/ppermute | solution.py:316
  158.8 10.5 %collective-permute-start.24 = (f32[128,128]{1,0:T(8,128)S(1)}, f32[128,128]{1,0:T(8,128)S(1)}, u32[]{:S(2)}, u32[]{:S(2)}) collective-permute-start(f32[128,128]{1,0:T(8,128)S(1)} %add.193), channel_id=1, source_target_pairs={{32,0},{33,3},{34,2},{35,1},{64,32},{65,35},{66,34},{67,33},{96,64... | collective-permute-start | bytes 196616 | tf_op jit(solution)/shard_map/ppermute | solution.py:333
  170.6 12.7 %collective-permute-start.33 = (bf16[64,3584]{1,0:T(8,128)(2,1)}, bf16[64,3584]{1,0:T(8,128)(2,1)}, u32[]{:S(2)}, u32[]{:S(2)}) collective-permute-start(bf16[64,3584]{1,0:T(8,128)(2,1)} %collective-permute-done.26.refs_2_), channel_id=1, source_target_pairs={{0,24},{4,28},{8,0},{12,4},{16,8},{20,12},{24,16},{28,20},{1,25},{... | collective-permute-start | bytes 1376264 | tf_op jit(solution)/shard_map/ppermute | solution.py:316
  171.8 13.1 %collective-permute-start.32 = (bf16[64,3584]{1,0:T(8,128)(2,1)}, bf16[64,3584]{1,0:T(8,128)(2,1)S(1)}, u32[]{:S(2)}, u32[]{:S(2)}) collective-permute-start(bf16[64,3584]{1,0:T(8,128)(2,1)} %collective-permute-done.26.refs_2_), channel_id=1, source_target_pairs={{0,8},{4,12},{8,16},{12,20},{16,24},{20,28},{24,0},{28,4},{1,9},{5... | collective-permute-start | bytes 1376264 | tf_op jit(solution)/shard_map/ppermute | solution.py:316
  182.0 14.2 %collective-permute-start.37 = (bf16[64,3584]{1,0:T(8,128)(2,1)}, bf16[64,3584]{1,0:T(8,128)(2,1)}, u32[]{:S(2)}, u32[]{:S(2)}) collective-permute-start(bf16[64,3584]{1,0:T(8,128)(2,1)} %collective-permute-done.27.refs_4_), channel_id=1, source_target_pairs={{0,8},{4,12},{8,16},{12,20},{16,24},{20,28},{24,0},{28,4},{1,9},{5... | collective-permute-start | bytes 1376264 | tf_op jit(solution)/shard_map/ppermute | solution.py:316
  184.9 12.6 %collective-permute-start.38 = (bf16[64,3584]{1,0:T(8,128)(2,1)}, bf16[64,3584]{1,0:T(8,128)(2,1)}, u32[]{:S(2)}, u32[]{:S(2)}) collective-permute-start(bf16[64,3584]{1,0:T(8,128)(2,1)} %collective-permute-done.33.refs_8_), channel_id=1, source_target_pairs={{0,24},{4,28},{8,0},{12,4},{16,8},{20,12},{24,16},{28,20},{1,25},{... | collective-permute-start | bytes 1376264 | tf_op jit(solution)/shard_map/ppermute | solution.py:316
  198.3 13.4 %all-to-all-start.2 = ((bf16[8,128,256]{2,1,0:T(8,128)(2,1)}), bf16[8,128,256]{2,1,0:T(8,128)(2,1)}, u32[]{:S(2)}, u32[]{:S(2)}) async-start(bf16[8,128,256]{2,1,0:T(8,128)(2,1)} %broadcast_in_dim.12), calls=%async_computation.2 | async-start | bytes 1048576 | tf_op jit(solution)/shard_map/all_to_all | solution.py:368
  211.6 21.4 %collective-permute-start.40 = (f32[256,128]{1,0:T(8,128)S(1)}, f32[256,128]{1,0:T(8,128)S(1)}, u32[]{:S(2)}, u32[]{:S(2)}) collective-permute-start(f32[256,128]{1,0:T(8,128)S(1)} %fusion), channel_id=1, source_target_pairs={{0,2},{1,3},{2,0},{3,1},{4,6},{5,7},{6,4},{7,5},{8,10},{9,11},{10,... | collective-permute-start | bytes 393224 | tf_op jit(solution)/shard_map/ppermute | solution.py:321
  (39 other events, 368.5 us)

commit v8 on v7

--- a/solution.py
+++ b/solution.py
@@ -12,6 +12,8 @@
 HIGHEST = lax.Precision.HIGHEST
 NT = (((1,), (1,)), ((), ()))
 CHUNK = 512
+WIDE_CHUNK = 1792
+PROJ_CHUNK = 896
 X_SIZE = 4
 RELATIVE = ((0, 0), (0, 1), (-1, 0), (-1, 1), (1, 0), (1, 1), (2, 0), (2, 1))
 EARLY, LATE = (7, 6, 3, 5), (2, 4, 1, 0)
@@ -147,13 +149,13 @@
     own = micro * tokens // dp
     count = len(blocks)
     heights = [sum(end - begin for _, begin, end in parts) for parts in plan]
-    column = lambda rows: pl.BlockSpec((rows, CHUNK), lambda i, p: (0, i))
+    column = lambda rows: pl.BlockSpec((rows, WIDE_CHUNK), lambda i, p: (0, i))
     return pl.pallas_call(
         functools.partial(product_kernel, count, plan),
         out_shape=[jax.ShapeDtypeStruct((rows, hid), BF) for rows in heights],
         grid_spec=pltpu.PrefetchScalarGridSpec(
             num_scalar_prefetch=1,
-            grid=(hid // CHUNK,),
+            grid=(hid // WIDE_CHUNK,),
             in_specs=base_specs(base, dp, blocks) + [column(width)],
             out_specs=[column(rows) for rows in heights],
             scratch_shapes=[pltpu.VMEM((own * count, width), BF)],
@@ -178,12 +180,12 @@
         out_ref[:, :share, cols - rank :] = hi.reshape(count, share, rank)
         out_ref[:, share:, cols - rank :] = lo.reshape(count, share, rank)
 
-    here = pl.ds(pl.multiple_of(step * CHUNK, CHUNK), CHUNK)
+    here = pl.ds(pl.multiple_of(step * PROJ_CHUNK, PROJ_CHUNK), PROJ_CHUNK)
     up = mm(tall_ref[...], w_in_ref[...])
     down = mm(w_out_ref[...], wide_ref[...])
-    out_ref[:, :share, here] = (up[:rank] + up[rank:]).astype(BF).reshape(count, share, CHUNK)
+    out_ref[:, :share, here] = (up[:rank] + up[rank:]).astype(BF).reshape(count, share, PROJ_CHUNK)
     down = (down[:, :rank] + down[:, rank:]).T
-    out_ref[:, share:, here] = down.astype(BF).reshape(count, share, CHUNK)
+    out_ref[:, share:, here] = down.astype(BF).reshape(count, share, PROJ_CHUNK)
 
 
 def project(basis, w_in, w_out, dp):
@@ -193,11 +195,11 @@
     return pl.pallas_call(
         project_kernel,
         out_shape=jax.ShapeDtypeStruct(shape, BF),
-        grid=(hid // CHUNK,),
+        grid=(hid // PROJ_CHUNK,),
         in_specs=[
             pl.BlockSpec((width, rank), lambda i: (0, 0)),
-            pl.BlockSpec((width, CHUNK), lambda i: (0, i)),
-            pl.BlockSpec((CHUNK, width), lambda i: (i, 0)),
+            pl.BlockSpec((width, PROJ_CHUNK), lambda i: (0, i)),
+            pl.BlockSpec((PROJ_CHUNK, width), lambda i: (i, 0)),
         ],
         out_specs=pl.BlockSpec(shape, lambda i: (0, 0, 0)),
         scratch_shapes=[pltpu.VMEM((width, 2 * rank), BF), pltpu.VMEM((2 * rank, width), BF)],

time: 237 us -> 235 us (level)
  Pallas kernels: 63.7 us -> 59.6 us
    pallas_call x2, Pallas kernels: 19.7 us -> 17.1 us  [product(): pl.pallas_call(functools.partial(product_kernel, count, plan), out_shape=...]
  transfers between devices with their start and end apart: 44 -> 44, of which waited for: 25 -> 26; matrix products, arithmetic and copies ran while one was open for 7% -> 7% of each run, Pallas kernels for 23% -> 22%
where the time goes in v8:
time: 235 us; the launch traced here: 232 us
  waiting for transfers between devices  80.9 us (34%)
  starting transfers between devices  68.6 us (29%)
  Pallas kernels  59.6 us (25%)
  local copies, waits for them, and re-layouts  12.3 us (5%)
  other arithmetic  9.87 us (4%)
    ppermute x6, waiting for transfers between devices, hop(): got = lax.ppermute(pair_sum, ('section', 'tensor'), pairs)  24.5 us
    ppermute x21, starting transfers between devices, to_dp(): return lax.ppermute(x, 'dp', pairs)  24.4 us
    all_to_all x3, waiting for transfers between devices, swap(): return lax.all_to_all(x, 'dp', 0, 0, tiled=True)  23.6 us
    ppermute x6, starting transfers between devices, hop(): got = lax.ppermute(pair_sum, ('section', 'tensor'), pairs)  23.3 us
    ppermute x21, waiting for transfers between devices, to_dp(): return lax.ppermute(x, 'dp', pairs)  22.1 us
    pallas_call x1, Pallas kernels, finish(): pl.pallas_call(finish_kernel, out_shape=[jax.ShapeDtypeStruct((width, hid...  21.4 us
    pallas_call x2, Pallas kernels, product(): pl.pallas_call(functools.partial(product_kernel, count, plan), out_shape=...  17.1 us
    all_to_all x3, starting transfers between devices, swap(): return lax.all_to_all(x, 'dp', 0, 0, tiled=True)  12 us
  transfers between devices with their start and end apart: 44, of which 26 were waited for; matrix products, arithmetic and copies ran while one was open for 7% of the time, Pallas kernels for 22%

profile of v8, /device:TPU:1, one launch (start us, length us, event | category | flops | bytes accessed | tf_op | source)
XLA Modules:
  0.0 232.4 jit_solution(16946716283546152360)
XLA Ops:
  1.4 8.5 %shard_map.84 = (bf16[32,3584]{1,0:T(8,128)(2,1)}, bf16[32,3584]{1,0:T(8,128)(2,1)}, bf16[64,3584]{1,0:T(8,128)(2,1)}, bf16[128,3584]{1,0:T(8,128)(2,1)}, bf16[6...) custom-call(s32[8]{0:T(128)} %stack.35.place_ref, bf16[4,256,1024]{2,1,0:T(8,128)(2,1)} %refs_3_.3, ...), custom_call_target="tpu_custom_call" | custom-call | tf_op jit(solution)/shard_map/pallas_call | solution.py:153
  15.8 4.3 %shard_map.85.base_ref = bf16[1024,1024]{1,0:T(8,128)(2,1)} custom-call(s32[8]{0:T(128)} %stack.35.place_ref, bf16[4,256,1024]{2,1,0:T(8,128)(2,1)} %refs_3_.3, bf16[4,256,1024]{2,1,0:T(8,128)(2,1)} %refs_3_.3, bf16[4,256,1024]{2,1,0:T(8,128)(2,1)} %refs_3_.3, bf16[4,256,1024]{2,1,0:T(8,128)(2,1)} %refs_3_.3, bf16[4,256,1024]{2,1,0:T(8,128)(2,1)} %refs_3_.3, ...), custom_call_target="tpu_custom_call" | custom-call | tf_op jit(solution)/shard_map/pallas_call | solution.py:236
  27.0 10.1 %shard_map.87 = bf16[8,32,3712]{2,1,0:T(8,128)(2,1)} custom-call(f32[1024,128]{1,0:T(8,128)} %basis_ref.2, bf16[1024,3584]{1,0:T(8,128)(2,1)} %bitcast.24, bf16[3584,1024]{1,0:T(8,128)(2,1)} %bitcast.26), custom_call_target="tpu_custom_call" | custom-call | tf_op jit(solution)/shard_map/pallas_call | solution.py:195
  37.1 4.0 %all-to-all-start = ((bf16[8,32,3712]{2,1,0:T(8,128)(2,1)}), bf16[8,32,3712]{2,1,0:T(8,128)(2,1)S(1)}, u32[]{:S(2)}, u32[]{:S(2)}) async-start(bf16[8,32,3712]{2,1,0:T(8,128)(2,1)} %shard_map.87), calls=%async_computation | async-start | bytes 3801088 | tf_op jit(solution)/shard_map/all_to_all | solution.py:370
  44.9 2.3 fusion.3
  47.1 8.6 %shard_map.86 = (bf16[128,3584]{1,0:T(8,128)(2,1)}, bf16[128,3584]{1,0:T(8,128)(2,1)}, bf16[128,3584]{1,0:T(8,128)(2,1)}, bf16[128,3584]{1,0:T(8,128)(2,1)}) custom-call(s32[8]{0:T(128)} %stack.35.place_ref, bf16[4,256,1024]{2,1,0:T(8,128)(2,1)} %refs_3_.3, bf16[4,256,1024]{2,1,0:T(8,128)(2,1)} %refs_3_.3, bf16[4,256,1024]{2,1,0:T(8,128)(2,1)} %refs_3_.3, ...), custom_call_target="tpu_custom_call" | custom-call | tf_op jit(solution)/shard_map/pallas_call | solution.py:153
  55.8 2.8 %add_convert_fusion.3 = bf16[128,3584]{1,0:T(8,128)(2,1)} fusion(bf16[128,3584]{1,0:T(8,128)(2,1)} %get-tuple-element.89, bf16[64,3584]{1,0:T(8,128)(2,1)} %get-tuple-element.134, bf16[128,3584]{1,0:T(8,128)(2,1)S(1)} %collective-permute-done.3, pred[128]{0:T(512)(128)(4,1)S(1)} %copy-done.17), kind=kLoop, calls=%fused_computation.3 | loop fusion | flops 3211264 | bytes 3211392 | tf_op jit(solution)/shard_map/convert_element_type | solution.py:349
  68.0 3.8 %all-to-all-start.1 = ((bf16[8,32,3712]{2,1,0:T(8,128)(2,1)}), bf16[8,32,3712]{2,1,0:T(8,128)(2,1)S(1)}, u32[]{:S(2)}, u32[]{:S(2)}) async-start(bf16[8,32,3712]{2,1,0:T(8,128)(2,1)} %copy-done.4), calls=%async_computation.1 | async-start | bytes 3801088 | tf_op jit(solution)/shard_map/all_to_all | solution.py:370
  71.7 15.5 %collective-permute-done.6 = bf16[128,3584]{1,0:T(8,128)(2,1)S(1)} collective-permute-done((bf16[128,3584]{1,0:T(8,128)(2,1)}, bf16[128,3584]{1,0:T(8,128)(2,1)S(1)}, u32[]{:S(2)}, u32[]{:S(2)}) %collective-permute-start.6) | collective-permute-done | bytes 917536 | tf_op jit(solution)/shard_map/ppermute | solution.py:318
  88.2 2.5 %add_convert_fusion.base_ref.refs_0_ = bf16[128,3584]{1,0:T(8,128)(2,1)S(1)} fusion(bf16[128,3584]{1,0:T(8,128)(2,1)} %collective-permute-done.8, bf16[128,3584]{1,0:T(8,128)(2,1)} %collective-permute-done.7, bf16[128,3584]{1,0:T(8,128)(2,1)} %copy-done.11, bf16[128,3584]{1,0:T(8,128)(2,1)} %get-tuple-element.88), kind=kLoop, calls=%fused_computation | loop fusion | flops 3670016 | bytes 4587520 | tf_op jit(solution)/shard_map/convert_element_type | solution.py:416
  90.7 15.8 %all-to-all-done.1.all_ref = bf16[8,32,3712]{2,1,0:T(8,128)(2,1)S(1)} async-done(((bf16[8,32,3712]{2,1,0:T(8,128)(2,1)}), bf16[8,32,3712]{2,1,0:T(8,128)(2,1)S(1)}, u32[]{:S(2)}, u32[]{:S(2)}) %all-to-all-start.1) | async-done | bytes 1900576 | tf_op jit(solution)/shard_map/all_to_all | solution.py:370
  107.0 3.7 %collective-permute-start.9 = (f32[128,128]{1,0:T(8,128)S(1)}, f32[128,128]{1,0:T(8,128)S(1)}, u32[]{:S(2)}, u32[]{:S(2)}) collective-permute-start(f32[128,128]{1,0:T(8,128)S(1)} %shard_map.89), channel_id=1, source_target_pairs={{0,1},{1,0},{2,3},{3,2},{4,5},{5,4},{6,7},{7,6},{8,9},{9,8},{10,11... | collective-permute-start | bytes 196616 | tf_op jit(solution)/shard_map/ppermute | solution.py:323
  112.2 6.4 %collective-permute-start.10 = (f32[128,128]{1,0:T(8,128)S(1)}, f32[128,128]{1,0:T(8,128)S(1)}, u32[]{:S(2)}, u32[]{:S(2)}) collective-permute-start(f32[128,128]{1,0:T(8,128)S(1)} %add.190), channel_id=1, source_target_pairs={{0,32},{1,35},{2,34},{3,33},{32,64},{33,67},{34,66},{35,65},{64,96... | collective-permute-start | bytes 196616 | tf_op jit(solution)/shard_map/ppermute | solution.py:335
  119.9 2.3 collective-permute-start.17
  125.6 6.7 %collective-permute-start.13 = (f32[128,128]{1,0:T(8,128)S(1)}, f32[128,128]{1,0:T(8,128)S(1)}, u32[]{:S(2)}, u32[]{:S(2)}) collective-permute-start(f32[128,128]{1,0:T(8,128)S(1)} %add.191), channel_id=1, source_target_pairs={{0,32},{1,35},{2,34},{3,33},{32,64},{33,67},{34,66},{35,65},{64,96... | collective-permute-start | bytes 196616 | tf_op jit(solution)/shard_map/ppermute | solution.py:335
  136.7 2.5 %collective-permute-start.22 = (bf16[64,3584]{1,0:T(8,128)(2,1)}, bf16[64,3584]{1,0:T(8,128)(2,1)}, u32[]{:S(2)}, u32[]{:S(2)}) collective-permute-start(bf16[64,3584]{1,0:T(8,128)(2,1)} %slice.53), channel_id=1, source_target_pairs={{0,24},{4,28},{8,0},{12,4},{16,8},{20,12},{24,16},{28,20},{1,25},{... | collective-permute-start | bytes 1376264 | tf_op jit(solution)/shard_map/ppermute | solution.py:318
  141.8 6.4 %collective-permute-start.19 = (f32[128,128]{1,0:T(8,128)S(1)}, f32[128,128]{1,0:T(8,128)S(1)}, u32[]{:S(2)}, u32[]{:S(2)}) collective-permute-start(f32[128,128]{1,0:T(8,128)S(1)} %add.192), channel_id=1, source_target_pairs={{0,32},{1,35},{2,34},{3,33},{32,64},{33,67},{34,66},{35,65},{64,96... | collective-permute-start | bytes 196616 | tf_op jit(solution)/shard_map/ppermute | solution.py:335
  149.5 2.3 collective-permute-start.26
  158.8 9.2 %collective-permute-done.24.r0 = f32[128,128]{1,0:T(8,128)S(1)} collective-permute-done((f32[128,128]{1,0:T(8,128)S(1)}, f32[128,128]{1,0:T(8,128)S(1)}, u32[]{:S(2)}, u32[]{:S(2)}) %collective-permute-start.24) | collective-permute-done | bytes 65568 | tf_op jit(solution)/shard_map/ppermute | solution.py:335
  174.5 6.1 %collective-permute-done.30.r0 = f32[128,128]{1,0:T(8,128)S(1)} collective-permute-done((f32[128,128]{1,0:T(8,128)S(1)}, f32[128,128]{1,0:T(8,128)S(1)}, u32[]{:S(2)}, u32[]{:S(2)}) %collective-permute-start.30) | collective-permute-done | bytes 65568 | tf_op jit(solution)/shard_map/ppermute | solution.py:335
  188.7 6.1 %collective-permute-done.35.r0 = f32[128,128]{1,0:T(8,128)S(1)} collective-permute-done((f32[128,128]{1,0:T(8,128)S(1)}, f32[128,128]{1,0:T(8,128)S(1)}, u32[]{:S(2)}, u32[]{:S(2)}) %collective-permute-start.35) | collective-permute-done | bytes 65568 | tf_op jit(solution)/shard_map/ppermute | solution.py:335
  196.9 4.1 %all-to-all-start.2 = ((bf16[8,128,256]{2,1,0:T(8,128)(2,1)}), bf16[8,128,256]{2,1,0:T(8,128)(2,1)}, u32[]{:S(2)}, u32[]{:S(2)}) async-start(bf16[8,128,256]{2,1,0:T(8,128)(2,1)} %broadcast_in_dim.12), calls=%async_computation.2 | async-start | bytes 1048576 | tf_op jit(solution)/shard_map/all_to_all | solution.py:370
  203.7 6.6 %all-to-all-done.2.ex_ref = bf16[8,128,256]{2,1,0:T(8,128)(2,1)} async-done(((bf16[8,128,256]{2,1,0:T(8,128)(2,1)}), bf16[8,128,256]{2,1,0:T(8,128)(2,1)}, u32[]{:S(2)}, u32[]{:S(2)}) %all-to-all-start.2) | async-done | bytes 524320 | tf_op jit(solution)/shard_map/all_to_all | solution.py:370
  210.3 21.4 %shard_map.97 = (bf16[1024,3584]{1,0:T(8,128)(2,1)}, f32[3584,128]{1,0:T(8,128)}) custom-call(s32[8]{0:T(128)} %stack.35.place_ref, bf16[8,128,256]{2,1,0:T(8,128)(2,1)} %all-to-all-done.2.ex_ref, bf16[8,32,3712]{2,1,0:T(8,128)(2,1)} %copy-done, bf16[1024,1024]{1,0:T(8,128)(2,1)} %shard_map.85.base_ref, f32[1024,128]{1,0:T(8,128)} %basis_ref.2, ...), custom_call_target="tpu_custom_call" | custom-call | tf_op jit(solution)/shard_map/pallas_call | solution.py:288
  (144 shorter events, 69.5 us)
Async XLA Ops:
  9.8 12.1 %collective-permute-start.2 = (bf16[64,3584]{1,0:T(8,128)(2,1)}, bf16[64,3584]{1,0:T(8,128)(2,1)S(1)}, u32[]{:S(2)}, u32[]{:S(2)}) collective-permute-start(bf16[64,3584]{1,0:T(8,128)(2,1)} %get-tuple-element.79), channel_id=1, source_target_pairs={{0,4},{4,0},{8,12},{12,8},{16,20},{20,16},{24,28},{28,24},{1,5},{5... | collective-permute-start | bytes 1376264 | tf_op jit(solution)/shard_map/ppermute | solution.py:318
  14.6 27.1 %collective-permute-start.5 = (bf16[128,3584]{1,0:T(8,128)(2,1)}, bf16[128,3584]{1,0:T(8,128)(2,1)}, u32[]{:S(2)}, u32[]{:S(2)}) collective-permute-start(bf16[128,3584]{1,0:T(8,128)(2,1)} %get-tuple-element.91), channel_id=1, source_target_pairs={{0,4},{4,0},{8,12},{12,8},{16,20},{20,16},{24,28},{28,24},{1,5},{5... | collective-permute-start | bytes 2752520 | tf_op jit(solution)/shard_map/ppermute | solution.py:318
  24.2 20.6 %collective-permute-start.3 = (bf16[128,3584]{1,0:T(8,128)(2,1)}, bf16[128,3584]{1,0:T(8,128)(2,1)S(1)}, u32[]{:S(2)}, u32[]{:S(2)}) collective-permute-start(bf16[128,3584]{1,0:T(8,128)(2,1)} %pad_maximum_fusion), channel_id=1, source_target_pairs={{0,8},{4,12},{8,16},{12,20},{16,24},{20,28},{24,0},{28,4},{1,9},{5... | collective-permute-start | bytes 2752520 | tf_op jit(solution)/shard_map/ppermute | solution.py:318
  25.7 19.2 %collective-permute-start.4 = (bf16[128,3584]{1,0:T(8,128)(2,1)}, bf16[128,3584]{1,0:T(8,128)(2,1)}, u32[]{:S(2)}, u32[]{:S(2)}) collective-permute-start(bf16[128,3584]{1,0:T(8,128)(2,1)} %pad_maximum_fusion.1), channel_id=1, source_target_pairs={{0,24},{4,28},{8,0},{12,4},{16,8},{20,12},{24,16},{28,20},{1,25},{... | collective-permute-start | bytes 2752520 | tf_op jit(solution)/shard_map/ppermute | solution.py:318
  37.1 29.3 %all-to-all-start = ((bf16[8,32,3712]{2,1,0:T(8,128)(2,1)}), bf16[8,32,3712]{2,1,0:T(8,128)(2,1)S(1)}, u32[]{:S(2)}, u32[]{:S(2)}) async-start(bf16[8,32,3712]{2,1,0:T(8,128)(2,1)} %shard_map.87), calls=%async_computation | async-start | bytes 3801088 | tf_op jit(solution)/shard_map/all_to_all | solution.py:370
  58.6 28.7 %collective-permute-start.6 = (bf16[128,3584]{1,0:T(8,128)(2,1)}, bf16[128,3584]{1,0:T(8,128)(2,1)S(1)}, u32[]{:S(2)}, u32[]{:S(2)}) collective-permute-start(bf16[128,3584]{1,0:T(8,128)(2,1)} %add_convert_fusion.3), channel_id=1, source_target_pairs={{0,8},{4,12},{8,16},{12,20},{16,24},{20,28},{24,0},{28,4},{1,9},{5... | collective-permute-start | bytes 2752520 | tf_op jit(solution)/shard_map/ppermute | solution.py:318
  60.9 26.4 %collective-permute-start.7 = (bf16[128,3584]{1,0:T(8,128)(2,1)}, bf16[128,3584]{1,0:T(8,128)(2,1)}, u32[]{:S(2)}, u32[]{:S(2)}) collective-permute-start(bf16[128,3584]{1,0:T(8,128)(2,1)} %add_convert_fusion.2), channel_id=1, source_target_pairs={{0,24},{4,28},{8,0},{12,4},{16,8},{20,12},{24,16},{28,20},{1,25},{... | collective-permute-start | bytes 2752520 | tf_op jit(solution)/shard_map/ppermute | solution.py:318
  63.5 23.7 %collective-permute-start.8 = (bf16[128,3584]{1,0:T(8,128)(2,1)}, bf16[128,3584]{1,0:T(8,128)(2,1)}, u32[]{:S(2)}, u32[]{:S(2)}) collective-permute-start(bf16[128,3584]{1,0:T(8,128)(2,1)} %add_convert_fusion.1), channel_id=1, source_target_pairs={{0,4},{4,0},{8,12},{12,8},{16,20},{20,16},{24,28},{28,24},{1,5},{5... | collective-permute-start | bytes 2752520 | tf_op jit(solution)/shard_map/ppermute | solution.py:318
  68.0 38.5 %all-to-all-start.1 = ((bf16[8,32,3712]{2,1,0:T(8,128)(2,1)}), bf16[8,32,3712]{2,1,0:T(8,128)(2,1)S(1)}, u32[]{:S(2)}, u32[]{:S(2)}) async-start(bf16[8,32,3712]{2,1,0:T(8,128)(2,1)} %copy-done.4), calls=%async_computation.1 | async-start | bytes 3801088 | tf_op jit(solution)/shard_map/all_to_all | solution.py:370
  110.7 22.9 %collective-permute-start.16 = (bf16[128,3584]{1,0:T(8,128)(2,1)S(1)}, bf16[128,3584]{1,0:T(8,128)(2,1)S(1)}, u32[]{:S(2)}, u32[]{:S(2)}) collective-permute-start(bf16[128,3584]{1,0:T(8,128)(2,1)S(1)} %add_convert_fusion.base_ref.refs_0_), channel_id=1, source_target_pairs={{0,24},{4,28},{8,0},{12,4},{16,8},{20,12},{24,16},{28,20},{1,25},{... | collective-permute-start | bytes 2752520 | tf_op jit(solution)/shard_map/ppermute | solution.py:318
  112.2 22.8 %collective-permute-start.15 = (bf16[128,3584]{1,0:T(8,128)(2,1)S(1)}, bf16[128,3584]{1,0:T(8,128)(2,1)S(1)}, u32[]{:S(2)}, u32[]{:S(2)}) collective-permute-start(bf16[128,3584]{1,0:T(8,128)(2,1)S(1)} %add_convert_fusion.base_ref.refs_0_), channel_id=1, source_target_pairs={{0,8},{4,12},{8,16},{12,20},{16,24},{20,28},{24,0},{28,4},{1,9},{5... | collective-permute-start | bytes 2752520 | tf_op jit(solution)/shard_map/ppermute | solution.py:318
  119.9 15.1 %collective-permute-start.17 = (bf16[64,3584]{1,0:T(8,128)(2,1)S(1)}, bf16[64,3584]{1,0:T(8,128)(2,1)}, u32[]{:S(2)}, u32[]{:S(2)}) collective-permute-start(bf16[64,3584]{1,0:T(8,128)(2,1)S(1)} %get-tuple-element.99), channel_id=1, source_target_pairs={{0,4},{4,0},{8,12},{12,8},{16,20},{20,16},{24,28},{28,24},{1,5},{5... | collective-permute-start | bytes 1376264 | tf_op jit(solution)/shard_map/ppermute | solution.py:318
  136.7 16.5 %collective-permute-start.22 = (bf16[64,3584]{1,0:T(8,128)(2,1)}, bf16[64,3584]{1,0:T(8,128)(2,1)}, u32[]{:S(2)}, u32[]{:S(2)}) collective-permute-start(bf16[64,3584]{1,0:T(8,128)(2,1)} %slice.53), channel_id=1, source_target_pairs={{0,24},{4,28},{8,0},{12,4},{16,8},{20,12},{24,16},{28,20},{1,25},{... | collective-permute-start | bytes 1376264 | tf_op jit(solution)/shard_map/ppermute | solution.py:318
  139.2 14.0 %collective-permute-start.21 = (bf16[64,3584]{1,0:T(8,128)(2,1)}, bf16[64,3584]{1,0:T(8,128)(2,1)}, u32[]{:S(2)}, u32[]{:S(2)}) collective-permute-start(bf16[64,3584]{1,0:T(8,128)(2,1)} %slice.52), channel_id=1, source_target_pairs={{0,8},{4,12},{8,16},{12,20},{16,24},{20,28},{24,0},{28,4},{1,9},{5... | collective-permute-start | bytes 1376264 | tf_op jit(solution)/shard_map/ppermute | solution.py:318
  149.5 18.5 %collective-permute-start.26 = (bf16[64,3584]{1,0:T(8,128)(2,1)}, bf16[64,3584]{1,0:T(8,128)(2,1)}, u32[]{:S(2)}, u32[]{:S(2)}) collective-permute-start(bf16[64,3584]{1,0:T(8,128)(2,1)} %get-tuple-element.108), channel_id=1, source_target_pairs={{0,4},{4,0},{8,12},{12,8},{16,20},{20,16},{24,28},{28,24},{1,5},{5... | collective-permute-start | bytes 1376264 | tf_op jit(solution)/shard_map/ppermute | solution.py:318
  151.7 16.2 %collective-permute-start.28 = (bf16[64,3584]{1,0:T(8,128)(2,1)}, bf16[64,3584]{1,0:T(8,128)(2,1)}, u32[]{:S(2)}, u32[]{:S(2)}) collective-permute-start(bf16[64,3584]{1,0:T(8,128)(2,1)} %collective-permute-done.17.refs_1_), channel_id=1, source_target_pairs={{0,24},{4,28},{8,0},{12,4},{16,8},{20,12},{24,16},{28,20},{1,25},{... | collective-permute-start | bytes 1376264 | tf_op jit(solution)/shard_map/ppermute | solution.py:318
  153.0 15.0 %collective-permute-start.27 = (bf16[64,3584]{1,0:T(8,128)(2,1)}, bf16[64,3584]{1,0:T(8,128)(2,1)}, u32[]{:S(2)}, u32[]{:S(2)}) collective-permute-start(bf16[64,3584]{1,0:T(8,128)(2,1)} %collective-permute-done.17.refs_1_), channel_id=1, source_target_pairs={{0,8},{4,12},{8,16},{12,20},{16,24},{20,28},{24,0},{28,4},{1,9},{5... | collective-permute-start | bytes 1376264 | tf_op jit(solution)/shard_map/ppermute | solution.py:318
  157.5 10.5 %collective-permute-start.24 = (f32[128,128]{1,0:T(8,128)S(1)}, f32[128,128]{1,0:T(8,128)S(1)}, u32[]{:S(2)}, u32[]{:S(2)}) collective-permute-start(f32[128,128]{1,0:T(8,128)S(1)} %add.193), channel_id=1, source_target_pairs={{32,0},{33,3},{34,2},{35,1},{64,32},{65,35},{66,34},{67,33},{96,64... | collective-permute-start | bytes 196616 | tf_op jit(solution)/shard_map/ppermute | solution.py:335
  169.2 12.7 %collective-permute-start.33 = (bf16[64,3584]{1,0:T(8,128)(2,1)}, bf16[64,3584]{1,0:T(8,128)(2,1)}, u32[]{:S(2)}, u32[]{:S(2)}) collective-permute-start(bf16[64,3584]{1,0:T(8,128)(2,1)} %collective-permute-done.26.refs_2_), channel_id=1, source_target_pairs={{0,24},{4,28},{8,0},{12,4},{16,8},{20,12},{24,16},{28,20},{1,25},{... | collective-permute-start | bytes 1376264 | tf_op jit(solution)/shard_map/ppermute | solution.py:318
  170.4 13.1 %collective-permute-start.32 = (bf16[64,3584]{1,0:T(8,128)(2,1)}, bf16[64,3584]{1,0:T(8,128)(2,1)S(1)}, u32[]{:S(2)}, u32[]{:S(2)}) collective-permute-start(bf16[64,3584]{1,0:T(8,128)(2,1)} %collective-permute-done.26.refs_2_), channel_id=1, source_target_pairs={{0,8},{4,12},{8,16},{12,20},{16,24},{20,28},{24,0},{28,4},{1,9},{5... | collective-permute-start | bytes 1376264 | tf_op jit(solution)/shard_map/ppermute | solution.py:318
  180.7 14.2 %collective-permute-start.37 = (bf16[64,3584]{1,0:T(8,128)(2,1)}, bf16[64,3584]{1,0:T(8,128)(2,1)}, u32[]{:S(2)}, u32[]{:S(2)}) collective-permute-start(bf16[64,3584]{1,0:T(8,128)(2,1)} %collective-permute-done.27.refs_4_), channel_id=1, source_target_pairs={{0,8},{4,12},{8,16},{12,20},{16,24},{20,28},{24,0},{28,4},{1,9},{5... | collective-permute-start | bytes 1376264 | tf_op jit(solution)/shard_map/ppermute | solution.py:318
  183.5 12.6 %collective-permute-start.38 = (bf16[64,3584]{1,0:T(8,128)(2,1)}, bf16[64,3584]{1,0:T(8,128)(2,1)}, u32[]{:S(2)}, u32[]{:S(2)}) collective-permute-start(bf16[64,3584]{1,0:T(8,128)(2,1)} %collective-permute-done.33.refs_8_), channel_id=1, source_target_pairs={{0,24},{4,28},{8,0},{12,4},{16,8},{20,12},{24,16},{28,20},{1,25},{... | collective-permute-start | bytes 1376264 | tf_op jit(solution)/shard_map/ppermute | solution.py:318
  196.9 13.4 %all-to-all-start.2 = ((bf16[8,128,256]{2,1,0:T(8,128)(2,1)}), bf16[8,128,256]{2,1,0:T(8,128)(2,1)}, u32[]{:S(2)}, u32[]{:S(2)}) async-start(bf16[8,128,256]{2,1,0:T(8,128)(2,1)} %broadcast_in_dim.12), calls=%async_computation.2 | async-start | bytes 1048576 | tf_op jit(solution)/shard_map/all_to_all | solution.py:370
  210.3 21.4 %collective-permute-start.40 = (f32[256,128]{1,0:T(8,128)S(1)}, f32[256,128]{1,0:T(8,128)S(1)}, u32[]{:S(2)}, u32[]{:S(2)}) collective-permute-start(f32[256,128]{1,0:T(8,128)S(1)} %fusion), channel_id=1, source_target_pairs={{0,2},{1,3},{2,0},{3,1},{4,6},{5,7},{6,4},{7,5},{8,10},{9,11},{10,... | collective-permute-start | bytes 393224 | tf_op jit(solution)/shard_map/ppermute | solution.py:323
  (39 other events, 365.1 us)
